TPU v7x, 256 devices: a whole 4x4x8 slice. The times are simulated.
256 devices in a mesh: ia: 16 (over y, x), ja: 4 (over z_hi, core), ta: 4 (over z_lo).
Axes of the slice: x: 4, y: 4, z: 8 (z_hi: 2, z_lo: 4; z = z_hi * 4 + z_lo), core: 2. Of those that a mesh axis runs over, the one named last changes fastest.
Arguments:
- readings: bfloat16 [48, 4096, 4096], P('ta', 'ia', 'ja'), may hold values from 0.049804688 to 20
- factor_first: float32 [4096, 128], P(('ia', 'ja', 'ta')), may hold values from 0.1 to 0.4
- factor_second: float32 [128, 4096], P('ia', ('ja', 'ta')), may hold values from 0.1 to 0.4
- factor_time: float32 [48, 128], P('ta'), may hold values from 0.05 to 0.4
- mean_first: float32 [4096, 128], P(('ia', 'ja', 'ta')), may hold values from -4 to 4
- square_first: float32 [4096, 128], P(('ia', 'ja', 'ta')), may hold values from 0.3 to 5
- mean_second: float32 [128, 4096], P('ia', ('ja', 'ta')), may hold values from -4 to 4
- square_second: float32 [128, 4096], P('ia', ('ja', 'ta')), may hold values from 0.3 to 5
- mean_time: float32 [48, 128], P('ta'), may hold values from -4 to 4
- square_time: float32 [48, 128], P('ta'), may hold values from 0.3 to 5
Outputs:
- result_first: float32 [4096, 128], P(('ia', 'ja', 'ta'))
- result_second: float32 [128, 4096], P('ia', ('ja', 'ta'))
- result_time: float32 [48, 128], P('ta')
- drift_first: float32 [4096, 128], P(('ia', 'ja', 'ta'))
- spread_first: float32 [4096, 128], P(('ia', 'ja', 'ta'))
- drift_second: float32 [128, 4096], P('ia', ('ja', 'ta'))
- spread_second: float32 [128, 4096], P('ia', ('ja', 'ta'))
- drift_time: float32 [48, 128], P('ta')
- spread_time: float32 [48, 128], P('ta')
All inputs are finite; a program needn't handle non-finite values.
Results may differ from a plain program's by a relative error of at most 0.0024.
Values may be sent and summed in bfloat16 or wider, within the bound.
No kernel may reach another device: no remote copies, remote signals or barrier semaphores. Data moves between devices by JAX's collectives and lax.ppermute only.
A program may use at most 64 MiB of HBM per device.

v0:
```python
import jax
import jax.numpy as jnp
from jax import lax
from jax.sharding import PartitionSpec as P

STEPS = 2
ADAM_STEP = 20


beta_one = 0.9
beta_two = 0.99
step_rate = 0.02
tiny_eps = 1e-08


def adam(value, grad, mean, square, count):
    drift = beta_one * mean + (1.0 - beta_one) * grad
    spread = beta_two * square + (1.0 - beta_two) * grad * grad
    fixed_one = 1.0 - beta_one**count
    fixed_two = 1.0 - beta_two**count
    value = value - step_rate * (drift / fixed_one) / (jnp.sqrt(spread / fixed_two) + tiny_eps)
    return (value, drift, spread)


def body(
    readings,
    factor_first,
    factor_second,
    factor_time,
    mean_first,
    square_first,
    mean_second,
    square_second,
    mean_time,
    square_time,
):
    whole_i = readings.shape[1] * lax.axis_size("ia")
    whole_j = readings.shape[2] * lax.axis_size("ja")
    whole_k = readings.shape[0] * lax.axis_size("ta")
    rank = factor_first.shape[1]
    for step in range(STEPS):
        count = ADAM_STEP + step + 1
        a16 = lax.all_gather(factor_first.astype(jnp.bfloat16), ("ja", "ta"), axis=0, tiled=True)
        b_piece = factor_second.astype(jnp.bfloat16)
        b_ranks = lax.all_gather(b_piece, "ia", axis=0, tiled=True)
        b16 = lax.all_gather(b_ranks, "ta", axis=1, tiled=True)
        c16 = factor_time.astype(jnp.bfloat16)
        af = a16.astype(jnp.float32)
        cf = c16.astype(jnp.float32)
        scaled = (af[None, :, :] * cf[:, None, :]).astype(jnp.bfloat16)
        model = lax.dot_general(
            scaled, b16, (((2,), (0,)), ((), ())), preferred_element_type=jnp.float32
        )
        slope = (1.0 / model - readings.astype(jnp.float32) / (model * model)).astype(jnp.bfloat16)
        cross = lax.dot_general(
            slope, b16, (((2,), (1,)), ((), ())), preferred_element_type=jnp.float32
        )
        part_second = lax.dot_general(
            scaled, slope, (((0, 1), (0, 1)), ((), ())), preferred_element_type=jnp.float32
        )
        part_first = jnp.sum(cross * cf[:, None, :], axis=0)
        part_time = jnp.sum(cross * af[None, :, :], axis=1)
        grad_first = lax.psum_scatter(part_first, ("ja", "ta"), scatter_dimension=0, tiled=True) * (
            rank / (whole_j * whole_k)
        )
        reduced = lax.psum_scatter(part_second, "ia", scatter_dimension=0, tiled=True)
        grad_second = lax.psum_scatter(reduced, "ta", scatter_dimension=1, tiled=True)
        grad_second = grad_second * (rank / (whole_i * whole_k))
        grad_time = lax.psum(part_time, ("ia", "ja")) * (rank / (whole_i * whole_j))
        factor_first, mean_first, square_first = adam(
            factor_first, grad_first, mean_first, square_first, count
        )
        factor_second, mean_second, square_second = adam(
            factor_second, grad_second, mean_second, square_second, count
        )
        factor_time, mean_time, square_time = adam(
            factor_time, grad_time, mean_time, square_time, count
        )
    return (
        factor_first,
        factor_second,
        factor_time,
        mean_first,
        square_first,
        mean_second,
        square_second,
        mean_time,
        square_time,
    )


def solution(mesh):
    placed = (
        P("ta", "ia", "ja"),
        P(("ia", "ja", "ta"), None),
        P("ia", ("ja", "ta")),
        P("ta", None),
        P(("ia", "ja", "ta"), None),
        P(("ia", "ja", "ta"), None),
        P("ia", ("ja", "ta")),
        P("ia", ("ja", "ta")),
        P("ta", None),
        P("ta", None),
    )
    return jax.shard_map(
        body,
        mesh=mesh,
        in_specs=placed,
        out_specs=(
            P(("ia", "ja", "ta"), None),
            P("ia", ("ja", "ta")),
            P("ta", None),
            P(("ia", "ja", "ta"), None),
            P(("ia", "ja", "ta"), None),
            P("ia", ("ja", "ta")),
            P("ia", ("ja", "ta")),
            P("ta", None),
            P("ta", None),
        ),
        check_vma=False,
    )
```

profile of v0, /device:TPU:32, one launch (start us, length us, event | category | flops | bytes accessed | tf_op | source)
XLA Modules:
  0.0 662.6 jit_solution(1984181548405349236)
XLA Ops:
  8.1 0.7 convert_element_type.46
  8.8 26.4 %all_gather.18 = bf16[256,128]{1,0:T(8,128)(2,1)S(1)} all-gather(bf16[16,128]{1,0:T(8,128)(2,1)S(1)} %convert_element_type.46), channel_id=1, replica_groups=mesh['ia'=16,'ja'=4,'ta'=4] {'ja','ta'}, dimensions={0}, use_global_device_ids=true | all-gather | bytes 69632 | tf_op jit(solution)/shard_map/all_gather | solution.py:43
  35.1 0.7 convert_convert_fusion.1
  35.9 0.7 convert_element_type.51
  36.5 23.9 %all_gather.19 = bf16[128,256]{1,0:T(8,128)(2,1)S(1)} all-gather(bf16[8,256]{1,0:T(8,128)(2,1)S(1)} %convert_element_type.51), channel_id=1, replica_groups=mesh['ia'=16,'ja'=4,'ta'=4] {'ia'}, dimensions={0}, use_global_device_ids=true | all-gather | bytes 69632 | tf_op jit(solution)/shard_map/all_gather | solution.py:45
  60.5 14.0 %all_gather.20 = bf16[128,1024]{1,0:T(8,128)(2,1)S(1)} all-gather(bf16[128,256]{1,0:T(8,128)(2,1)S(1)} %all_gather.19), channel_id=1, replica_groups=mesh['ia'=16,'ja'=4,'ta'=4] {'ta'}, dimensions={1}, use_global_device_ids=true | all-gather | bytes 327680 | tf_op jit(solution)/shard_map/all_gather | solution.py:46
  74.5 5.5 fusion.1
  80.0 2.6 copy-done
  82.7 1.9 convolution_bitcast_fusion.1
  84.7 0.0 reduce-scatter.5.cloned.1.call-start
  84.7 5.3 multiply_reduce_fusion.2
  90.1 203.2 %psum.14 = f32[12,128]{1,0:T(8,128)S(1)} all-reduce(f32[12,128]{1,0:T(8,128)S(1)} %get-tuple-element.11), channel_id=1, replica_groups=mesh['ia'=16,'ja'=4,'ta'=4] {'ia','ja'}, use_global_device_ids=true, to_apply=%region_3.0 | all-reduce | flops 1536 | bytes 12288 | tf_op jit(solution)/shard_map/psum | solution.py:69
  293.3 0.6 dynamic-slice
  294.6 1.4 constant_dynamic-slice_fusion.1
  296.2 0.7 fusion.19
  296.9 25.9 %all_gather.21 = bf16[256,128]{1,0:T(8,128)(2,1)S(1)} all-gather(bf16[16,128]{1,0:T(8,128)(2,1)S(1)} %get-tuple-element.24), channel_id=1, replica_groups=mesh['ia'=16,'ja'=4,'ta'=4] {'ja','ta'}, dimensions={0}, use_global_device_ids=true | all-gather | bytes 69632 | tf_op jit(solution)/shard_map/all_gather | solution.py:43
  322.8 0.7 fusion.18
  323.6 20.3 %all_gather.22 = bf16[128,256]{1,0:T(8,128)(2,1)S(1)} all-gather(bf16[8,256]{1,0:T(8,128)(2,1)S(1)} %get-tuple-element.22), channel_id=1, replica_groups=mesh['ia'=16,'ja'=4,'ta'=4] {'ia'}, dimensions={0}, use_global_device_ids=true | all-gather | bytes 69632 | tf_op jit(solution)/shard_map/all_gather | solution.py:45
  343.9 14.1 %all_gather.23 = bf16[128,1024]{1,0:T(8,128)(2,1)S(1)} all-gather(bf16[128,256]{1,0:T(8,128)(2,1)S(1)} %all_gather.22), channel_id=1, replica_groups=mesh['ia'=16,'ja'=4,'ta'=4] {'ta'}, dimensions={1}, use_global_device_ids=true | all-gather | bytes 327680 | tf_op jit(solution)/shard_map/all_gather | solution.py:46
  358.0 5.5 fusion.3
  363.5 2.6 copy-done.1
  366.2 1.9 convolution_bitcast_fusion
  368.1 0.0 reduce-scatter.9.cloned.1.call-start
  368.2 5.3 multiply_reduce_fusion
  373.5 203.2 %psum.15 = f32[12,128]{1,0:T(8,128)S(1)} all-reduce(f32[12,128]{1,0:T(8,128)S(1)} %get-tuple-element.9), channel_id=1, replica_groups=mesh['ia'=16,'ja'=4,'ta'=4] {'ia','ja'}, use_global_device_ids=true, to_apply=%region_11.0 | all-reduce | flops 1536 | bytes 12288 | tf_op jit(solution)/shard_map/psum | solution.py:69
  576.6 0.0 reduce-scatter.11.cloned.1.call-start
  576.7 0.6 divide_subtract_fusion
  577.3 1.4 constant_dynamic-slice_fusion
  578.7 49.9 %reduce-scatter.9.cloned.1.call-done = f32[16,128]{1,0:T(8,128)} async-done(((f32[256,128]{1,0:T(8,128)}), f32[16,128]{1,0:T(8,128)}) %reduce-scatter.9.cloned.1.call-update) | async-done | bytes 8208 | tf_op jit(solution)/shard_map/reduce_scatter | solution.py:63
  628.6 1.3 divide_subtract_fusion.2
  630.0 23.7 %reduce-scatter.11.cloned.1.call-done = f32[8,256]{1,0:T(8,128)} async-done(((f32[8,1024]{1,0:T(8,128)}), f32[8,256]{1,0:T(8,128)}) %reduce-scatter.11.cloned.1.call-update) | async-done | bytes 8208 | tf_op jit(solution)/shard_map/reduce_scatter | solution.py:67
  653.6 1.3 divide_subtract_fusion.1
  (42 shorter events, 0.4 us)
Async XLA Ops:
  8.0 286.6 %all-reduce.5.cloned.1.call-start = ((), (), s32[]{:S(2)}) async-start(), calls=%async_computation.8 | async-start | bytes 1048576
  80.0 2.7 copy-start
  84.6 208.8 %copy-start.13 = (u32[256]{0:T(256)S(1)}, u32[256]{0:T(256)}, u32[]{:S(2)}) copy-start(u32[256]{0:T(256)} %constant.88) | copy-start | bytes 3076
  84.6 210.0 %copy-start.2 = (f32[12,128]{1,0:T(8,128)S(1)}, f32[12,128]{1,0:T(8,128)}, u32[]{:S(2)}) copy-start(f32[12,128]{1,0:T(8,128)} %param.13) | copy-start | bytes 18436
  84.6 210.0 %copy-start.5 = (f32[12,128]{1,0:T(8,128)S(1)}, f32[12,128]{1,0:T(8,128)}, u32[]{:S(2)}) copy-start(f32[12,128]{1,0:T(8,128)} %param.19) | copy-start | bytes 18436
  84.6 210.0 %copy-start.6 = (f32[12,128]{1,0:T(8,128)S(1)}, f32[12,128]{1,0:T(8,128)}, u32[]{:S(2)}) copy-start(f32[12,128]{1,0:T(8,128)} %param.18) | copy-start | bytes 18436
  84.6 211.5 %copy-start.3 = (f32[16,128]{1,0:T(8,128)S(1)}, f32[16,128]{1,0:T(8,128)}, u32[]{:S(2)}) copy-start(f32[16,128]{1,0:T(8,128)} %param.11) | copy-start | bytes 24580
  84.6 211.5 %copy-start.7 = (f32[16,128]{1,0:T(8,128)S(1)}, f32[16,128]{1,0:T(8,128)}, u32[]{:S(2)}) copy-start(f32[16,128]{1,0:T(8,128)} %param.15) | copy-start | bytes 24580
  84.6 211.5 %copy-start.8 = (f32[16,128]{1,0:T(8,128)S(1)}, f32[16,128]{1,0:T(8,128)}, u32[]{:S(2)}) copy-start(f32[16,128]{1,0:T(8,128)} %param.14) | copy-start | bytes 24580
  84.6 238.2 %copy-start.4 = (f32[8,256]{1,0:T(8,128)S(1)}, f32[8,256]{1,0:T(8,128)}, u32[]{:S(2)}) copy-start(f32[8,256]{1,0:T(8,128)} %param.12) | copy-start | bytes 24580
  84.7 238.2 %copy-start.9 = (f32[8,256]{1,0:T(8,128)S(1)}, f32[8,256]{1,0:T(8,128)}, u32[]{:S(2)}) copy-start(f32[8,256]{1,0:T(8,128)} %param.17) | copy-start | bytes 24580
  84.7 238.2 %copy-start.10 = (f32[8,256]{1,0:T(8,128)S(1)}, f32[8,256]{1,0:T(8,128)}, u32[]{:S(2)}) copy-start(f32[8,256]{1,0:T(8,128)} %param.16) | copy-start | bytes 24580
  84.7 211.4 %reduce-scatter.5.cloned.1.call-start = ((), (), s32[]{:S(2)}) async-start(), calls=%async_computation.4 | async-start | bytes 139264 | tf_op jit(solution)/shard_map/reduce_scatter | solution.py:63
  90.1 232.7 %reduce-scatter.7.cloned.1.call-start = ((), (), s32[]{:S(2)}) async-start(), calls=%async_computation.5 | async-start | bytes 40960 | tf_op jit(solution)/shard_map/reduce_scatter | solution.py:67
  296.1 281.3 %all-reduce.7.cloned.1.call-start = ((), (), s32[]{:S(2)}) async-start(), calls=%async_computation.9 | async-start | bytes 1048576
  363.5 2.7 copy-start.1
  368.1 260.6 %copy-start.11 = (f32[16,128]{1,0:T(8,128)S(1)}, f32[16,128]{1,0:T(8,128)}, u32[]{:S(2)}) copy-start(f32[16,128]{1,0:T(8,128)} %reduce-scatter.5.cloned.1.call-done) | copy-start | bytes 24580
  368.1 285.6 %copy-start.12 = (f32[8,256]{1,0:T(8,128)S(1)}, f32[8,256]{1,0:T(8,128)}, u32[]{:S(2)}) copy-start(f32[8,256]{1,0:T(8,128)} %reduce-scatter.7.cloned.1.call-done) | copy-start | bytes 24580
  368.1 260.5 %reduce-scatter.9.cloned.1.call-start = ((), (), s32[]{:S(2)}) async-start(), calls=%async_computation.6 | async-start | bytes 139264 | tf_op jit(solution)/shard_map/reduce_scatter | solution.py:63
  576.6 77.0 %reduce-scatter.11.cloned.1.call-start = ((), (), s32[]{:S(2)}) async-start(), calls=%async_computation.7 | async-start | bytes 40960 | tf_op jit(solution)/shard_map/reduce_scatter | solution.py:67
Sparse Core Ops, SparseCore 0:
  84.7 94.1 all-reduce.4
  368.2 93.0 all-reduce.6
Sparse Core Ops, SparseCore 1:
  90.1 57.2 reduce-scatter.4
  296.1 15.6 reduce-scatter.6
  576.7 51.8 reduce-scatter.8
  631.3 22.3 reduce-scatter.10
where the time goes:
time: 666 us; the launch traced here: 663 us
  blocking collectives  531 us (80%)
  waiting for transfers between devices  73.8 us (11%)
  matrix products  25.4 us (4%)
  between operations  16.6 us (2%)
  local copies, waits for them, and re-layouts  8.7 us (1%)
  other arithmetic  6.84 us (1%)
    psum x2, blocking collectives, body(): grad_time = lax.psum(part_time, ('ia', 'ja')) * (rank / (whole_i * whole_j))  406 us
    all_gather x2, blocking collectives, body(): lax.all_gather(factor_first.astype(jnp.bfloat16), ('ja', 'ta'), axis=0, t...  52.3 us
    reduce_scatter x2, waiting for transfers between devices, body(): lax.psum_scatter(part_first, ('ja', 'ta'), scatter_dimension=0, tiled=True)  49.9 us
    all_gather x2, blocking collectives, body(): b_ranks = lax.all_gather(b_piece, 'ia', axis=0, tiled=True)  44.2 us
    all_gather x2, blocking collectives, body(): b16 = lax.all_gather(b_ranks, 'ta', axis=1, tiled=True)  28.1 us
    reduce_scatter x2, waiting for transfers between devices, body(): lax.psum_scatter(reduced, 'ta', scatter_dimension=1, tiled=True)  23.7 us
  transfers between devices with their start and end apart: 6, of which 2 were waited for; matrix products, arithmetic and copies ran while one was open for 3% of the time, Pallas kernels for 0%

commit v1 on v0

v1 whole, which is shorter than its diff:
```python
import jax
import jax.numpy as jnp
from jax import lax
from jax.sharding import PartitionSpec as P

STEPS = 2
ADAM_STEP = 20


beta_one = 0.9
beta_two = 0.99
step_rate = 0.02
tiny_eps = 1e-08


def adam(value, grad, mean, square, count):
    drift = beta_one * mean + (1.0 - beta_one) * grad
    spread = beta_two * square + (1.0 - beta_two) * grad * grad
    fixed_one = 1.0 - beta_one**count
    fixed_two = 1.0 - beta_two**count
    value = value - step_rate * (drift / fixed_one) / (jnp.sqrt(spread / fixed_two) + tiny_eps)
    return (value, drift, spread)


def gather_factors(factor_first, factor_second, ni, nj, nt):
    rows, rank = factor_first.shape
    ranks, cols = factor_second.shape
    ja = lax.axis_index("ja")
    a_piece = factor_first.astype(jnp.bfloat16)
    b_piece = factor_second.astype(jnp.bfloat16)
    b_flat = jnp.concatenate([b_piece[:, :rank], b_piece[:, rank:]], axis=0)
    both = jnp.concatenate([a_piece, b_flat], axis=0)
    got = lax.all_to_all(
        jnp.broadcast_to(both, (nj * nt,) + both.shape), ("ja", "ta"), 0, 0
    )
    a16 = got[:, :rows].reshape(nj * nt * rows, rank)
    mine = lax.dynamic_slice_in_dim(got[:, rows:], ja * nt, nt, axis=0)
    halves = []
    for t in range(nt):
        halves += [mine[t, :ranks], mine[t, ranks:]]
    flat = jnp.concatenate(
        [jnp.concatenate(halves[:nt], axis=1), jnp.concatenate(halves[nt:], axis=1)], axis=0
    )
    got = lax.all_to_all(jnp.broadcast_to(flat, (ni,) + flat.shape), "ia", 0, 0)
    width = flat.shape[1]
    b16 = jnp.concatenate(
        [got[:, :ranks].reshape(ni * ranks, width), got[:, ranks:].reshape(ni * ranks, width)],
        axis=1,
    )
    return a16, b16


def reduce_parts(part_first, part_second, part_time, ni, nj, nt):
    rank = part_first.shape[1]
    ja, ta = lax.axis_index("ja"), lax.axis_index("ta")
    n_time = part_time.shape[0]
    ranks = part_second.shape[0] // ni
    cols = part_second.shape[1]
    time_pad = jnp.pad(part_time, ((0, 2 * ranks - n_time), (0, 0)))
    time_flat = jnp.concatenate([time_pad[:ranks], time_pad[ranks:]], axis=1)
    slots = jnp.concatenate(
        [
            part_second.reshape(ni, ranks, cols),
            jnp.broadcast_to(time_flat, (ni,) + time_flat.shape),
        ],
        axis=2,
    )
    got = jnp.sum(lax.all_to_all(slots, "ia", 0, 0), axis=0)
    time_flat = got[:, cols:]
    time_rows = jnp.concatenate([time_flat[:, :rank], time_flat[:, rank:]], axis=0)
    wide = cols // nt
    second = jnp.stack(
        [
            jnp.concatenate(
                [got[:, t * wide : t * wide + rank], got[:, t * wide + rank : (t + 1) * wide]],
                axis=0,
            )
            for t in range(nt)
        ]
    )
    same = jnp.arange(nj) == ja
    extra = jnp.where(
        same[:, None, None, None], second[None], time_rows[None, None]
    ).reshape(nj * nt, 2 * ranks, rank)
    rows = part_first.shape[0] // (nj * nt)
    slots = jnp.concatenate([part_first.reshape(nj * nt, rows, rank), extra], axis=1)
    got = lax.all_to_all(slots, ("ja", "ta"), 0, 0)
    grad_first = jnp.sum(got[:, :rows], axis=0)
    extra = got[:, rows:]
    mine = jnp.sum(lax.dynamic_slice_in_dim(extra, ja * nt, nt, axis=0), axis=0)
    grad_second = jnp.concatenate([mine[:ranks], mine[ranks:]], axis=1)
    others = lax.dynamic_index_in_dim(
        extra.reshape(nj, nt, 2 * ranks, rank), ta, axis=1, keepdims=False
    )
    grad_time = jnp.sum(jnp.where(same[:, None, None], time_rows[None], others), axis=0)
    return grad_first, grad_second, grad_time[:n_time]


def body(
    readings,
    factor_first,
    factor_second,
    factor_time,
    mean_first,
    square_first,
    mean_second,
    square_second,
    mean_time,
    square_time,
):
    ni, nj, nt = lax.axis_size("ia"), lax.axis_size("ja"), lax.axis_size("ta")
    whole_i = readings.shape[1] * ni
    whole_j = readings.shape[2] * nj
    whole_k = readings.shape[0] * nt
    rank = factor_first.shape[1]
    for step in range(STEPS):
        count = ADAM_STEP + step + 1
        a16, b16 = gather_factors(factor_first, factor_second, ni, nj, nt)
        c16 = factor_time.astype(jnp.bfloat16)
        af = a16.astype(jnp.float32)
        cf = c16.astype(jnp.float32)
        scaled = (af[None, :, :] * cf[:, None, :]).astype(jnp.bfloat16)
        model = lax.dot_general(
            scaled, b16, (((2,), (0,)), ((), ())), preferred_element_type=jnp.float32
        )
        slope = (1.0 / model - readings.astype(jnp.float32) / (model * model)).astype(jnp.bfloat16)
        cross = lax.dot_general(
            slope, b16, (((2,), (1,)), ((), ())), preferred_element_type=jnp.float32
        )
        part_second = lax.dot_general(
            scaled, slope, (((0, 1), (0, 1)), ((), ())), preferred_element_type=jnp.float32
        )
        part_first = jnp.sum(cross * cf[:, None, :], axis=0)
        part_time = jnp.sum(cross * af[None, :, :], axis=1)
        grad_first, grad_second, grad_time = reduce_parts(
            part_first, part_second, part_time, ni, nj, nt
        )
        grad_first = grad_first * (rank / (whole_j * whole_k))
        grad_second = grad_second * (rank / (whole_i * whole_k))
        grad_time = grad_time * (rank / (whole_i * whole_j))
        factor_first, mean_first, square_first = adam(
            factor_first, grad_first, mean_first, square_first, count
        )
        factor_second, mean_second, square_second = adam(
            factor_second, grad_second, mean_second, square_second, count
        )
        factor_time, mean_time, square_time = adam(
            factor_time, grad_time, mean_time, square_time, count
        )
    return (
        factor_first,
        factor_second,
        factor_time,
        mean_first,
        square_first,
        mean_second,
        square_second,
        mean_time,
        square_time,
    )


def solution(mesh):
    first = P(("ia", "ja", "ta"), None)
    second = P("ia", ("ja", "ta"))
    time = P("ta", None)
    return jax.shard_map(
        body,
        mesh=mesh,
        in_specs=(
            P("ta", "ia", "ja"),
            first,
            second,
            time,
            first,
            first,
            second,
            second,
            time,
            time,
        ),
        out_specs=(first, second, time, first, first, second, second, time, time),
        check_vma=False,
    )
```

time: 666 us -> 144 us (0.22)
  blocking collectives: 531 us -> 41.9 us
  waiting for transfers between devices: 73.8 us -> 46 us
  starting transfers between devices: 0.25 us -> 27.3 us
  between operations: 16.6 us -> 1.16 us
  matrix products: 25.4 us -> 17.2 us
    psum x2 -> x0, blocking collectives: 406 us -> none  [body(): grad_time = lax.psum(part_time, ('ia', 'ja')) * (rank / (whole_i * whole_j))]
    all_gather x6 -> x0, blocking collectives: 125 us -> none  [the longest x2 52.3 us: body(): lax.all_gather(factor_first.astype(jnp.bfloat16), ('ja', 'ta'), axis=0, t...]
    reduce_scatter x4 -> x0, waiting for transfers between devices: 73.6 us -> none  [the longest x2 49.9 us: body(): lax.psum_scatter(part_first, ('ja', 'ta'), scatter_dimension=0, tiled=True)]
    all_to_all x0 -> x5, waiting for transfers between devices: none -> 46 us  [the longest x2 18 us: gather_factors(): got = lax.all_to_all(jnp.broadcast_to(flat, (ni,) + flat.shape), 'ia', 0, 0)]
    all_to_all x0 -> x3, blocking collectives: none -> 41.9 us  [the longest x2 26.3 us: reduce_parts(): got = lax.all_to_all(slots, ('ja', 'ta'), 0, 0)]
    all_to_all x0 -> x5, starting transfers between devices: none -> 27.3 us  [the longest x2 13.2 us: gather_factors(): lax.all_to_all(jnp.broadcast_to(both, (nj * nt,) + both.shape), ('ja', 't...]
    unnamed x31 -> x18, local copies, waits for them, and re-layouts: 8.7 us -> 0.06 us
    dot_general x2, matrix products: 10.6 us -> 3.81 us  [body(): lax.dot_general(slope, b16, (((2,), (1,)), ((), ())), preferred_element_t...]
  transfers between devices with their start and end apart: 6 -> 5, of which waited for: 2 -> 5; matrix products, arithmetic and copies ran while one was open for 3% -> 1% of each run, Pallas kernels for 0% -> 0%
where the time goes in v1:
time: 144 us; the launch traced here: 142 us
  waiting for transfers between devices  46 us (32%)
  blocking collectives  41.9 us (29%)
  starting transfers between devices  27.3 us (19%)
  matrix products  17.2 us (12%)
  other arithmetic  5.59 us (4%)
  local copies, waits for them, and re-layouts  3.16 us (2%)
    all_to_all x2, blocking collectives, reduce_parts(): got = lax.all_to_all(slots, ('ja', 'ta'), 0, 0)  26.3 us
    all_to_all x2, waiting for transfers between devices, gather_factors(): got = lax.all_to_all(jnp.broadcast_to(flat, (ni,) + flat.shape), 'ia', 0, 0)  18 us
    all_to_all x1, blocking collectives, reduce_parts(): got = jnp.sum(lax.all_to_all(slots, 'ia', 0, 0), axis=0)  15.6 us
    all_to_all x2, waiting for transfers between devices, gather_factors(): lax.all_to_all(jnp.broadcast_to(both, (nj * nt,) + both.shape), ('ja', 't...  15.5 us
    all_to_all x2, starting transfers between devices, gather_factors(): lax.all_to_all(jnp.broadcast_to(both, (nj * nt,) + both.shape), ('ja', 't...  13.2 us
    all_to_all x1, waiting for transfers between devices, reduce_parts(): got = jnp.sum(lax.all_to_all(slots, 'ia', 0, 0), axis=0)  12.5 us
    dot_general x2, matrix products, body(): lax.dot_general(scaled, b16, (((2,), (0,)), ((), ())), preferred_element_...  11.3 us
    all_to_all x2, starting transfers between devices, gather_factors(): got = lax.all_to_all(jnp.broadcast_to(flat, (ni,) + flat.shape), 'ia', 0, 0)  10.6 us
  transfers between devices with their start and end apart: 5, of which 5 were waited for; matrix products, arithmetic and copies ran while one was open for 1% of the time, Pallas kernels for 0%

profile of v1, /device:TPU:32, one launch (start us, length us, event | category | flops | bytes accessed | tf_op | source)
XLA Modules:
  0.0 142.3 jit_solution(6208587618758332051)
XLA Ops:
  0.6 0.7 convert_element_type.63
  1.3 0.7 convert_element_type.64
  2.1 0.7 broadcast_in_dim.105
  2.7 8.6 %all-to-all-start = ((bf16[16,32,128]{2,1,0:T(8,128)(2,1)}), bf16[16,32,128]{2,1,0:T(8,128)(2,1)S(1)}, u32[]{:S(2)}, u32[]{:S(2)}) async-start(bf16[16,32,128]{2,1,0:T(8,128)(2,1)} %broadcast_in_dim.105), calls=%async_computation | async-start | bytes 262144 | tf_op jit(solution)/shard_map/all_to_all | solution.py:33
  11.3 7.8 %all-to-all-done = bf16[16,32,128]{2,1,0:T(8,128)(2,1)S(1)} async-done(((bf16[16,32,128]{2,1,0:T(8,128)(2,1)}), bf16[16,32,128]{2,1,0:T(8,128)(2,1)S(1)}, u32[]{:S(2)}, u32[]{:S(2)}) %all-to-all-start) | async-done | bytes 131104 | tf_op jit(solution)/shard_map/all_to_all | solution.py:33
  19.1 0.7 broadcast_in_dim.106
  19.9 7.0 %all-to-all-start.1 = ((bf16[16,16,512]{2,1,0:T(8,128)(2,1)}), bf16[16,16,512]{2,1,0:T(8,128)(2,1)S(1)}, u32[]{:S(2)}, u32[]{:S(2)}) async-start(bf16[16,16,512]{2,1,0:T(8,128)(2,1)} %broadcast_in_dim.106), calls=%async_computation.1 | async-start | bytes 524288 | tf_op jit(solution)/shard_map/all_to_all | solution.py:44
  26.9 0.7 convert_convert_fusion.1
  27.6 8.6 %all-to-all-done.1 = bf16[16,16,512]{2,1,0:T(8,128)(2,1)S(1)} async-done(((bf16[16,16,512]{2,1,0:T(8,128)(2,1)}), bf16[16,16,512]{2,1,0:T(8,128)(2,1)S(1)}, u32[]{:S(2)}, u32[]{:S(2)}) %all-to-all-start.1) | async-done | bytes 262176 | tf_op jit(solution)/shard_map/all_to_all | solution.py:44
  36.2 5.6 %fusion.1 = bf16[12,256,1024]{2,1,0:T(8,128)(2,1)S(1)} fusion(bf16[12,256,1024]{2,1,0:T(8,128)(2,1)} %param.10, f32[12,128]{1,0:T(8,128)S(1)} %convert_convert_fusion.1, f32[256,128]{1,0:T(8,128)S(1)} %bitcast_convert_fusion.1, bf16[128,512]{1,0:T(8,128)(2,1)S(1)} %get-tuple-element.35, bf16[128,512]{1,0:T(8,128)(2,1)S(1)} %get-tuple-element.34), kind=kOutput, calls=%fused_computation.3 | convolution fusion | flops 825491456 | bytes 12982272 | tf_op jit(solution)/shard_map/dot_general | solution.py:123
  41.9 1.9 %multiply_reduce_fusion.3 = (f32[256,128]{1,0:T(8,128)S(1)}, f32[12,128]{1,0:T(8,128)S(1)}) fusion(f32[12,128]{1,0:T(8,128)S(1)} %convert_convert_fusion.1, f32[256,128]{1,0:T(8,128)S(1)} %bitcast_convert_fusion.1, bf16[12,256,1024]{2,1,0:T(8,128)(2,1)S(1)} %fusion.1, bf16[128,512]{1,0:T(8,128)(2,1)S(1)} %get-tuple-element.35, ...), kind=kOutput, calls=%fused_computation.10 | convolution fusion | flops 807369216 | bytes 6828032 | tf_op jit(solution)/shard_map/dot_general | solution.py:127
  43.8 1.1 convolution_bitcast_fusion.1
  45.0 0.9 pad_maximum_fusion
  45.9 3.6 %all-to-all-start.2 = ((f32[16,8,1280]{2,1,0:T(8,128)}), f32[16,8,1280]{2,1,0:T(8,128)S(1)}, u32[]{:S(2)}, u32[]{:S(2)}) async-start(f32[16,8,1280]{2,1,0:T(8,128)} %pad_maximum_fusion), calls=%async_computation.2 | async-start | bytes 1310720 | tf_op jit(solution)/shard_map/all_to_all | solution.py:68
  49.5 0.1 broadcast_in_dim.108
  49.6 12.5 %all-to-all-done.2 = f32[16,8,1280]{2,1,0:T(8,128)S(1)} async-done(((f32[16,8,1280]{2,1,0:T(8,128)}), f32[16,8,1280]{2,1,0:T(8,128)S(1)}, u32[]{:S(2)}, u32[]{:S(2)}) %all-to-all-start.2) | async-done | bytes 655392 | tf_op jit(solution)/shard_map/all_to_all | solution.py:68
  62.4 13.1 %all_to_all.40 = f32[16,32,128]{2,1,0:T(8,128)S(1)} all-to-all(f32[16,32,128]{2,1,0:T(8,128)S(1)} %pad_maximum_fusion.2), channel_id=1, replica_groups=mesh['ia'=16,'ja'=4,'ta'=4] {'ja','ta'}, dimensions={0} | all-to-all | bytes 524288 | tf_op jit(solution)/shard_map/all_to_all | solution.py:87
  75.7 0.7 broadcast_in_dim.114
  76.4 4.6 %all-to-all-start.4 = ((bf16[16,32,128]{2,1,0:T(8,128)(2,1)}), bf16[16,32,128]{2,1,0:T(8,128)(2,1)S(1)}, u32[]{:S(2)}, u32[]{:S(2)}) async-start(bf16[16,32,128]{2,1,0:T(8,128)(2,1)} %broadcast_in_dim.114), calls=%async_computation.4 | async-start | bytes 262144 | tf_op jit(solution)/shard_map/all_to_all | solution.py:33
  81.0 7.7 %all-to-all-done.4 = bf16[16,32,128]{2,1,0:T(8,128)(2,1)S(1)} async-done(((bf16[16,32,128]{2,1,0:T(8,128)(2,1)}), bf16[16,32,128]{2,1,0:T(8,128)(2,1)S(1)}, u32[]{:S(2)}, u32[]{:S(2)}) %all-to-all-start.4) | async-done | bytes 131104 | tf_op jit(solution)/shard_map/all_to_all | solution.py:33
  88.8 0.7 broadcast_in_dim.117
  89.5 3.5 %all-to-all-start.5 = ((bf16[16,16,512]{2,1,0:T(8,128)(2,1)}), bf16[16,16,512]{2,1,0:T(8,128)(2,1)S(1)}, u32[]{:S(2)}, u32[]{:S(2)}) async-start(bf16[16,16,512]{2,1,0:T(8,128)(2,1)} %broadcast_in_dim.117), calls=%async_computation.5 | async-start | bytes 524288 | tf_op jit(solution)/shard_map/all_to_all | solution.py:44
  93.1 9.5 %all-to-all-done.5 = bf16[16,16,512]{2,1,0:T(8,128)(2,1)S(1)} async-done(((bf16[16,16,512]{2,1,0:T(8,128)(2,1)}), bf16[16,16,512]{2,1,0:T(8,128)(2,1)S(1)}, u32[]{:S(2)}, u32[]{:S(2)}) %all-to-all-start.5) | async-done | bytes 262176 | tf_op jit(solution)/shard_map/all_to_all | solution.py:44
  102.6 5.6 %fusion.3 = bf16[12,256,1024]{2,1,0:T(8,128)(2,1)S(1)} fusion(bf16[12,256,1024]{2,1,0:T(8,128)(2,1)} %param.10, f32[12,128]{1,0:T(8,128)S(1)} %get-tuple-element.26, f32[256,128]{1,0:T(8,128)S(1)} %bitcast_convert_fusion, bf16[128,512]{1,0:T(8,128)(2,1)S(1)} %get-tuple-element.31, bf16[128,512]{1,0:T(8,128)(2,1)S(1)} %get-tuple-element.30), kind=kOutput, calls=%fused_computation.5 | convolution fusion | flops 825491456 | bytes 12982272 | tf_op jit(solution)/shard_map/dot_general | solution.py:123
  108.3 1.9 %multiply_reduce_fusion.1 = (f32[256,128]{1,0:T(8,128)S(1)}, f32[12,128]{1,0:T(8,128)S(1)}) fusion(f32[12,128]{1,0:T(8,128)S(1)} %get-tuple-element.26, f32[256,128]{1,0:T(8,128)S(1)} %bitcast_convert_fusion, bf16[12,256,1024]{2,1,0:T(8,128)(2,1)S(1)} %fusion.3, bf16[128,512]{1,0:T(8,128)(2,1)S(1)} %get-tuple-element.31, ...), kind=kOutput, calls=%fused_computation.7 | convolution fusion | flops 807369216 | bytes 6828032 | tf_op jit(solution)/shard_map/dot_general | solution.py:127
  110.2 1.1 convolution_bitcast_fusion
  111.3 15.6 %all_to_all.41 = f32[16,8,1280]{2,1,0:T(8,128)S(1)} all-to-all(f32[16,8,1280]{2,1,0:T(8,128)S(1)} %pad_maximum_fusion.1), channel_id=1, replica_groups=mesh['ia'=16,'ja'=4,'ta'=4] {'ia'}, dimensions={0} | all-to-all | bytes 1310720 | tf_op jit(solution)/shard_map/all_to_all | solution.py:68
  127.1 0.1 bitcast_select_fusion
  127.2 13.1 %all_to_all.42 = f32[16,32,128]{2,1,0:T(8,128)S(1)} all-to-all(f32[16,32,128]{2,1,0:T(8,128)S(1)} %pad_maximum_fusion.3), channel_id=1, replica_groups=mesh['ia'=16,'ja'=4,'ta'=4] {'ja','ta'}, dimensions={0} | all-to-all | bytes 524288 | tf_op jit(solution)/shard_map/all_to_all | solution.py:87
  140.5 0.6 divide_subtract_fusion
  141.1 0.6 divide_subtract_fusion.2
  141.7 0.6 divide_subtract_fusion.1
  (69 shorter events, 0.9 us)
Async XLA Ops:
  2.7 16.4 %all-to-all-start = ((bf16[16,32,128]{2,1,0:T(8,128)(2,1)}), bf16[16,32,128]{2,1,0:T(8,128)(2,1)S(1)}, u32[]{:S(2)}, u32[]{:S(2)}) async-start(bf16[16,32,128]{2,1,0:T(8,128)(2,1)} %broadcast_in_dim.105), calls=%async_computation | async-start | bytes 262144 | tf_op jit(solution)/shard_map/all_to_all | solution.py:33
  19.9 16.3 %all-to-all-start.1 = ((bf16[16,16,512]{2,1,0:T(8,128)(2,1)}), bf16[16,16,512]{2,1,0:T(8,128)(2,1)S(1)}, u32[]{:S(2)}, u32[]{:S(2)}) async-start(bf16[16,16,512]{2,1,0:T(8,128)(2,1)} %broadcast_in_dim.106), calls=%async_computation.1 | async-start | bytes 524288 | tf_op jit(solution)/shard_map/all_to_all | solution.py:44
  43.8 31.8 %copy-start = (f32[8,256]{1,0:T(8,128)S(1)}, f32[8,256]{1,0:T(8,128)}, u32[]{:S(2)}) copy-start(f32[8,256]{1,0:T(8,128)} %param.12) | copy-start | bytes 24580
  43.8 31.8 %copy-start.7 = (f32[8,256]{1,0:T(8,128)S(1)}, f32[8,256]{1,0:T(8,128)}, u32[]{:S(2)}) copy-start(f32[8,256]{1,0:T(8,128)} %param.17) | copy-start | bytes 24580
  43.8 31.8 %copy-start.8 = (f32[8,256]{1,0:T(8,128)S(1)}, f32[8,256]{1,0:T(8,128)}, u32[]{:S(2)}) copy-start(f32[8,256]{1,0:T(8,128)} %param.16) | copy-start | bytes 24580
  43.8 31.8 %copy-start.1 = (f32[16,128]{1,0:T(8,128)S(1)}, f32[16,128]{1,0:T(8,128)}, u32[]{:S(2)}) copy-start(f32[16,128]{1,0:T(8,128)} %param.11) | copy-start | bytes 24580
  43.8 31.8 %copy-start.5 = (f32[16,128]{1,0:T(8,128)S(1)}, f32[16,128]{1,0:T(8,128)}, u32[]{:S(2)}) copy-start(f32[16,128]{1,0:T(8,128)} %param.15) | copy-start | bytes 24580
  43.8 31.8 %copy-start.6 = (f32[16,128]{1,0:T(8,128)S(1)}, f32[16,128]{1,0:T(8,128)}, u32[]{:S(2)}) copy-start(f32[16,128]{1,0:T(8,128)} %param.14) | copy-start | bytes 24580
  44.9 48.1 %copy-start.2 = (f32[12,128]{1,0:T(8,128)S(1)}, f32[12,128]{1,0:T(8,128)}, u32[]{:S(2)}) copy-start(f32[12,128]{1,0:T(8,128)} %param.13) | copy-start | bytes 18436
  44.9 48.1 %copy-start.3 = (f32[12,128]{1,0:T(8,128)S(1)}, f32[12,128]{1,0:T(8,128)}, u32[]{:S(2)}) copy-start(f32[12,128]{1,0:T(8,128)} %param.19) | copy-start | bytes 18436
  44.9 48.1 %copy-start.4 = (f32[12,128]{1,0:T(8,128)S(1)}, f32[12,128]{1,0:T(8,128)}, u32[]{:S(2)}) copy-start(f32[12,128]{1,0:T(8,128)} %param.18) | copy-start | bytes 18436
  45.9 16.3 %all-to-all-start.2 = ((f32[16,8,1280]{2,1,0:T(8,128)}), f32[16,8,1280]{2,1,0:T(8,128)S(1)}, u32[]{:S(2)}, u32[]{:S(2)}) async-start(f32[16,8,1280]{2,1,0:T(8,128)} %pad_maximum_fusion), calls=%async_computation.2 | async-start | bytes 1310720 | tf_op jit(solution)/shard_map/all_to_all | solution.py:68
  76.4 12.3 %all-to-all-start.4 = ((bf16[16,32,128]{2,1,0:T(8,128)(2,1)}), bf16[16,32,128]{2,1,0:T(8,128)(2,1)S(1)}, u32[]{:S(2)}, u32[]{:S(2)}) async-start(bf16[16,32,128]{2,1,0:T(8,128)(2,1)} %broadcast_in_dim.114), calls=%async_computation.4 | async-start | bytes 262144 | tf_op jit(solution)/shard_map/all_to_all | solution.py:33
  89.5 13.1 %all-to-all-start.5 = ((bf16[16,16,512]{2,1,0:T(8,128)(2,1)}), bf16[16,16,512]{2,1,0:T(8,128)(2,1)S(1)}, u32[]{:S(2)}, u32[]{:S(2)}) async-start(bf16[16,16,512]{2,1,0:T(8,128)(2,1)} %broadcast_in_dim.117), calls=%async_computation.5 | async-start | bytes 524288 | tf_op jit(solution)/shard_map/all_to_all | solution.py:44

commit v2 on v0

v2 whole, which is shorter than its diff:
```python
import jax
import jax.numpy as jnp
from jax import lax
from jax.sharding import PartitionSpec as P

STEPS = 2
ADAM_STEP = 20


beta_one = 0.9
beta_two = 0.99
step_rate = 0.02
tiny_eps = 1e-08


def adam(value, grad, mean, square, count):
    drift = beta_one * mean + (1.0 - beta_one) * grad
    spread = beta_two * square + (1.0 - beta_two) * grad * grad
    fixed_one = 1.0 - beta_one**count
    fixed_two = 1.0 - beta_two**count
    value = value - step_rate * (drift / fixed_one) / (jnp.sqrt(spread / fixed_two) + tiny_eps)
    return (value, drift, spread)


def swap(x, axis, k):
    n = lax.axis_size(axis)
    return lax.ppermute(x, axis, [(i, i ^ k) for i in range(n)])


def pick(flag, x, y):
    return jnp.where(flag, y, x), jnp.where(flag, x, y)


def gather_ta(x):
    ta = lax.axis_index("ta")
    p = [x] + [swap(x, "ta", k) for k in (1, 2, 3)]
    odd, high = (ta & 1) == 1, (ta & 2) == 2
    q0, q1 = pick(odd, p[0], p[1])
    q2, q3 = pick(odd, p[2], p[3])
    q0, q2 = pick(high, q0, q2)
    q1, q3 = pick(high, q1, q3)
    return [q0, q1, q2, q3]


def sum_ta(pieces):
    ta = lax.axis_index("ta")
    got = [pieces(ta)] + [swap(pieces(ta ^ k), "ta", k) for k in (1, 2, 3)]
    return (got[0] + got[1]) + (got[2] + got[3])


def gather_first(piece):
    ja = lax.axis_index("ja")
    x = jnp.concatenate(gather_ta(piece), axis=0)
    for k in (1, 2):
        low, high = pick((ja & k) == k, x, swap(x, "ja", k))
        x = jnp.concatenate([low, high], axis=0)
    return x


def reduce_first(part, part_time):
    ja = lax.axis_index("ja")
    n_time = part_time.shape[0]
    pad = 16 - n_time
    part_time = jnp.pad(part_time, ((0, pad), (0, 0)))
    for k in (1, 2):
        half = part.shape[0] // 2
        high = (ja & k) == k
        if k == 1:
            quarter = half // 2
            q = [part[n * quarter : (n + 1) * quarter] for n in range(4)]
            keep0, send0 = pick(high, q[0], q[1])
            keep1, send1 = pick(high, q[2], q[3])
            keep = jnp.concatenate([keep0, keep1], axis=0)
            send = jnp.concatenate([send0, send1, part_time], axis=0)
        else:
            keep, send = pick(high, part[:half], part[half:])
            send = jnp.concatenate([send, part_time], axis=0)
        got = swap(send, "ja", k)
        part = keep + got[:half]
        part_time = part_time + got[half:]
    rows = part.shape[0] // 4
    mine = sum_ta(lambda t: lax.dynamic_slice_in_dim(part, t * rows, rows, axis=0))
    return mine, part_time


def flatten(piece):
    half = piece.shape[1] // 2
    return jnp.concatenate([piece[:, :half], piece[:, half:]], axis=0)


def spread_second(wide, time_parts):
    ni = lax.axis_size("ia")
    ranks, cols = wide.shape
    half = cols // 2
    flat = jnp.concatenate([wide[:, :half], wide[:, half:]], axis=0)
    if time_parts is not None:
        rows, rank = time_parts.shape
        t_rows = rows * rank // half
        per = half // rank
        line = jnp.concatenate([time_parts[n * t_rows : (n + 1) * t_rows] for n in range(per)], axis=1)
        top = lax.reduce_precision(line, 8, 7)
        low = (line - top).astype(jnp.bfloat16)
        flat = jnp.concatenate([flat, top.astype(jnp.bfloat16), low], axis=0)
    got = lax.all_to_all(jnp.broadcast_to(flat, (ni,) + flat.shape), "ia", 0, 0)
    b16 = jnp.concatenate(
        [
            got[:, :ranks].reshape(ni * ranks, half),
            got[:, ranks : 2 * ranks].reshape(ni * ranks, half),
        ],
        axis=1,
    )
    if time_parts is None:
        return b16, None
    top = got[:, 2 * ranks : 2 * ranks + t_rows].astype(jnp.float32)
    low = got[:, 2 * ranks + t_rows :].astype(jnp.float32)
    line = jnp.sum(top + low, axis=0)
    time_sum = jnp.concatenate([line[:, n * rank : (n + 1) * rank] for n in range(per)], axis=0)
    return b16, time_sum


def parts(readings, a16, b16, c16):
    af = a16.astype(jnp.float32)
    cf = c16.astype(jnp.float32)
    scaled = (af[None, :, :] * cf[:, None, :]).astype(jnp.bfloat16)
    model = lax.dot_general(
        scaled, b16, (((2,), (0,)), ((), ())), preferred_element_type=jnp.float32
    )
    slope = (1.0 / model - readings.astype(jnp.float32) / (model * model)).astype(jnp.bfloat16)
    part_second = lax.dot_general(
        scaled, slope, (((0, 1), (0, 1)), ((), ())), preferred_element_type=jnp.float32
    )
    cross = lax.dot_general(
        slope, b16, (((2,), (1,)), ((), ())), preferred_element_type=jnp.float32
    )
    part_first = jnp.sum(cross * cf[:, None, :], axis=0)
    part_time = jnp.sum(cross * af[None, :, :], axis=1)
    return part_first, part_second, part_time


def body(
    readings,
    factor_first,
    factor_second,
    factor_time,
    mean_first,
    square_first,
    mean_second,
    square_second,
    mean_time,
    square_time,
):
    ni, nj, nt = lax.axis_size("ia"), lax.axis_size("ja"), lax.axis_size("ta")
    whole_i = readings.shape[1] * ni
    whole_j = readings.shape[2] * nj
    whole_k = readings.shape[0] * nt
    n_time, rank = factor_time.shape
    scale_first = rank / (whole_j * whole_k)
    scale_second = rank / (whole_i * whole_k)
    scale_time = rank / (whole_i * whole_j)
    ranks, cols = factor_second.shape
    ta = lax.axis_index("ta")

    pieces = gather_ta(flatten(factor_second.astype(jnp.bfloat16)))
    wide = jnp.concatenate([p for q in pieces for p in (q[:ranks], q[ranks:])], axis=1)
    a16 = gather_first(factor_first.astype(jnp.bfloat16))
    b16, _ = spread_second(wide, None)
    c16 = factor_time.astype(jnp.bfloat16)
    part_first, part_second, part_time = parts(readings, a16, b16, c16)

    state = jnp.concatenate([factor_second, mean_second, square_second], axis=0)
    state, part_second = lax.optimization_barrier((state, part_second))
    state = jnp.concatenate(gather_ta(state), axis=1)

    mine_first, time_ja = reduce_first(part_first, part_time)
    got = lax.all_to_all(part_second.reshape(ni, ranks, nt * cols), "ia", 0, 0)
    second = jnp.sum(got, axis=0)
    second = (second + swap(second, "ta", 1)) + (swap(second, "ta", 2) + swap(second, "ta", 3))
    count = ADAM_STEP + 1
    wide_second, wide_mean, wide_square = adam(
        state[:ranks],
        second * scale_second,
        state[ranks : 2 * ranks],
        state[2 * ranks :],
        count,
    )
    factor_first, mean_first, square_first = adam(
        factor_first, mine_first * scale_first, mean_first, square_first, count
    )

    a16 = gather_first(factor_first.astype(jnp.bfloat16))
    b16, time_sum = spread_second(wide_second.astype(jnp.bfloat16), time_ja)
    factor_time, mean_time, square_time = adam(
        factor_time, time_sum[:n_time] * scale_time, mean_time, square_time, count
    )
    c16 = factor_time.astype(jnp.bfloat16)
    part_first, part_second, part_time = parts(readings, a16, b16, c16)
    mine_first, time_ja = reduce_first(part_first, part_time)
    got = lax.all_to_all(part_second.reshape(ni, ranks, nt * cols), "ia", 0, 0)
    second = jnp.sum(got, axis=0)
    mine_second = sum_ta(lambda t: lax.dynamic_slice_in_dim(second, t * cols, cols, axis=1))
    time_sum = jnp.sum(
        lax.all_to_all(jnp.broadcast_to(time_ja, (ni,) + time_ja.shape), "ia", 0, 0), axis=0
    )
    count = ADAM_STEP + 2
    own = lambda x: lax.dynamic_slice_in_dim(x, ta * cols, cols, axis=1)
    factor_first, mean_first, square_first = adam(
        factor_first, mine_first * scale_first, mean_first, square_first, count
    )
    factor_second, mean_second, square_second = adam(
        own(wide_second), mine_second * scale_second, own(wide_mean), own(wide_square), count
    )
    factor_time, mean_time, square_time = adam(
        factor_time, time_sum[:n_time] * scale_time, mean_time, square_time, count
    )
    return (
        factor_first,
        factor_second,
        factor_time,
        mean_first,
        square_first,
        mean_second,
        square_second,
        mean_time,
        square_time,
    )


def solution(mesh):
    first = P(("ia", "ja", "ta"), None)
    second = P("ia", ("ja", "ta"))
    time = P("ta", None)
    return jax.shard_map(
        body,
        mesh=mesh,
        in_specs=(
            P("ta", "ia", "ja"),
            first,
            second,
            time,
            first,
            first,
            second,
            second,
            time,
            time,
        ),
        out_specs=(first, second, time, first, first, second, second, time, time),
        check_vma=False,
    )
```

time: 666 us -> 157 us (0.24)
  blocking collectives: 531 us -> 0 us
  starting transfers between devices: 0.25 us -> 71.4 us
  waiting for transfers between devices: 73.8 us -> 52.6 us
  between operations: 16.6 us -> 1.18 us
    psum x2 -> x0, blocking collectives: 406 us -> none  [body(): grad_time = lax.psum(part_time, ('ia', 'ja')) * (rank / (whole_i * whole_j))]
    all_gather x6 -> x0, blocking collectives: 125 us -> none  [the longest x2 52.3 us: body(): lax.all_gather(factor_first.astype(jnp.bfloat16), ('ja', 'ta'), axis=0, t...]
    reduce_scatter x4 -> x0, waiting for transfers between devices: 73.6 us -> none  [the longest x2 49.9 us: body(): lax.psum_scatter(part_first, ('ja', 'ta'), scatter_dimension=0, tiled=True)]
    ppermute x0 -> x32, starting transfers between devices: none -> 46.1 us  [swap(): return lax.ppermute(x, axis, [(i, i ^ k) for i in range(n)])]
    ppermute x0 -> x32, waiting for transfers between devices: none -> 28.9 us  [swap(): return lax.ppermute(x, axis, [(i, i ^ k) for i in range(n)])]
    all_to_all x0 -> x5, starting transfers between devices: none -> 25.3 us  [the longest x2 14.2 us: spread_second(): got = lax.all_to_all(jnp.broadcast_to(flat, (ni,) + flat.shape), 'ia', 0, 0)]
    all_to_all x0 -> x5, waiting for transfers between devices: none -> 23.6 us  [the longest x2 18 us: spread_second(): got = lax.all_to_all(jnp.broadcast_to(flat, (ni,) + flat.shape), 'ia', 0, 0)]
    unnamed x31 -> x14, local copies, waits for them, and re-layouts: 8.7 us -> 0.86 us
  transfers between devices with their start and end apart: 6 -> 37, of which waited for: 2 -> 23; matrix products, arithmetic and copies ran while one was open for 3% -> 6% of each run, Pallas kernels for 0% -> 0%
where the time goes in v2:
time: 157 us; the launch traced here: 156 us
  starting transfers between devices  71.4 us (45%)
  waiting for transfers between devices  52.6 us (34%)
  matrix products  21.4 us (14%)
  other arithmetic  5.98 us (4%)
  local copies, waits for them, and re-layouts  3.15 us (2%)
    ppermute x32, starting transfers between devices, swap(): return lax.ppermute(x, axis, [(i, i ^ k) for i in range(n)])  46.1 us
    ppermute x32, waiting for transfers between devices, swap(): return lax.ppermute(x, axis, [(i, i ^ k) for i in range(n)])  28.9 us
    all_to_all x2, waiting for transfers between devices, spread_second(): got = lax.all_to_all(jnp.broadcast_to(flat, (ni,) + flat.shape), 'ia', 0, 0)  18 us
    all_to_all x2, starting transfers between devices, spread_second(): got = lax.all_to_all(jnp.broadcast_to(flat, (ni,) + flat.shape), 'ia', 0, 0)  14.2 us
    dot_general x2, matrix products, parts(): lax.dot_general(scaled, b16, (((2,), (0,)), ((), ())), preferred_element_...  11.2 us
    all_to_all x2, starting transfers between devices, body(): got = lax.all_to_all(part_second.reshape(ni, ranks, nt * cols), 'ia', 0, 0)  7.43 us
    dot_general x2, matrix products, parts(): lax.dot_general(scaled, slope, (((0, 1), (0, 1)), ((), ())), preferred_el...  6.52 us
    dot_general x2, matrix products, parts(): lax.dot_general(slope, b16, (((2,), (1,)), ((), ())), preferred_element_t...  3.77 us
  transfers between devices with their start and end apart: 37, of which 23 were waited for; matrix products, arithmetic and copies ran while one was open for 6% of the time, Pallas kernels for 0%

profile of v2, /device:TPU:32, one launch (start us, length us, event | category | flops | bytes accessed | tf_op | source)
XLA Modules:
  0.0 155.8 jit_solution(9692526431127455825)
XLA Ops:
  1.4 1.9 %collective-permute-start.5 = (bf16[16,128]{1,0:T(8,128)(2,1)S(1)}, bf16[16,128]{1,0:T(8,128)(2,1)S(1)}, u32[]{:S(2)}, u32[]{:S(2)}) collective-permute-start(bf16[16,128]{1,0:T(8,128)(2,1)S(1)} %pad_maximum_fusion.13), channel_id=1, source_target_pairs={{0,3},{1,2},{2,1},{3,0},{4,7},{5,6},{6,5},{7,4},{8,11},{9,10},{10,... | collective-permute-start | bytes 12296 | tf_op jit(solution)/shard_map/ppermute | solution.py:27
  3.3 2.3 %collective-permute-start.6 = (bf16[16,128]{1,0:T(8,128)(2,1)S(1)}, bf16[16,128]{1,0:T(8,128)(2,1)S(1)}, u32[]{:S(2)}, u32[]{:S(2)}) collective-permute-start(bf16[16,128]{1,0:T(8,128)(2,1)S(1)} %pad_maximum_fusion.13), channel_id=1, source_target_pairs={{0,2},{1,3},{2,0},{3,1},{4,6},{5,7},{6,4},{7,5},{8,10},{9,11},{10,... | collective-permute-start | bytes 12296 | tf_op jit(solution)/shard_map/ppermute | solution.py:27
  6.8 2.9 %collective-permute-start.1 = (bf16[16,128]{1,0:T(8,128)(2,1)S(1)}, bf16[16,128]{1,0:T(8,128)(2,1)S(1)}, u32[]{:S(2)}, u32[]{:S(2)}) collective-permute-start(bf16[16,128]{1,0:T(8,128)(2,1)S(1)} %convert_element_type.69), channel_id=1, source_target_pairs={{0,2},{1,3},{2,0},{3,1},{4,6},{5,7},{6,4},{7,5},{8,10},{9,11},{10,... | collective-permute-start | bytes 12296 | tf_op jit(solution)/shard_map/ppermute | solution.py:27
  16.1 5.5 %collective-permute-start.4 = (bf16[128,128]{1,0:T(8,128)(2,1)S(1)}, bf16[128,128]{1,0:T(8,128)(2,1)S(1)}, u32[]{:S(2)}, u32[]{:S(2)}) collective-permute-start(bf16[128,128]{1,0:T(8,128)(2,1)S(1)} %pad_maximum_fusion.5), channel_id=1, source_target_pairs={{0,8},{4,12},{8,0},{12,4},{1,9},{5,13},{9,1},{13,5},{2,10},{6,14},... | collective-permute-start | bytes 98312 | tf_op jit(solution)/shard_map/ppermute | solution.py:27
  22.4 7.0 %all-to-all-start = ((bf16[16,16,512]{2,1,0:T(8,128)(2,1)}), bf16[16,16,512]{2,1,0:T(8,128)(2,1)S(1)}, u32[]{:S(2)}, u32[]{:S(2)}) async-start(bf16[16,16,512]{2,1,0:T(8,128)(2,1)} %broadcast_in_dim.6), calls=%async_computation | async-start | bytes 524288 | tf_op jit(solution)/shard_map/all_to_all | solution.py:104
  29.5 8.7 %all-to-all-done = bf16[16,16,512]{2,1,0:T(8,128)(2,1)S(1)} async-done(((bf16[16,16,512]{2,1,0:T(8,128)(2,1)}), bf16[16,16,512]{2,1,0:T(8,128)(2,1)S(1)}, u32[]{:S(2)}, u32[]{:S(2)}) %all-to-all-start) | async-done | bytes 262176 | tf_op jit(solution)/shard_map/all_to_all | solution.py:104
  38.2 5.6 %fusion.1 = bf16[12,256,1024]{2,1,0:T(8,128)(2,1)S(1)} fusion(bf16[12,256,1024]{2,1,0:T(8,128)(2,1)} %param.10, f32[12,128]{1,0:T(8,128)S(1)} %convert_convert_fusion.1, f32[256,128]{1,0:T(8,128)S(1)} %maximum_convert_fusion, bf16[128,512]{1,0:T(8,128)(2,1)S(1)} %get-tuple-element.38, bf16[128,512]{1,0:T(8,128)(2,1)S(1)} %get-tuple-element.37), kind=kOutput, calls=%fused_computation.3 | convolution fusion | flops 825491456 | bytes 12982272 | tf_op jit(solution)/shard_map/dot_general | solution.py:125
  43.7 1.9 %multiply_reduce_fusion.3 = (f32[256,128]{1,0:T(8,128)S(1)}, f32[12,128]{1,0:T(8,128)S(1)}) fusion(f32[12,128]{1,0:T(8,128)S(1)} %convert_convert_fusion.1, f32[256,128]{1,0:T(8,128)S(1)} %maximum_convert_fusion, bf16[12,256,1024]{2,1,0:T(8,128)(2,1)S(1)} %fusion.1, bf16[128,512]{1,0:T(8,128)(2,1)S(1)} %get-tuple-element.38, ...), kind=kOutput, calls=%fused_computation.10 | convolution fusion | flops 807369216 | bytes 6828032 | tf_op jit(solution)/shard_map/dot_general | solution.py:132
  45.7 1.9 %convolution_bitcast_fusion.1 = f32[128,1024]{1,0:T(8,128)} fusion(bf16[12,256,1024]{2,1,0:T(8,128)(2,1)S(1)} %fusion.1, f32[12,128]{1,0:T(8,128)S(1)} %convert_convert_fusion.1, f32[256,128]{1,0:T(8,128)S(1)} %maximum_convert_fusion), kind=kOutput, calls=%fused_computation.13 | convolution fusion | flops 806092800 | bytes 6952960 | tf_op jit(solution)/shard_map/dot_general | solution.py:129
  48.6 2.4 %collective-permute-start.19 = (f32[24,256]{1,0:T(8,128)S(1)}, f32[24,256]{1,0:T(8,128)S(1)}, u32[]{:S(2)}, u32[]{:S(2)}) collective-permute-start(f32[24,256]{1,0:T(8,128)S(1)} %pad_maximum_fusion.7), channel_id=1, source_target_pairs={{0,2},{1,3},{2,0},{3,1},{4,6},{5,7},{6,4},{7,5},{8,10},{9,11},{10,... | collective-permute-start | bytes 73736 | tf_op jit(solution)/shard_map/ppermute | solution.py:27
  51.2 3.6 %all-to-all-start.1 = ((f32[16,8,1024]{2,1,0:T(8,128)}), f32[16,8,1024]{2,1,0:T(8,128)S(1)}, u32[]{:S(2)}, u32[]{:S(2)}) async-start(f32[16,8,1024]{2,1,0:T(8,128)} %bitcast.4), calls=%async_computation.1 | async-start | bytes 1048576 | tf_op jit(solution)/shard_map/all_to_all | solution.py:175
  56.0 7.1 %collective-permute-done.9 = f32[80,128]{1,0:T(8,128)S(1)} collective-permute-done((f32[80,128]{1,0:T(8,128)S(1)}, f32[80,128]{1,0:T(8,128)S(1)}, u32[]{:S(2)}, u32[]{:S(2)}) %collective-permute-start.9) | collective-permute-done | bytes 40992 | tf_op jit(solution)/shard_map/ppermute | solution.py:27
  63.1 2.5 %collective-permute-start.11 = (f32[16,128]{1,0:T(8,128)S(1)}, f32[16,128]{1,0:T(8,128)S(1)}, u32[]{:S(2)}, u32[]{:S(2)}) collective-permute-start(f32[16,128]{1,0:T(8,128)S(1)} %get-tuple-element.65), channel_id=1, source_target_pairs={{0,2},{1,3},{2,0},{3,1},{4,6},{5,7},{6,4},{7,5},{8,10},{9,11},{10,... | collective-permute-start | bytes 24584 | tf_op jit(solution)/shard_map/ppermute | solution.py:27
  67.8 1.5 collective-permute-done.12
  71.4 2.4 %collective-permute-start.14 = (bf16[16,128]{1,0:T(8,128)(2,1)S(1)}, bf16[16,128]{1,0:T(8,128)(2,1)S(1)}, u32[]{:S(2)}, u32[]{:S(2)}) collective-permute-start(bf16[16,128]{1,0:T(8,128)(2,1)S(1)} %get-tuple-element.26), channel_id=1, source_target_pairs={{0,2},{1,3},{2,0},{3,1},{4,6},{5,7},{6,4},{7,5},{8,10},{9,11},{10,... | collective-permute-start | bytes 12296 | tf_op jit(solution)/shard_map/ppermute | solution.py:27
  74.0 1.9 %collective-permute-done.14 = bf16[16,128]{1,0:T(8,128)(2,1)S(1)} collective-permute-done((bf16[16,128]{1,0:T(8,128)(2,1)S(1)}, bf16[16,128]{1,0:T(8,128)(2,1)S(1)}, u32[]{:S(2)}, u32[]{:S(2)}) %collective-permute-start.14) | collective-permute-done | bytes 4128 | tf_op jit(solution)/shard_map/ppermute | solution.py:27
  75.9 1.5 collective-permute-done.15
  80.7 2.4 %collective-permute-start.21 = (f32[8,1024]{1,0:T(8,128)S(1)}, f32[8,1024]{1,0:T(8,128)S(1)}, u32[]{:S(2)}, u32[]{:S(2)}) collective-permute-start(f32[8,1024]{1,0:T(8,128)S(1)} %reduce_sum.74), channel_id=1, source_target_pairs={{0,1},{1,0},{2,3},{3,2},{4,5},{5,4},{6,7},{7,6},{8,9},{9,8},{10,11... | collective-permute-start | bytes 98312 | tf_op jit(solution)/shard_map/ppermute | solution.py:27
  86.6 7.2 %all-to-all-start.2 = ((bf16[16,24,512]{2,1,0:T(8,128)(2,1)}), bf16[16,24,512]{2,1,0:T(8,128)(2,1)S(1)}, u32[]{:S(2)}, u32[]{:S(2)}) async-start(bf16[16,24,512]{2,1,0:T(8,128)(2,1)} %broadcast_in_dim.7), calls=%async_computation.2 | async-start | bytes 786432 | tf_op jit(solution)/shard_map/all_to_all | solution.py:104
  93.8 9.3 %all-to-all-done.2 = bf16[16,24,512]{2,1,0:T(8,128)(2,1)S(1)} async-done(((bf16[16,24,512]{2,1,0:T(8,128)(2,1)}), bf16[16,24,512]{2,1,0:T(8,128)(2,1)S(1)}, u32[]{:S(2)}, u32[]{:S(2)}) %all-to-all-start.2) | async-done | bytes 393248 | tf_op jit(solution)/shard_map/all_to_all | solution.py:104
  103.3 5.6 %fusion.3 = bf16[12,256,1024]{2,1,0:T(8,128)(2,1)S(1)} fusion(bf16[12,256,1024]{2,1,0:T(8,128)(2,1)} %param.10, f32[12,128]{1,0:T(8,128)S(1)} %get-tuple-element.29, f32[256,128]{1,0:T(8,128)S(1)} %maximum_convert_fusion.1, bf16[128,512]{1,0:T(8,128)(2,1)S(1)} %get-tuple-element.36, bf16[128,512]{1,0:T(8,128)(2,1)S(1)} %get-tuple-element.35), kind=kOutput, calls=%fused_computation.5 | convolution fusion | flops 825491456 | bytes 12982272 | tf_op jit(solution)/shard_map/dot_general | solution.py:125
  109.0 1.9 %multiply_reduce_fusion.1 = (f32[256,128]{1,0:T(8,128)S(1)}, f32[12,128]{1,0:T(8,128)S(1)}) fusion(f32[12,128]{1,0:T(8,128)S(1)} %get-tuple-element.29, f32[256,128]{1,0:T(8,128)S(1)} %maximum_convert_fusion.1, bf16[12,256,1024]{2,1,0:T(8,128)(2,1)S(1)} %fusion.3, bf16[128,512]{1,0:T(8,128)(2,1)S(1)} %get-tuple-element.36, ...), kind=kOutput, calls=%fused_computation.7 | convolution fusion | flops 807369216 | bytes 6828032 | tf_op jit(solution)/shard_map/dot_general | solution.py:132
  113.1 3.5 %collective-permute-start.25 = (f32[80,128]{1,0:T(8,128)S(1)}, f32[80,128]{1,0:T(8,128)S(1)}, u32[]{:S(2)}, u32[]{:S(2)}) collective-permute-start(f32[80,128]{1,0:T(8,128)S(1)} %pad_maximum_fusion.4), channel_id=1, source_target_pairs={{0,8},{4,12},{8,0},{12,4},{1,9},{5,13},{9,1},{13,5},{2,10},{6,14},... | collective-permute-start | bytes 122888 | tf_op jit(solution)/shard_map/ppermute | solution.py:27
  116.5 4.5 %collective-permute-done.25 = f32[80,128]{1,0:T(8,128)S(1)} collective-permute-done((f32[80,128]{1,0:T(8,128)S(1)}, f32[80,128]{1,0:T(8,128)S(1)}, u32[]{:S(2)}, u32[]{:S(2)}) %collective-permute-start.25) | collective-permute-done | bytes 40992 | tf_op jit(solution)/shard_map/ppermute | solution.py:27
  121.7 3.7 %all-to-all-start.4 = ((f32[16,16,128]{2,1,0:T(8,128)}), f32[16,16,128]{2,1,0:T(8,128)S(1)}, u32[]{:S(2)}, u32[]{:S(2)}) async-start(f32[16,16,128]{2,1,0:T(8,128)} %broadcast_in_dim.8), calls=%async_computation.4 | async-start | bytes 262144 | tf_op jit(solution)/shard_map/all_to_all | solution.py:202
  125.5 4.6 %convolution_bitcast_fusion = f32[16,8,1024]{2,1,0:T(8,128)} fusion(bf16[12,256,1024]{2,1,0:T(8,128)(2,1)} %copy-done, f32[12,128]{1,0:T(8,128)S(1)} %get-tuple-element.29, f32[256,128]{1,0:T(8,128)S(1)} %maximum_convert_fusion.1), kind=kOutput, calls=%fused_computation.12 | convolution fusion | flops 806092800 | bytes 6952960 | tf_op jit(solution)/shard_map/dot_general | solution.py:129
  130.1 3.3 %all-to-all-done.4 = f32[16,16,128]{2,1,0:T(8,128)S(1)} async-done(((f32[16,16,128]{2,1,0:T(8,128)}), f32[16,16,128]{2,1,0:T(8,128)S(1)}, u32[]{:S(2)}, u32[]{:S(2)}) %all-to-all-start.4) | async-done | bytes 131104 | tf_op jit(solution)/shard_map/all_to_all | solution.py:202
  133.4 3.8 %all-to-all-start.3 = ((f32[16,8,1024]{2,1,0:T(8,128)}), f32[16,8,1024]{2,1,0:T(8,128)S(1)}, u32[]{:S(2)}, u32[]{:S(2)}) async-start(f32[16,8,1024]{2,1,0:T(8,128)} %convolution_bitcast_fusion), calls=%async_computation.3 | async-start | bytes 1048576 | tf_op jit(solution)/shard_map/all_to_all | solution.py:198
  137.3 3.1 %collective-permute-start.27 = (f32[16,128]{1,0:T(8,128)S(1)}, f32[16,128]{1,0:T(8,128)S(1)}, u32[]{:S(2)}, u32[]{:S(2)}) collective-permute-start(f32[16,128]{1,0:T(8,128)S(1)} %get-tuple-element.60), channel_id=1, source_target_pairs={{0,2},{1,3},{2,0},{3,1},{4,6},{5,7},{6,4},{7,5},{8,10},{9,11},{10,... | collective-permute-start | bytes 24584 | tf_op jit(solution)/shard_map/ppermute | solution.py:27
  142.1 2.0 %collective-permute-done.28 = f32[16,128]{1,0:T(8,128)S(1)} collective-permute-done((f32[16,128]{1,0:T(8,128)S(1)}, f32[16,128]{1,0:T(8,128)S(1)}, u32[]{:S(2)}, u32[]{:S(2)}) %collective-permute-start.28) | collective-permute-done | bytes 8224 | tf_op jit(solution)/shard_map/ppermute | solution.py:27
  145.4 2.3 %all-to-all-done.3 = f32[16,8,1024]{2,1,0:T(8,128)S(1)} async-done(((f32[16,8,1024]{2,1,0:T(8,128)}), f32[16,8,1024]{2,1,0:T(8,128)S(1)}, u32[]{:S(2)}, u32[]{:S(2)}) %all-to-all-start.3) | async-done | bytes 524320 | tf_op jit(solution)/shard_map/all_to_all | solution.py:198
  147.8 2.7 %collective-permute-start.30 = (f32[8,256]{1,0:T(8,128)S(1)}, f32[8,256]{1,0:T(8,128)S(1)}, u32[]{:S(2)}, u32[]{:S(2)}) collective-permute-start(f32[8,256]{1,0:T(8,128)S(1)} %get-tuple-element.57), channel_id=1, source_target_pairs={{0,2},{1,3},{2,0},{3,1},{4,6},{5,7},{6,4},{7,5},{8,10},{9,11},{10,... | collective-permute-start | bytes 24584 | tf_op jit(solution)/shard_map/ppermute | solution.py:27
  (128 shorter events, 34.2 us)
Async XLA Ops:
  1.4 9.1 %collective-permute-start.5 = (bf16[16,128]{1,0:T(8,128)(2,1)S(1)}, bf16[16,128]{1,0:T(8,128)(2,1)S(1)}, u32[]{:S(2)}, u32[]{:S(2)}) collective-permute-start(bf16[16,128]{1,0:T(8,128)(2,1)S(1)} %pad_maximum_fusion.13), channel_id=1, source_target_pairs={{0,3},{1,2},{2,1},{3,0},{4,7},{5,6},{6,5},{7,4},{8,11},{9,10},{10,... | collective-permute-start | bytes 12296 | tf_op jit(solution)/shard_map/ppermute | solution.py:27
  3.3 9.4 %collective-permute-start.6 = (bf16[16,128]{1,0:T(8,128)(2,1)S(1)}, bf16[16,128]{1,0:T(8,128)(2,1)S(1)}, u32[]{:S(2)}, u32[]{:S(2)}) collective-permute-start(bf16[16,128]{1,0:T(8,128)(2,1)S(1)} %pad_maximum_fusion.13), channel_id=1, source_target_pairs={{0,2},{1,3},{2,0},{3,1},{4,6},{5,7},{6,4},{7,5},{8,10},{9,11},{10,... | collective-permute-start | bytes 12296 | tf_op jit(solution)/shard_map/ppermute | solution.py:27
  5.6 7.1 %collective-permute-start.7 = (bf16[16,128]{1,0:T(8,128)(2,1)S(1)}, bf16[16,128]{1,0:T(8,128)(2,1)S(1)}, u32[]{:S(2)}, u32[]{:S(2)}) collective-permute-start(bf16[16,128]{1,0:T(8,128)(2,1)S(1)} %pad_maximum_fusion.13), channel_id=1, source_target_pairs={{0,1},{1,0},{2,3},{3,2},{4,5},{5,4},{6,7},{7,6},{8,9},{9,8},{10,11... | collective-permute-start | bytes 12296 | tf_op jit(solution)/shard_map/ppermute | solution.py:27
  6.8 5.8 %collective-permute-start.1 = (bf16[16,128]{1,0:T(8,128)(2,1)S(1)}, bf16[16,128]{1,0:T(8,128)(2,1)S(1)}, u32[]{:S(2)}, u32[]{:S(2)}) collective-permute-start(bf16[16,128]{1,0:T(8,128)(2,1)S(1)} %convert_element_type.69), channel_id=1, source_target_pairs={{0,2},{1,3},{2,0},{3,1},{4,6},{5,7},{6,4},{7,5},{8,10},{9,11},{10,... | collective-permute-start | bytes 12296 | tf_op jit(solution)/shard_map/ppermute | solution.py:27
  10.5 3.6 %collective-permute-start.2 = (bf16[16,128]{1,0:T(8,128)(2,1)S(1)}, bf16[16,128]{1,0:T(8,128)(2,1)S(1)}, u32[]{:S(2)}, u32[]{:S(2)}) collective-permute-start(bf16[16,128]{1,0:T(8,128)(2,1)S(1)} %convert_element_type.69), channel_id=1, source_target_pairs={{0,1},{1,0},{2,3},{3,2},{4,5},{5,4},{6,7},{7,6},{8,9},{9,8},{10,11... | collective-permute-start | bytes 12296 | tf_op jit(solution)/shard_map/ppermute | solution.py:27
  16.1 13.3 %collective-permute-start.4 = (bf16[128,128]{1,0:T(8,128)(2,1)S(1)}, bf16[128,128]{1,0:T(8,128)(2,1)S(1)}, u32[]{:S(2)}, u32[]{:S(2)}) collective-permute-start(bf16[128,128]{1,0:T(8,128)(2,1)S(1)} %pad_maximum_fusion.5), channel_id=1, source_target_pairs={{0,8},{4,12},{8,0},{12,4},{1,9},{5,13},{9,1},{13,5},{2,10},{6,14},... | collective-permute-start | bytes 98312 | tf_op jit(solution)/shard_map/ppermute | solution.py:27
  22.4 15.8 %all-to-all-start = ((bf16[16,16,512]{2,1,0:T(8,128)(2,1)}), bf16[16,16,512]{2,1,0:T(8,128)(2,1)S(1)}, u32[]{:S(2)}, u32[]{:S(2)}) async-start(bf16[16,16,512]{2,1,0:T(8,128)(2,1)} %broadcast_in_dim.6), calls=%async_computation | async-start | bytes 524288 | tf_op jit(solution)/shard_map/all_to_all | solution.py:104
  47.6 7.2 %collective-permute-start.18 = (f32[24,256]{1,0:T(8,128)S(1)}, f32[24,256]{1,0:T(8,128)S(1)}, u32[]{:S(2)}, u32[]{:S(2)}) collective-permute-start(f32[24,256]{1,0:T(8,128)S(1)} %pad_maximum_fusion.7), channel_id=1, source_target_pairs={{0,3},{1,2},{2,1},{3,0},{4,7},{5,6},{6,5},{7,4},{8,11},{9,10},{10,... | collective-permute-start | bytes 73736 | tf_op jit(solution)/shard_map/ppermute | solution.py:27
  48.6 6.2 %collective-permute-start.19 = (f32[24,256]{1,0:T(8,128)S(1)}, f32[24,256]{1,0:T(8,128)S(1)}, u32[]{:S(2)}, u32[]{:S(2)}) collective-permute-start(f32[24,256]{1,0:T(8,128)S(1)} %pad_maximum_fusion.7), channel_id=1, source_target_pairs={{0,2},{1,3},{2,0},{3,1},{4,6},{5,7},{6,4},{7,5},{8,10},{9,11},{10,... | collective-permute-start | bytes 73736 | tf_op jit(solution)/shard_map/ppermute | solution.py:27
  51.0 3.9 %collective-permute-start.20 = (f32[24,256]{1,0:T(8,128)S(1)}, f32[24,256]{1,0:T(8,128)S(1)}, u32[]{:S(2)}, u32[]{:S(2)}) collective-permute-start(f32[24,256]{1,0:T(8,128)S(1)} %pad_maximum_fusion.7), channel_id=1, source_target_pairs={{0,1},{1,0},{2,3},{3,2},{4,5},{5,4},{6,7},{7,6},{8,9},{9,8},{10,11... | collective-permute-start | bytes 73736 | tf_op jit(solution)/shard_map/ppermute | solution.py:27
  51.1 3.7 %collective-permute-start.8 = (f32[144,128]{1,0:T(8,128)S(1)}, f32[144,128]{1,0:T(8,128)S(1)}, u32[]{:S(2)}, u32[]{:S(2)}) collective-permute-start(f32[144,128]{1,0:T(8,128)S(1)} %pad_maximum_fusion.1), channel_id=1, source_target_pairs={{0,4},{4,0},{8,12},{12,8},{1,5},{5,1},{9,13},{13,9},{2,6},{6,2},{1... | collective-permute-start | bytes 221192 | tf_op jit(solution)/shard_map/ppermute | solution.py:27
  51.2 27.4 %all-to-all-start.1 = ((f32[16,8,1024]{2,1,0:T(8,128)}), f32[16,8,1024]{2,1,0:T(8,128)S(1)}, u32[]{:S(2)}, u32[]{:S(2)}) async-start(f32[16,8,1024]{2,1,0:T(8,128)} %bitcast.4), calls=%async_computation.1 | async-start | bytes 1048576 | tf_op jit(solution)/shard_map/all_to_all | solution.py:175
  54.9 8.2 %collective-permute-start.9 = (f32[80,128]{1,0:T(8,128)S(1)}, f32[80,128]{1,0:T(8,128)S(1)}, u32[]{:S(2)}, u32[]{:S(2)}) collective-permute-start(f32[80,128]{1,0:T(8,128)S(1)} %pad_maximum_fusion.3), channel_id=1, source_target_pairs={{0,8},{4,12},{8,0},{12,4},{1,9},{5,13},{9,1},{13,5},{2,10},{6,14},... | collective-permute-start | bytes 122888 | tf_op jit(solution)/shard_map/ppermute | solution.py:27
  63.1 4.6 %collective-permute-start.11 = (f32[16,128]{1,0:T(8,128)S(1)}, f32[16,128]{1,0:T(8,128)S(1)}, u32[]{:S(2)}, u32[]{:S(2)}) collective-permute-start(f32[16,128]{1,0:T(8,128)S(1)} %get-tuple-element.65), channel_id=1, source_target_pairs={{0,2},{1,3},{2,0},{3,1},{4,6},{5,7},{6,4},{7,5},{8,10},{9,11},{10,... | collective-permute-start | bytes 24584 | tf_op jit(solution)/shard_map/ppermute | solution.py:27
  65.6 3.7 %collective-permute-start.12 = (f32[16,128]{1,0:T(8,128)S(1)}, f32[16,128]{1,0:T(8,128)S(1)}, u32[]{:S(2)}, u32[]{:S(2)}) collective-permute-start(f32[16,128]{1,0:T(8,128)S(1)} %get-tuple-element.64), channel_id=1, source_target_pairs={{0,3},{1,2},{2,1},{3,0},{4,7},{5,6},{6,5},{7,4},{8,11},{9,10},{10,... | collective-permute-start | bytes 24584 | tf_op jit(solution)/shard_map/ppermute | solution.py:27
  66.6 3.7 %collective-permute-start.10 = (f32[16,128]{1,0:T(8,128)S(1)}, f32[16,128]{1,0:T(8,128)S(1)}, u32[]{:S(2)}, u32[]{:S(2)}) collective-permute-start(f32[16,128]{1,0:T(8,128)S(1)} %get-tuple-element.63), channel_id=1, source_target_pairs={{0,1},{1,0},{2,3},{3,2},{4,5},{5,4},{6,7},{7,6},{8,9},{9,8},{10,11... | collective-permute-start | bytes 24584 | tf_op jit(solution)/shard_map/ppermute | solution.py:27
  70.3 3.7 %collective-permute-start.13 = (bf16[16,128]{1,0:T(8,128)(2,1)S(1)}, bf16[16,128]{1,0:T(8,128)(2,1)S(1)}, u32[]{:S(2)}, u32[]{:S(2)}) collective-permute-start(bf16[16,128]{1,0:T(8,128)(2,1)S(1)} %get-tuple-element.26), channel_id=1, source_target_pairs={{0,3},{1,2},{2,1},{3,0},{4,7},{5,6},{6,5},{7,4},{8,11},{9,10},{10,... | collective-permute-start | bytes 12296 | tf_op jit(solution)/shard_map/ppermute | solution.py:27
  71.4 4.5 %collective-permute-start.14 = (bf16[16,128]{1,0:T(8,128)(2,1)S(1)}, bf16[16,128]{1,0:T(8,128)(2,1)S(1)}, u32[]{:S(2)}, u32[]{:S(2)}) collective-permute-start(bf16[16,128]{1,0:T(8,128)(2,1)S(1)} %get-tuple-element.26), channel_id=1, source_target_pairs={{0,2},{1,3},{2,0},{3,1},{4,6},{5,7},{6,4},{7,5},{8,10},{9,11},{10,... | collective-permute-start | bytes 12296 | tf_op jit(solution)/shard_map/ppermute | solution.py:27
  78.7 5.8 %collective-permute-start.22 = (f32[8,1024]{1,0:T(8,128)S(1)}, f32[8,1024]{1,0:T(8,128)S(1)}, u32[]{:S(2)}, u32[]{:S(2)}) collective-permute-start(f32[8,1024]{1,0:T(8,128)S(1)} %reduce_sum.74), channel_id=1, source_target_pairs={{0,2},{1,3},{2,0},{3,1},{4,6},{5,7},{6,4},{7,5},{8,10},{9,11},{10,... | collective-permute-start | bytes 98312 | tf_op jit(solution)/shard_map/ppermute | solution.py:27
  79.7 4.8 %collective-permute-start.23 = (f32[8,1024]{1,0:T(8,128)S(1)}, f32[8,1024]{1,0:T(8,128)S(1)}, u32[]{:S(2)}, u32[]{:S(2)}) collective-permute-start(f32[8,1024]{1,0:T(8,128)S(1)} %reduce_sum.74), channel_id=1, source_target_pairs={{0,3},{1,2},{2,1},{3,0},{4,7},{5,6},{6,5},{7,4},{8,11},{9,10},{10,... | collective-permute-start | bytes 98312 | tf_op jit(solution)/shard_map/ppermute | solution.py:27
  80.7 5.0 %collective-permute-start.21 = (f32[8,1024]{1,0:T(8,128)S(1)}, f32[8,1024]{1,0:T(8,128)S(1)}, u32[]{:S(2)}, u32[]{:S(2)}) collective-permute-start(f32[8,1024]{1,0:T(8,128)S(1)} %reduce_sum.74), channel_id=1, source_target_pairs={{0,1},{1,0},{2,3},{3,2},{4,5},{5,4},{6,7},{7,6},{8,9},{9,8},{10,11... | collective-permute-start | bytes 98312 | tf_op jit(solution)/shard_map/ppermute | solution.py:27
  83.2 10.6 %collective-permute-start.17 = (bf16[128,128]{1,0:T(8,128)(2,1)S(1)}, bf16[128,128]{1,0:T(8,128)(2,1)S(1)}, u32[]{:S(2)}, u32[]{:S(2)}) collective-permute-start(bf16[128,128]{1,0:T(8,128)(2,1)S(1)} %pad_maximum_fusion.6), channel_id=1, source_target_pairs={{0,8},{4,12},{8,0},{12,4},{1,9},{5,13},{9,1},{13,5},{2,10},{6,14},... | collective-permute-start | bytes 98312 | tf_op jit(solution)/shard_map/ppermute | solution.py:27
  86.6 16.6 %all-to-all-start.2 = ((bf16[16,24,512]{2,1,0:T(8,128)(2,1)}), bf16[16,24,512]{2,1,0:T(8,128)(2,1)S(1)}, u32[]{:S(2)}, u32[]{:S(2)}) async-start(bf16[16,24,512]{2,1,0:T(8,128)(2,1)} %broadcast_in_dim.7), calls=%async_computation.2 | async-start | bytes 786432 | tf_op jit(solution)/shard_map/all_to_all | solution.py:104
  113.1 8.0 %collective-permute-start.25 = (f32[80,128]{1,0:T(8,128)S(1)}, f32[80,128]{1,0:T(8,128)S(1)}, u32[]{:S(2)}, u32[]{:S(2)}) collective-permute-start(f32[80,128]{1,0:T(8,128)S(1)} %pad_maximum_fusion.4), channel_id=1, source_target_pairs={{0,8},{4,12},{8,0},{12,4},{1,9},{5,13},{9,1},{13,5},{2,10},{6,14},... | collective-permute-start | bytes 122888 | tf_op jit(solution)/shard_map/ppermute | solution.py:27
  121.7 11.7 %all-to-all-start.4 = ((f32[16,16,128]{2,1,0:T(8,128)}), f32[16,16,128]{2,1,0:T(8,128)S(1)}, u32[]{:S(2)}, u32[]{:S(2)}) async-start(f32[16,16,128]{2,1,0:T(8,128)} %broadcast_in_dim.8), calls=%async_computation.4 | async-start | bytes 262144 | tf_op jit(solution)/shard_map/all_to_all | solution.py:202
  133.4 14.3 %all-to-all-start.3 = ((f32[16,8,1024]{2,1,0:T(8,128)}), f32[16,8,1024]{2,1,0:T(8,128)S(1)}, u32[]{:S(2)}, u32[]{:S(2)}) async-start(f32[16,8,1024]{2,1,0:T(8,128)} %convolution_bitcast_fusion), calls=%async_computation.3 | async-start | bytes 1048576 | tf_op jit(solution)/shard_map/all_to_all | solution.py:198
  137.3 4.8 %collective-permute-start.27 = (f32[16,128]{1,0:T(8,128)S(1)}, f32[16,128]{1,0:T(8,128)S(1)}, u32[]{:S(2)}, u32[]{:S(2)}) collective-permute-start(f32[16,128]{1,0:T(8,128)S(1)} %get-tuple-element.60), channel_id=1, source_target_pairs={{0,2},{1,3},{2,0},{3,1},{4,6},{5,7},{6,4},{7,5},{8,10},{9,11},{10,... | collective-permute-start | bytes 24584 | tf_op jit(solution)/shard_map/ppermute | solution.py:27
  140.4 3.7 %collective-permute-start.28 = (f32[16,128]{1,0:T(8,128)S(1)}, f32[16,128]{1,0:T(8,128)S(1)}, u32[]{:S(2)}, u32[]{:S(2)}) collective-permute-start(f32[16,128]{1,0:T(8,128)S(1)} %get-tuple-element.59), channel_id=1, source_target_pairs={{0,3},{1,2},{2,1},{3,0},{4,7},{5,6},{6,5},{7,4},{8,11},{9,10},{10,... | collective-permute-start | bytes 24584 | tf_op jit(solution)/shard_map/ppermute | solution.py:27
  141.1 3.7 %collective-permute-start.26 = (f32[16,128]{1,0:T(8,128)S(1)}, f32[16,128]{1,0:T(8,128)S(1)}, u32[]{:S(2)}, u32[]{:S(2)}) collective-permute-start(f32[16,128]{1,0:T(8,128)S(1)} %get-tuple-element.58), channel_id=1, source_target_pairs={{0,1},{1,0},{2,3},{3,2},{4,5},{5,4},{6,7},{7,6},{8,9},{9,8},{10,11... | collective-permute-start | bytes 24584 | tf_op jit(solution)/shard_map/ppermute | solution.py:27
  147.8 5.1 %collective-permute-start.30 = (f32[8,256]{1,0:T(8,128)S(1)}, f32[8,256]{1,0:T(8,128)S(1)}, u32[]{:S(2)}, u32[]{:S(2)}) collective-permute-start(f32[8,256]{1,0:T(8,128)S(1)} %get-tuple-element.57), channel_id=1, source_target_pairs={{0,2},{1,3},{2,0},{3,1},{4,6},{5,7},{6,4},{7,5},{8,10},{9,11},{10,... | collective-permute-start | bytes 24584 | tf_op jit(solution)/shard_map/ppermute | solution.py:27
  150.5 3.7 %collective-permute-start.31 = (f32[8,256]{1,0:T(8,128)S(1)}, f32[8,256]{1,0:T(8,128)S(1)}, u32[]{:S(2)}, u32[]{:S(2)}) collective-permute-start(f32[8,256]{1,0:T(8,128)S(1)} %get-tuple-element.56), channel_id=1, source_target_pairs={{0,3},{1,2},{2,1},{3,0},{4,7},{5,6},{6,5},{7,4},{8,11},{9,10},{10,... | collective-permute-start | bytes 24584 | tf_op jit(solution)/shard_map/ppermute | solution.py:27
  151.5 3.7 %collective-permute-start.29 = (f32[8,256]{1,0:T(8,128)S(1)}, f32[8,256]{1,0:T(8,128)S(1)}, u32[]{:S(2)}, u32[]{:S(2)}) collective-permute-start(f32[8,256]{1,0:T(8,128)S(1)} %get-tuple-element.55), channel_id=1, source_target_pairs={{0,1},{1,0},{2,3},{3,2},{4,5},{5,4},{6,7},{7,6},{8,9},{9,8},{10,11... | collective-permute-start | bytes 24584 | tf_op jit(solution)/shard_map/ppermute | solution.py:27
  (12 other events, 260.4 us)

commit v3 on v2

--- a/solution.py
+++ b/solution.py
@@ -31,37 +31,44 @@
     return jnp.where(flag, y, x), jnp.where(flag, x, y)
 
 
-def gather_ta(x):
-    ta = lax.axis_index("ta")
+def exchange_ta(slots):
+    return lax.all_to_all(slots, "ta", 0, 0)
+
+
+def stack_columns(x):
+    return jnp.concatenate([x[:, n * 128 : (n + 1) * 128] for n in range(x.shape[1] // 128)], axis=0)
+
+
+def unstack_columns(x, ranks):
+    return jnp.concatenate([x[n * ranks : (n + 1) * ranks] for n in range(x.shape[0] // ranks)], axis=1)
+
+
+def gather_ja(x):
+    ja = lax.axis_index("ja")
+    for k in (1, 2):
+        low, high = pick((ja & k) == k, x, swap(x, "ja", k))
+        x = jnp.concatenate([low, high], axis=0)
+    return x
+
+
+def gather_pairs(piece):
+    ja, ta = lax.axis_index("ja"), lax.axis_index("ta")
+    x = piece[None]
+    for k in (2, 1):
+        low, high = pick((ja & k) == k, x, swap(x, "ja", k))
+        x = jnp.concatenate([low, high], axis=0) if k == 2 else jnp.stack([low, high], axis=1)
+    x = x.reshape((-1,) + piece.shape)
     p = [x] + [swap(x, "ta", k) for k in (1, 2, 3)]
     odd, high = (ta & 1) == 1, (ta & 2) == 2
     q0, q1 = pick(odd, p[0], p[1])
     q2, q3 = pick(odd, p[2], p[3])
     q0, q2 = pick(high, q0, q2)
     q1, q3 = pick(high, q1, q3)
-    return [q0, q1, q2, q3]
-
-
-def sum_ta(pieces):
-    ta = lax.axis_index("ta")
-    got = [pieces(ta)] + [swap(pieces(ta ^ k), "ta", k) for k in (1, 2, 3)]
-    return (got[0] + got[1]) + (got[2] + got[3])
-
-
-def gather_first(piece):
+    return jnp.stack([q0, q1, q2, q3], axis=1).reshape(-1, piece.shape[1])
+
+
+def reduce_ja(part, part_time):
     ja = lax.axis_index("ja")
-    x = jnp.concatenate(gather_ta(piece), axis=0)
-    for k in (1, 2):
-        low, high = pick((ja & k) == k, x, swap(x, "ja", k))
-        x = jnp.concatenate([low, high], axis=0)
-    return x
-
-
-def reduce_first(part, part_time):
-    ja = lax.axis_index("ja")
-    n_time = part_time.shape[0]
-    pad = 16 - n_time
-    part_time = jnp.pad(part_time, ((0, pad), (0, 0)))
     for k in (1, 2):
         half = part.shape[0] // 2
         high = (ja & k) == k
@@ -71,21 +78,23 @@
             keep0, send0 = pick(high, q[0], q[1])
             keep1, send1 = pick(high, q[2], q[3])
             keep = jnp.concatenate([keep0, keep1], axis=0)
-            send = jnp.concatenate([send0, send1, part_time], axis=0)
+            send = [send0, send1]
         else:
             keep, send = pick(high, part[:half], part[half:])
-            send = jnp.concatenate([send, part_time], axis=0)
-        got = swap(send, "ja", k)
+            send = [send]
+        if part_time is not None:
+            send = send + [part_time]
+        got = swap(jnp.concatenate(send, axis=0), "ja", k)
         part = keep + got[:half]
-        part_time = part_time + got[half:]
-    rows = part.shape[0] // 4
-    mine = sum_ta(lambda t: lax.dynamic_slice_in_dim(part, t * rows, rows, axis=0))
-    return mine, part_time
-
-
-def flatten(piece):
-    half = piece.shape[1] // 2
-    return jnp.concatenate([piece[:, :half], piece[:, half:]], axis=0)
+        if part_time is not None:
+            part_time = part_time + got[half:]
+    return part, part_time
+
+
+def sum_ja(x):
+    for k in (1, 2):
+        x = x + swap(x, "ja", k)
+    return x
 
 
 def spread_second(wide, time_parts):
@@ -129,6 +138,7 @@
     part_second = lax.dot_general(
         scaled, slope, (((0, 1), (0, 1)), ((), ())), preferred_element_type=jnp.float32
     )
+    slope, part_second = lax.optimization_barrier((slope, part_second))
     cross = lax.dot_general(
         slope, b16, (((2,), (1,)), ((), ())), preferred_element_type=jnp.float32
     )
@@ -160,54 +170,86 @@
     ranks, cols = factor_second.shape
     ta = lax.axis_index("ta")
 
-    pieces = gather_ta(flatten(factor_second.astype(jnp.bfloat16)))
-    wide = jnp.concatenate([p for q in pieces for p in (q[:ranks], q[ranks:])], axis=1)
-    a16 = gather_first(factor_first.astype(jnp.bfloat16))
-    b16, _ = spread_second(wide, None)
+    rows = factor_first.shape[0]
+    flat = 2 * ranks
+    pad_time = ((0, 16 - n_time), (0, 0))
+
+    slot = jnp.concatenate(
+        [factor_first]
+        + [stack_columns(x) for x in (factor_second, mean_second, square_second)],
+        axis=0,
+    )
+    got = exchange_ta(jnp.broadcast_to(slot, (nt,) + slot.shape))
+    a16 = gather_ja(got[:, :rows].astype(jnp.bfloat16).reshape(nt * rows, rank))
+    wide_second, wide_mean, wide_square = [
+        unstack_columns(got[:, n : n + flat].reshape(nt * flat, rank), ranks)
+        for n in (rows, rows + flat, rows + 2 * flat)
+    ]
+    b16, _ = spread_second(wide_second.astype(jnp.bfloat16), None)
     c16 = factor_time.astype(jnp.bfloat16)
     part_first, part_second, part_time = parts(readings, a16, b16, c16)
 
-    state = jnp.concatenate([factor_second, mean_second, square_second], axis=0)
-    state, part_second = lax.optimization_barrier((state, part_second))
-    state = jnp.concatenate(gather_ta(state), axis=1)
-
-    mine_first, time_ja = reduce_first(part_first, part_time)
-    got = lax.all_to_all(part_second.reshape(ni, ranks, nt * cols), "ia", 0, 0)
-    second = jnp.sum(got, axis=0)
-    second = (second + swap(second, "ta", 1)) + (swap(second, "ta", 2) + swap(second, "ta", 3))
+    second = jnp.sum(
+        lax.all_to_all(part_second.reshape(ni, ranks, nt * cols), "ia", 0, 0), axis=0
+    )
+    part_first, time_ja = reduce_ja(part_first, jnp.pad(part_time, pad_time))
+    second = stack_columns(second)
+    slots = jnp.concatenate(
+        [part_first.reshape(nt, rows, rank), jnp.broadcast_to(second, (nt,) + second.shape)],
+        axis=1,
+    )
+    got = jnp.sum(exchange_ta(slots), axis=0)
     count = ADAM_STEP + 1
+    factor_first, mean_first, square_first = adam(
+        factor_first, got[:rows] * scale_first, mean_first, square_first, count
+    )
     wide_second, wide_mean, wide_square = adam(
-        state[:ranks],
-        second * scale_second,
-        state[ranks : 2 * ranks],
-        state[2 * ranks :],
-        count,
-    )
-    factor_first, mean_first, square_first = adam(
-        factor_first, mine_first * scale_first, mean_first, square_first, count
-    )
-
-    a16 = gather_first(factor_first.astype(jnp.bfloat16))
+        wide_second, unstack_columns(got[rows:], ranks) * scale_second, wide_mean, wide_square, count
+    )
+
+    a16 = gather_pairs(factor_first.astype(jnp.bfloat16))
     b16, time_sum = spread_second(wide_second.astype(jnp.bfloat16), time_ja)
     factor_time, mean_time, square_time = adam(
         factor_time, time_sum[:n_time] * scale_time, mean_time, square_time, count
     )
     c16 = factor_time.astype(jnp.bfloat16)
     part_first, part_second, part_time = parts(readings, a16, b16, c16)
-    mine_first, time_ja = reduce_first(part_first, part_time)
-    got = lax.all_to_all(part_second.reshape(ni, ranks, nt * cols), "ia", 0, 0)
-    second = jnp.sum(got, axis=0)
-    mine_second = sum_ta(lambda t: lax.dynamic_slice_in_dim(second, t * cols, cols, axis=1))
-    time_sum = jnp.sum(
-        lax.all_to_all(jnp.broadcast_to(time_ja, (ni,) + time_ja.shape), "ia", 0, 0), axis=0
-    )
+    line = jnp.pad(part_time, pad_time)
+    line = jnp.concatenate([line[:ranks], line[ranks:]], axis=1)
+    got = jnp.sum(
+        lax.all_to_all(
+            jnp.concatenate(
+                [
+                    part_second.reshape(ni, ranks, nt * cols),
+                    jnp.broadcast_to(line, (ni,) + line.shape),
+                ],
+                axis=2,
+            ),
+            "ia",
+            0,
+            0,
+        ),
+        axis=0,
+    )
+    part_first, _ = reduce_ja(part_first, None)
+    line = got[:, nt * cols :]
+    time_sum = sum_ja(jnp.concatenate([line[:, :rank], line[:, rank:]], axis=0))
+    second = stack_columns(got[:, : nt * cols])
+    slots = jnp.concatenate(
+        [part_first.reshape(nt, rows, rank), second.reshape(nt, flat, rank)], axis=1
+    )
+    got = jnp.sum(exchange_ta(slots), axis=0)
     count = ADAM_STEP + 2
     own = lambda x: lax.dynamic_slice_in_dim(x, ta * cols, cols, axis=1)
     factor_first, mean_first, square_first = adam(
-        factor_first, mine_first * scale_first, mean_first, square_first, count
+        factor_first, got[:rows] * scale_first, mean_first, square_first, count
     )
     factor_second, mean_second, square_second = adam(
-        own(wide_second), mine_second * scale_second, own(wide_mean), own(wide_square), count
+        own(wide_second),
+        unstack_columns(got[rows:], ranks) * scale_second,
+        own(wide_mean),
+        own(wide_square),
+        count,
     )
     factor_time, mean_time, square_time = adam(
         factor_time, time_sum[:n_time] * scale_time, mean_time, square_time, count

time: 157 us -> 140 us (0.89)
  starting transfers between devices: 71.4 us -> 46.2 us
  waiting for transfers between devices: 52.6 us -> 60.4 us
  local copies, waits for them, and re-layouts: 3.15 us -> 7.25 us
  matrix products: 21.4 us -> 18 us
    ppermute x32 -> x13, starting transfers between devices: 46.1 us -> 13.9 us  [swap(): return lax.ppermute(x, axis, [(i, i ^ k) for i in range(n)])]
    all_to_all x3 -> x5, waiting for transfers between devices: 5.62 us -> 26.6 us  [the longest x3 12.4 us: exchange_ta(): return lax.all_to_all(slots, 'ta', 0, 0)]
    all_to_all x3 -> x5, starting transfers between devices: 11.2 us -> 21.8 us  [the longest x3 14.6 us: exchange_ta(): return lax.all_to_all(slots, 'ta', 0, 0)]
    ppermute x32 -> x13, waiting for transfers between devices: 28.9 us -> 20 us  [swap(): return lax.ppermute(x, axis, [(i, i ^ k) for i in range(n)])]
    all_to_all x2, waiting for transfers between devices: 18 us -> 13.9 us  [spread_second(): got = lax.all_to_all(jnp.broadcast_to(flat, (ni,) + flat.shape), 'ia', 0, 0)]
    all_to_all x2, starting transfers between devices: 14.2 us -> 10.6 us  [spread_second(): got = lax.all_to_all(jnp.broadcast_to(flat, (ni,) + flat.shape), 'ia', 0, 0)]
    dot_general x2, matrix products: 6.52 us -> 2.95 us  [parts(): lax.dot_general(scaled, slope, (((0, 1), (0, 1)), ((), ())), preferred_el...]
    unnamed x14 -> x60, local copies, waits for them, and re-layouts: 0.86 us -> 4.29 us
  transfers between devices with their start and end apart: 37 -> 20, of which waited for: 23 -> 15; matrix products, arithmetic and copies ran while one was open for 6% -> 3% of each run, Pallas kernels for 0% -> 0%
where the time goes in v3:
time: 140 us; the launch traced here: 139 us
  waiting for transfers between devices  60.4 us (43%)
  starting transfers between devices  46.2 us (33%)
  matrix products  18 us (13%)
  local copies, waits for them, and re-layouts  7.25 us (5%)
  other arithmetic  5.24 us (4%)
  between operations  1.49 us (1%)
    ppermute x13, waiting for transfers between devices, swap(): return lax.ppermute(x, axis, [(i, i ^ k) for i in range(n)])  20 us
    all_to_all x3, starting transfers between devices, exchange_ta(): return lax.all_to_all(slots, 'ta', 0, 0)  14.6 us
    ppermute x13, starting transfers between devices, swap(): return lax.ppermute(x, axis, [(i, i ^ k) for i in range(n)])  13.9 us
    all_to_all x2, waiting for transfers between devices, spread_second(): got = lax.all_to_all(jnp.broadcast_to(flat, (ni,) + flat.shape), 'ia', 0, 0)  13.9 us
    all_to_all x3, waiting for transfers between devices, exchange_ta(): return lax.all_to_all(slots, 'ta', 0, 0)  12.4 us
    dot_general x2, matrix products, parts(): lax.dot_general(scaled, b16, (((2,), (0,)), ((), ())), preferred_element_...  11.3 us
    all_to_all x2, starting transfers between devices, spread_second(): got = lax.all_to_all(jnp.broadcast_to(flat, (ni,) + flat.shape), 'ia', 0, 0)  10.6 us
    all_to_all x1, waiting for transfers between devices, body(): lax.all_to_all(jnp.concatenate([part_second.reshape(ni, ranks, nt * cols)...  10.1 us
  transfers between devices with their start and end apart: 20, of which 15 were waited for; matrix products, arithmetic and copies ran while one was open for 3% of the time, Pallas kernels for 0%

profile of v3, /device:TPU:32, one launch (start us, length us, event | category | flops | bytes accessed | tf_op | source)
XLA Modules:
  0.0 138.6 jit_solution(4529143161974553707)
XLA Ops:
  6.1 6.0 %all-to-all-start = ((f32[4,64,128]{2,1,0:T(8,128)}), f32[4,64,128]{2,1,0:T(8,128)S(1)}, u32[]{:S(2)}, u32[]{:S(2)}) async-start(f32[4,64,128]{2,1,0:T(8,128)} %broadcast_in_dim.12), calls=%async_computation | async-start | bytes 262144 | tf_op jit(solution)/shard_map/all_to_all | solution.py:35
  12.8 4.5 %all-to-all-done = f32[4,64,128]{2,1,0:T(8,128)S(1)} async-done(((f32[4,64,128]{2,1,0:T(8,128)}), f32[4,64,128]{2,1,0:T(8,128)S(1)}, u32[]{:S(2)}, u32[]{:S(2)}) %all-to-all-start) | async-done | bytes 131104 | tf_op jit(solution)/shard_map/all_to_all | solution.py:35
  18.5 4.7 %collective-permute-start.1 = (bf16[128,128]{1,0:T(8,128)(2,1)S(1)}, bf16[128,128]{1,0:T(8,128)(2,1)S(1)}, u32[]{:S(2)}, u32[]{:S(2)}) collective-permute-start(bf16[128,128]{1,0:T(8,128)(2,1)S(1)} %pad_maximum_fusion.6), channel_id=1, source_target_pairs={{0,8},{4,12},{8,0},{12,4},{1,9},{5,13},{9,1},{13,5},{2,10},{6,14},... | collective-permute-start | bytes 98312 | tf_op jit(solution)/shard_map/ppermute | solution.py:27
  23.9 7.0 %all-to-all-start.1 = ((bf16[16,16,512]{2,1,0:T(8,128)(2,1)}), bf16[16,16,512]{2,1,0:T(8,128)(2,1)S(1)}, u32[]{:S(2)}, u32[]{:S(2)}) async-start(bf16[16,16,512]{2,1,0:T(8,128)(2,1)} %broadcast_in_dim.13), calls=%async_computation.1 | async-start | bytes 524288 | tf_op jit(solution)/shard_map/all_to_all | solution.py:113
  31.0 8.7 %all-to-all-done.1 = bf16[16,16,512]{2,1,0:T(8,128)(2,1)S(1)} async-done(((bf16[16,16,512]{2,1,0:T(8,128)(2,1)}), bf16[16,16,512]{2,1,0:T(8,128)(2,1)S(1)}, u32[]{:S(2)}, u32[]{:S(2)}) %all-to-all-start.1) | async-done | bytes 262176 | tf_op jit(solution)/shard_map/all_to_all | solution.py:113
  39.7 5.6 %fusion.1 = bf16[12,256,1024]{2,1,0:T(8,128)(2,1)S(1)} fusion(bf16[12,256,1024]{2,1,0:T(8,128)(2,1)} %param.10, f32[12,128]{1,0:T(8,128)S(1)} %convert_convert_fusion.1, f32[256,128]{1,0:T(8,128)S(1)} %maximum_convert_fusion, bf16[128,512]{1,0:T(8,128)(2,1)S(1)} %get-tuple-element.41, bf16[128,512]{1,0:T(8,128)(2,1)S(1)} %get-tuple-element.40), kind=kOutput, calls=%fused_computation.3 | convolution fusion | flops 825491456 | bytes 12982272 | tf_op jit(solution)/shard_map/dot_general | solution.py:134
  45.3 1.9 %convolution_bitcast_fusion.1 = f32[128,1024]{1,0:T(8,128)} fusion(bf16[12,256,1024]{2,1,0:T(8,128)(2,1)S(1)} %fusion.1, f32[12,128]{1,0:T(8,128)S(1)} %convert_convert_fusion.1, f32[256,128]{1,0:T(8,128)S(1)} %maximum_convert_fusion), kind=kOutput, calls=%fused_computation.13 | convolution fusion | flops 806092800 | bytes 6952960 | tf_op jit(solution)/shard_map/dot_general | solution.py:138
  47.2 1.9 %multiply_reduce_fusion.3 = (f32[256,128]{1,0:T(8,128)S(1)}, f32[12,128]{1,0:T(8,128)S(1)}) fusion(f32[12,128]{1,0:T(8,128)S(1)} %convert_convert_fusion.1, f32[256,128]{1,0:T(8,128)S(1)} %maximum_convert_fusion, bf16[12,256,1024]{2,1,0:T(8,128)(2,1)S(1)} %fusion.1, bf16[128,512]{1,0:T(8,128)(2,1)S(1)} %get-tuple-element.41, ...), kind=kOutput, calls=%fused_computation.10 | convolution fusion | flops 807369216 | bytes 6828032 | tf_op jit(solution)/shard_map/dot_general | solution.py:142
  49.3 3.6 %all-to-all-start.2 = ((f32[16,8,1024]{2,1,0:T(8,128)}), f32[16,8,1024]{2,1,0:T(8,128)S(1)}, u32[]{:S(2)}, u32[]{:S(2)}) async-start(f32[16,8,1024]{2,1,0:T(8,128)} %bitcast.7), calls=%async_computation.2 | async-start | bytes 1048576 | tf_op jit(solution)/shard_map/all_to_all | solution.py:193
  53.0 1.4 %collective-permute-start.3 = (f32[80,128]{1,0:T(8,128)S(1)}, f32[80,128]{1,0:T(8,128)S(1)}, u32[]{:S(2)}, u32[]{:S(2)}) collective-permute-start(f32[80,128]{1,0:T(8,128)S(1)} %pad_maximum_fusion.5), channel_id=1, source_target_pairs={{0,8},{4,12},{8,0},{12,4},{1,9},{5,13},{9,1},{13,5},{2,10},{6,14},... | collective-permute-start | bytes 122888 | tf_op jit(solution)/shard_map/ppermute | solution.py:27
  54.4 6.8 %collective-permute-done.3 = f32[80,128]{1,0:T(8,128)S(1)} collective-permute-done((f32[80,128]{1,0:T(8,128)S(1)}, f32[80,128]{1,0:T(8,128)S(1)}, u32[]{:S(2)}, u32[]{:S(2)}) %collective-permute-start.3) | collective-permute-done | bytes 40992 | tf_op jit(solution)/shard_map/ppermute | solution.py:27
  61.3 4.1 %all-to-all-done.2 = f32[16,8,1024]{2,1,0:T(8,128)S(1)} async-done(((f32[16,8,1024]{2,1,0:T(8,128)}), f32[16,8,1024]{2,1,0:T(8,128)S(1)}, u32[]{:S(2)}, u32[]{:S(2)}) %all-to-all-start.2) | async-done | bytes 524320 | tf_op jit(solution)/shard_map/all_to_all | solution.py:193
  66.2 4.4 %all-to-all-start.3 = ((f32[4,80,128]{2,1,0:T(8,128)}), f32[4,80,128]{2,1,0:T(8,128)S(1)}, u32[]{:S(2)}, u32[]{:S(2)}) async-start(f32[4,80,128]{2,1,0:T(8,128)} %pad_maximum_fusion.1), calls=%async_computation.3 | async-start | bytes 327680 | tf_op jit(solution)/shard_map/all_to_all | solution.py:35
  70.5 5.4 %all-to-all-done.3 = f32[4,80,128]{2,1,0:T(8,128)S(1)} async-done(((f32[4,80,128]{2,1,0:T(8,128)}), f32[4,80,128]{2,1,0:T(8,128)S(1)}, u32[]{:S(2)}, u32[]{:S(2)}) %all-to-all-start.3) | async-done | bytes 163872 | tf_op jit(solution)/shard_map/all_to_all | solution.py:35
  76.0 1.3 collective-permute-start.4
  77.4 6.2 %collective-permute-done.4 = bf16[1,16,128]{2,1,0:T(8,128)(2,1)S(1)} collective-permute-done((bf16[1,16,128]{2,1,0:T(8,128)(2,1)S(1)}, bf16[1,16,128]{2,1,0:T(8,128)(2,1)S(1)}, u32[]{:S(2)}, u32[]{:S(2)}) %collective-permute-start.4) | collective-permute-done | bytes 4128 | tf_op jit(solution)/shard_map/ppermute | solution.py:27
  84.5 3.6 %all-to-all-start.4 = ((bf16[16,24,512]{2,1,0:T(8,128)(2,1)}), bf16[16,24,512]{2,1,0:T(8,128)(2,1)S(1)}, u32[]{:S(2)}, u32[]{:S(2)}) async-start(bf16[16,24,512]{2,1,0:T(8,128)(2,1)} %broadcast_in_dim.30), calls=%async_computation.4 | async-start | bytes 786432 | tf_op jit(solution)/shard_map/all_to_all | solution.py:113
  88.1 1.1 collective-permute-start.8
  89.8 1.9 %collective-permute-start.6 = (bf16[4,16,128]{2,1,0:T(8,128)(2,1)S(1)}, bf16[4,16,128]{2,1,0:T(8,128)(2,1)S(1)}, u32[]{:S(2)}, u32[]{:S(2)}) collective-permute-start(bf16[4,16,128]{2,1,0:T(8,128)(2,1)S(1)} %bitcast.92), channel_id=1, source_target_pairs={{0,3},{1,2},{2,1},{3,0},{4,7},{5,6},{6,5},{7,4},{8,11},{9,10},{10,... | collective-permute-start | bytes 49160 | tf_op jit(solution)/shard_map/ppermute | solution.py:27
  92.0 1.9 %collective-permute-done.7 = bf16[4,16,128]{2,1,0:T(8,128)(2,1)S(1)} collective-permute-done((bf16[4,16,128]{2,1,0:T(8,128)(2,1)S(1)}, bf16[4,16,128]{2,1,0:T(8,128)(2,1)S(1)}, u32[]{:S(2)}, u32[]{:S(2)}) %collective-permute-start.7) | collective-permute-done | bytes 16416 | tf_op jit(solution)/shard_map/ppermute | solution.py:27
  93.9 5.2 %all-to-all-done.4 = bf16[16,24,512]{2,1,0:T(8,128)(2,1)S(1)} async-done(((bf16[16,24,512]{2,1,0:T(8,128)(2,1)}), bf16[16,24,512]{2,1,0:T(8,128)(2,1)S(1)}, u32[]{:S(2)}, u32[]{:S(2)}) %all-to-all-start.4) | async-done | bytes 393248 | tf_op jit(solution)/shard_map/all_to_all | solution.py:113
  99.3 5.6 %fusion.3 = bf16[12,256,1024]{2,1,0:T(8,128)(2,1)S(1)} fusion(bf16[12,256,1024]{2,1,0:T(8,128)(2,1)} %param.10, f32[12,128]{1,0:T(8,128)S(1)} %get-tuple-element.32, f32[256,128]{1,0:T(8,128)S(1)} %bitcast.60, bf16[128,512]{1,0:T(8,128)(2,1)S(1)} %get-tuple-element.39, bf16[128,512]{1,0:T(8,128)(2,1)S(1)} %get-tuple-element.38), kind=kOutput, calls=%fused_computation.5 | convolution fusion | flops 825491456 | bytes 12982272 | tf_op jit(solution)/shard_map/dot_general | solution.py:134
  106.0 1.9 %multiply_reduce_fusion.1 = (f32[256,128]{1,0:T(8,128)S(1)}, f32[12,128]{1,0:T(8,128)S(1)}) fusion(f32[12,128]{1,0:T(8,128)S(1)} %get-tuple-element.32, f32[256,128]{1,0:T(8,128)S(1)} %bitcast.62, bf16[12,256,1024]{2,1,0:T(8,128)(2,1)S(1)} %fusion.3, bf16[128,512]{1,0:T(8,128)(2,1)S(1)} %get-tuple-element.39, bf16[128,512]{1,0:T(8,128)(2,1)S(1)} %get-tuple-element.38), kind=kOutput, calls=%fused_computation.7 | convolution fusion | flops 807369216 | bytes 6828032 | tf_op jit(solution)/shard_map/dot_general | solution.py:142
  108.8 3.6 %all-to-all-start.5 = ((f32[16,8,1280]{2,1,0:T(8,128)}), f32[16,8,1280]{2,1,0:T(8,128)S(1)}, u32[]{:S(2)}, u32[]{:S(2)}) async-start(f32[16,8,1280]{2,1,0:T(8,128)} %pad_maximum_fusion), calls=%async_computation.5 | async-start | bytes 1310720 | tf_op jit(solution)/shard_map/all_to_all | solution.py:220
  112.6 1.2 collective-permute-done.9
  113.8 1.3 collective-permute-start.10
  115.2 10.1 %all-to-all-done.5 = f32[16,8,1280]{2,1,0:T(8,128)S(1)} async-done(((f32[16,8,1280]{2,1,0:T(8,128)}), f32[16,8,1280]{2,1,0:T(8,128)S(1)}, u32[]{:S(2)}, u32[]{:S(2)}) %all-to-all-start.5) | async-done | bytes 655392 | tf_op jit(solution)/shard_map/all_to_all | solution.py:220
  125.5 1.1 collective-permute-done.11
  126.6 1.2 collective-permute-start.12
  128.5 4.2 %all-to-all-start.6 = ((f32[4,32,128]{2,1,0:T(8,128)}), f32[4,32,128]{2,1,0:T(8,128)S(1)}, u32[]{:S(2)}, u32[]{:S(2)}) async-start(f32[4,32,128]{2,1,0:T(8,128)} %pad_maximum_fusion.4), calls=%async_computation.6 | async-start | bytes 131072 | tf_op jit(solution)/shard_map/all_to_all | solution.py:35
  132.7 1.5 %collective-permute-done.12 = f32[16,128]{1,0:T(8,128)S(1)} collective-permute-done((f32[16,128]{1,0:T(8,128)S(1)}, f32[16,128]{1,0:T(8,128)S(1)}, u32[]{:S(2)}, u32[]{:S(2)}) %collective-permute-start.12) | collective-permute-done | bytes 8224 | tf_op jit(solution)/shard_map/ppermute | solution.py:27
  134.8 2.5 %all-to-all-done.6 = f32[4,32,128]{2,1,0:T(8,128)S(1)} async-done(((f32[4,32,128]{2,1,0:T(8,128)}), f32[4,32,128]{2,1,0:T(8,128)S(1)}, u32[]{:S(2)}, u32[]{:S(2)}) %all-to-all-start.6) | async-done | bytes 65568 | tf_op jit(solution)/shard_map/all_to_all | solution.py:35
  (143 shorter events, 15.7 us)
Async XLA Ops:
  6.1 11.2 %all-to-all-start = ((f32[4,64,128]{2,1,0:T(8,128)}), f32[4,64,128]{2,1,0:T(8,128)S(1)}, u32[]{:S(2)}, u32[]{:S(2)}) async-start(f32[4,64,128]{2,1,0:T(8,128)} %broadcast_in_dim.12), calls=%async_computation | async-start | bytes 262144 | tf_op jit(solution)/shard_map/all_to_all | solution.py:35
  17.3 1.2 collective-permute-start
  18.5 12.4 %collective-permute-start.1 = (bf16[128,128]{1,0:T(8,128)(2,1)S(1)}, bf16[128,128]{1,0:T(8,128)(2,1)S(1)}, u32[]{:S(2)}, u32[]{:S(2)}) collective-permute-start(bf16[128,128]{1,0:T(8,128)(2,1)S(1)} %pad_maximum_fusion.6), channel_id=1, source_target_pairs={{0,8},{4,12},{8,0},{12,4},{1,9},{5,13},{9,1},{13,5},{2,10},{6,14},... | collective-permute-start | bytes 98312 | tf_op jit(solution)/shard_map/ppermute | solution.py:27
  23.9 15.8 %all-to-all-start.1 = ((bf16[16,16,512]{2,1,0:T(8,128)(2,1)}), bf16[16,16,512]{2,1,0:T(8,128)(2,1)S(1)}, u32[]{:S(2)}, u32[]{:S(2)}) async-start(bf16[16,16,512]{2,1,0:T(8,128)(2,1)} %broadcast_in_dim.13), calls=%async_computation.1 | async-start | bytes 524288 | tf_op jit(solution)/shard_map/all_to_all | solution.py:113
  47.2 28.7 %copy-start.2 = (f32[16,128]{1,0:T(8,128)S(1)}, f32[16,128]{1,0:T(8,128)}, u32[]{:S(2)}) copy-start(f32[16,128]{1,0:T(8,128)} %param.11) | copy-start | bytes 24580
  47.2 28.8 %copy-start.4 = (f32[16,128]{1,0:T(8,128)S(1)}, f32[16,128]{1,0:T(8,128)}, u32[]{:S(2)}) copy-start(f32[16,128]{1,0:T(8,128)} %param.15) | copy-start | bytes 24580
  47.2 28.8 %copy-start.5 = (f32[16,128]{1,0:T(8,128)S(1)}, f32[16,128]{1,0:T(8,128)}, u32[]{:S(2)}) copy-start(f32[16,128]{1,0:T(8,128)} %param.14) | copy-start | bytes 24580
  49.1 50.1 %copy-start = (f32[12,128]{1,0:T(8,128)S(1)}, f32[12,128]{1,0:T(8,128)}, u32[]{:S(2)}) copy-start(f32[12,128]{1,0:T(8,128)} %param.19) | copy-start | bytes 18436
  49.2 50.0 %copy-start.1 = (f32[12,128]{1,0:T(8,128)S(1)}, f32[12,128]{1,0:T(8,128)}, u32[]{:S(2)}) copy-start(f32[12,128]{1,0:T(8,128)} %param.18) | copy-start | bytes 18436
  49.2 50.0 %copy-start.3 = (f32[12,128]{1,0:T(8,128)S(1)}, f32[12,128]{1,0:T(8,128)}, u32[]{:S(2)}) copy-start(f32[12,128]{1,0:T(8,128)} %param.13) | copy-start | bytes 18436
  49.2 3.7 %collective-permute-start.2 = (f32[144,128]{1,0:T(8,128)S(1)}, f32[144,128]{1,0:T(8,128)S(1)}, u32[]{:S(2)}, u32[]{:S(2)}) collective-permute-start(f32[144,128]{1,0:T(8,128)S(1)} %pad_maximum_fusion.2), channel_id=1, source_target_pairs={{0,4},{4,0},{8,12},{12,8},{1,5},{5,1},{9,13},{13,9},{2,6},{6,2},{1... | collective-permute-start | bytes 221192 | tf_op jit(solution)/shard_map/ppermute | solution.py:27
  49.3 16.0 %all-to-all-start.2 = ((f32[16,8,1024]{2,1,0:T(8,128)}), f32[16,8,1024]{2,1,0:T(8,128)S(1)}, u32[]{:S(2)}, u32[]{:S(2)}) async-start(f32[16,8,1024]{2,1,0:T(8,128)} %bitcast.7), calls=%async_computation.2 | async-start | bytes 1048576 | tf_op jit(solution)/shard_map/all_to_all | solution.py:193
  53.0 8.2 %collective-permute-start.3 = (f32[80,128]{1,0:T(8,128)S(1)}, f32[80,128]{1,0:T(8,128)S(1)}, u32[]{:S(2)}, u32[]{:S(2)}) collective-permute-start(f32[80,128]{1,0:T(8,128)S(1)} %pad_maximum_fusion.5), channel_id=1, source_target_pairs={{0,8},{4,12},{8,0},{12,4},{1,9},{5,13},{9,1},{13,5},{2,10},{6,14},... | collective-permute-start | bytes 122888 | tf_op jit(solution)/shard_map/ppermute | solution.py:27
  66.2 9.8 %all-to-all-start.3 = ((f32[4,80,128]{2,1,0:T(8,128)}), f32[4,80,128]{2,1,0:T(8,128)S(1)}, u32[]{:S(2)}, u32[]{:S(2)}) async-start(f32[4,80,128]{2,1,0:T(8,128)} %pad_maximum_fusion.1), calls=%async_computation.3 | async-start | bytes 327680 | tf_op jit(solution)/shard_map/all_to_all | solution.py:35
  76.0 7.6 %collective-permute-start.4 = (bf16[1,16,128]{2,1,0:T(8,128)(2,1)S(1)}, bf16[1,16,128]{2,1,0:T(8,128)(2,1)S(1)}, u32[]{:S(2)}, u32[]{:S(2)}) collective-permute-start(bf16[1,16,128]{2,1,0:T(8,128)(2,1)S(1)} %get-tuple-element.30), channel_id=1, source_target_pairs={{0,8},{4,12},{8,0},{12,4},{1,9},{5,13},{9,1},{13,5},{2,10},{6,14},... | collective-permute-start | bytes 12296 | tf_op jit(solution)/shard_map/ppermute | solution.py:27
  83.6 4.4 %collective-permute-start.5 = (bf16[2,16,128]{2,1,0:T(8,128)(2,1)S(1)}, bf16[2,16,128]{2,1,0:T(8,128)(2,1)S(1)}, u32[]{:S(2)}, u32[]{:S(2)}) collective-permute-start(bf16[2,16,128]{2,1,0:T(8,128)(2,1)S(1)} %pad_maximum_fusion.10), channel_id=1, source_target_pairs={{0,4},{4,0},{8,12},{12,8},{1,5},{5,1},{9,13},{13,9},{2,6},{6,2},{1... | collective-permute-start | bytes 24584 | tf_op jit(solution)/shard_map/ppermute | solution.py:27
  84.5 14.6 %all-to-all-start.4 = ((bf16[16,24,512]{2,1,0:T(8,128)(2,1)}), bf16[16,24,512]{2,1,0:T(8,128)(2,1)S(1)}, u32[]{:S(2)}, u32[]{:S(2)}) async-start(bf16[16,24,512]{2,1,0:T(8,128)(2,1)} %broadcast_in_dim.30), calls=%async_computation.4 | async-start | bytes 786432 | tf_op jit(solution)/shard_map/all_to_all | solution.py:113
  88.1 3.8 %collective-permute-start.8 = (bf16[4,16,128]{2,1,0:T(8,128)(2,1)S(1)}, bf16[4,16,128]{2,1,0:T(8,128)(2,1)S(1)}, u32[]{:S(2)}, u32[]{:S(2)}) collective-permute-start(bf16[4,16,128]{2,1,0:T(8,128)(2,1)S(1)} %bitcast.90), channel_id=1, source_target_pairs={{0,1},{1,0},{2,3},{3,2},{4,5},{5,4},{6,7},{7,6},{8,9},{9,8},{10,11... | collective-permute-start | bytes 49160 | tf_op jit(solution)/shard_map/ppermute | solution.py:27
  89.2 4.6 %collective-permute-start.7 = (bf16[4,16,128]{2,1,0:T(8,128)(2,1)S(1)}, bf16[4,16,128]{2,1,0:T(8,128)(2,1)S(1)}, u32[]{:S(2)}, u32[]{:S(2)}) collective-permute-start(bf16[4,16,128]{2,1,0:T(8,128)(2,1)S(1)} %bitcast.91), channel_id=1, source_target_pairs={{0,2},{1,3},{2,0},{3,1},{4,6},{5,7},{6,4},{7,5},{8,10},{9,11},{10,... | collective-permute-start | bytes 49160 | tf_op jit(solution)/shard_map/ppermute | solution.py:27
  89.8 4.1 %collective-permute-start.6 = (bf16[4,16,128]{2,1,0:T(8,128)(2,1)S(1)}, bf16[4,16,128]{2,1,0:T(8,128)(2,1)S(1)}, u32[]{:S(2)}, u32[]{:S(2)}) collective-permute-start(bf16[4,16,128]{2,1,0:T(8,128)(2,1)S(1)} %bitcast.92), channel_id=1, source_target_pairs={{0,3},{1,2},{2,1},{3,0},{4,7},{5,6},{6,5},{7,4},{8,11},{9,10},{10,... | collective-permute-start | bytes 49160 | tf_op jit(solution)/shard_map/ppermute | solution.py:27
  108.8 16.4 %all-to-all-start.5 = ((f32[16,8,1280]{2,1,0:T(8,128)}), f32[16,8,1280]{2,1,0:T(8,128)S(1)}, u32[]{:S(2)}, u32[]{:S(2)}) async-start(f32[16,8,1280]{2,1,0:T(8,128)} %pad_maximum_fusion), calls=%async_computation.5 | async-start | bytes 1310720 | tf_op jit(solution)/shard_map/all_to_all | solution.py:220
  112.5 1.3 collective-permute-start.9
  113.8 11.6 %collective-permute-start.10 = (f32[64,128]{1,0:T(8,128)S(1)}, f32[64,128]{1,0:T(8,128)S(1)}, u32[]{:S(2)}, u32[]{:S(2)}) collective-permute-start(f32[64,128]{1,0:T(8,128)S(1)} %slice_select_fusion), channel_id=1, source_target_pairs={{0,8},{4,12},{8,0},{12,4},{1,9},{5,13},{9,1},{13,5},{2,10},{6,14},... | collective-permute-start | bytes 98312 | tf_op jit(solution)/shard_map/ppermute | solution.py:27
  125.4 1.3 collective-permute-start.11
  126.6 7.6 %collective-permute-start.12 = (f32[16,128]{1,0:T(8,128)S(1)}, f32[16,128]{1,0:T(8,128)S(1)}, u32[]{:S(2)}, u32[]{:S(2)}) collective-permute-start(f32[16,128]{1,0:T(8,128)S(1)} %fusion.19), channel_id=1, source_target_pairs={{0,8},{4,12},{8,0},{12,4},{1,9},{5,13},{9,1},{13,5},{2,10},{6,14},... | collective-permute-start | bytes 24584 | tf_op jit(solution)/shard_map/ppermute | solution.py:27
  128.5 8.9 %all-to-all-start.6 = ((f32[4,32,128]{2,1,0:T(8,128)}), f32[4,32,128]{2,1,0:T(8,128)S(1)}, u32[]{:S(2)}, u32[]{:S(2)}) async-start(f32[4,32,128]{2,1,0:T(8,128)} %pad_maximum_fusion.4), calls=%async_computation.6 | async-start | bytes 131072 | tf_op jit(solution)/shard_map/all_to_all | solution.py:35

commit v4 on v2

v4 whole, which is shorter than its diff:
```python
import jax
import jax.numpy as jnp
from jax import lax
from jax.experimental import pallas as pl
from jax.experimental.pallas import tpu as pltpu
from jax.sharding import PartitionSpec as P

ADAM_STEP = 20


beta_one = 0.9
beta_two = 0.99
step_rate = 0.02
tiny_eps = 1e-08


def adam(value, grad, mean, square, count):
    drift = beta_one * mean + (1.0 - beta_one) * grad
    spread = beta_two * square + (1.0 - beta_two) * grad * grad
    fixed_one = 1.0 - beta_one**count
    fixed_two = 1.0 - beta_two**count
    value = value - step_rate * (drift / fixed_one) / (jnp.sqrt(spread / fixed_two) + tiny_eps)
    return (value, drift, spread)


def swap(x, axis, k):
    n = lax.axis_size(axis)
    return lax.ppermute(x, axis, [(i, i ^ k) for i in range(n)])


def pick(flag, x, y):
    return jnp.where(flag, y, x), jnp.where(flag, x, y)


def gather_ta(x):
    ta = lax.axis_index("ta")
    p = [x] + [swap(x, "ta", k) for k in (1, 2, 3)]
    odd, high = (ta & 1) == 1, (ta & 2) == 2
    q0, q1 = pick(odd, p[0], p[1])
    q2, q3 = pick(odd, p[2], p[3])
    q0, q2 = pick(high, q0, q2)
    q1, q3 = pick(high, q1, q3)
    return [q0, q1, q2, q3]


def stack_columns(x):
    return jnp.concatenate([x[:, n * 128 : (n + 1) * 128] for n in range(x.shape[1] // 128)], axis=0)


def unstack_columns(x, ranks):
    return jnp.concatenate([x[n * ranks : (n + 1) * ranks] for n in range(x.shape[0] // ranks)], axis=1)


def pack_kernel(f0, f1, f2, s0, s1, s2, out, state):
    rows = f0.shape[0]
    ranks = s0.shape[0]
    for p in range(out.shape[0]):
        for n, x in enumerate((s0, s1, s2)):
            for h in (0, 1):
                at = (2 * n + h) * ranks
                out[p, at : at + ranks, :] = x[:, h * 128 : (h + 1) * 128]
        out[p, 6 * ranks :, :] = f0[...]
    for n, x in enumerate((f0, f1, f2)):
        state[n * rows : (n + 1) * rows, :] = x[...]


def pack(copies, firsts, seconds):
    rows, rank = firsts[0].shape
    slots = (copies, rows + 6 * seconds[0].shape[0], rank)
    return pl.pallas_call(
        pack_kernel,
        out_shape=[
            jax.ShapeDtypeStruct(slots, jnp.float32),
            jax.ShapeDtypeStruct((3 * rows, rank), jnp.float32),
        ],
        in_specs=[pl.BlockSpec(memory_space=pltpu.VMEM)] * 6,
        out_specs=[pl.BlockSpec(memory_space=pltpu.VMEM)] * 2,
    )(*firsts, *seconds)


def join_cores(x):
    low, high = pick(lax.axis_index("co") == 1, x, swap(x, "co", 1))
    return jnp.stack([low, high], axis=1)


def gather_first(pair):
    rank = pair.shape[1]
    x = join_cores(pair.reshape(2, -1, rank))
    x = x.reshape((-1,) + x.shape[2:])
    return jnp.stack(gather_ta(x), axis=1).reshape(-1, rank)


def core_half(part, extra):
    one = lax.axis_index("co") == 1
    quarter = part.shape[0] // 4
    q = [part[n * quarter : (n + 1) * quarter] for n in range(4)]
    keep0, send0 = pick(one, q[0], q[1])
    keep1, send1 = pick(one, q[2], q[3])
    keep = jnp.concatenate([keep0, keep1], axis=0)
    got = swap(jnp.concatenate([send0, send1] + extra, axis=0), "co", 1)
    half = keep.shape[0]
    return keep + got[:half], [extra[0] + got[half:]] if extra else []


def bf16_pair(x):
    top = lax.reduce_precision(x, 8, 7)
    return [top.astype(jnp.bfloat16), (x - top).astype(jnp.bfloat16)]


def fold(x, rows):
    return jnp.concatenate([x[n * rows : (n + 1) * rows] for n in range(x.shape[0] // rows)], axis=1)


def time_of(got, rank):
    r = got.shape[1] // 2
    line = jnp.sum(got[:, :r].astype(jnp.float32) + got[:, r:].astype(jnp.float32), axis=0)
    return jnp.concatenate(
        [line[:, n * rank : (n + 1) * rank] for n in range(line.shape[1] // rank)], axis=0
    )


def spread_slots(stacked, extra):
    ni = lax.axis_size("ia")
    wide = stacked.astype(jnp.bfloat16)
    half = wide.shape[0] // 2
    ranks = half // 4
    flat = jnp.concatenate(
        [unstack_columns(wide[:half], ranks), unstack_columns(wide[half:], ranks)] + extra, axis=0
    )
    return jnp.broadcast_to(flat, (ni,) + flat.shape)


def spread_second(slots, ranks):
    ni, _, width = slots.shape
    got = lax.all_to_all(slots, "ia", 0, 0)
    b16 = jnp.concatenate(
        [
            got[:, :ranks].reshape(ni * ranks, width),
            got[:, ranks : 2 * ranks].reshape(ni * ranks, width),
        ],
        axis=1,
    )
    return b16, got[:, 2 * ranks :]


def second_slots(part, ni, extra):
    ranks = part.shape[0] // ni
    half = part.shape[1] // 2
    cut = part.astype(jnp.bfloat16).reshape(ni, ranks, 2, half)
    slots = [cut[:, :, 0], cut[:, :, 1]]
    slots += [jnp.broadcast_to(x, (ni,) + x.shape) for x in extra]
    return jnp.concatenate(slots, axis=1)


def sum_second(slots, ranks):
    got = lax.all_to_all(slots, "ia", 0, 0)
    total = jnp.sum(got[:, : 2 * ranks].astype(jnp.float32), axis=0)
    return jnp.concatenate([total[:ranks], total[ranks:]], axis=1), got[:, 2 * ranks :]


def make_slope(readings, a16, b16, c16):
    af = a16.astype(jnp.float32)
    cf = c16.astype(jnp.float32)
    scaled = (af[None, :, :] * cf[:, None, :]).astype(jnp.bfloat16)
    model = lax.dot_general(
        scaled, b16, (((2,), (0,)), ((), ())), preferred_element_type=jnp.float32
    )
    slope = ((model - readings.astype(jnp.float32)) / (model * model)).astype(jnp.bfloat16)
    part_second = lax.dot_general(
        scaled, slope, (((0, 1), (0, 1)), ((), ())), preferred_element_type=jnp.float32
    )
    return slope, part_second


def make_cross(slope, a16, b16, c16):
    af = a16.astype(jnp.float32)
    cf = c16.astype(jnp.float32)
    cross = lax.dot_general(
        slope, b16, (((2,), (1,)), ((), ())), preferred_element_type=jnp.float32
    )
    part_first = jnp.sum(cross * cf[:, None, :], axis=0)
    part_time = jnp.sum(cross * af[None, :, :], axis=1)
    return part_first, jnp.pad(part_time, ((0, 16 - part_time.shape[0]), (0, 0)))


def body(
    readings,
    factor_first,
    factor_second,
    factor_time,
    mean_first,
    square_first,
    mean_second,
    square_second,
    mean_time,
    square_time,
):
    ni, nt = lax.axis_size("ia"), lax.axis_size("ta")
    nj = lax.axis_size("zh") * lax.axis_size("co")
    whole_i = readings.shape[1] * ni
    whole_j = readings.shape[2] * nj
    whole_k = readings.shape[0] * nt
    n_time, rank = factor_time.shape
    scale_first = rank / (whole_j * whole_k)
    scale_second = rank / (whole_i * whole_k)
    scale_time = rank / (whole_i * whole_j)
    rows = factor_first.shape[0]
    ranks, cols = factor_second.shape
    flat = 2 * ranks
    zh, ta = lax.axis_index("zh"), lax.axis_index("ta")
    high = zh == 1

    slots, own_first = pack(
        nt,
        (factor_first, mean_first, square_first),
        (factor_second, mean_second, square_second),
    )
    got = lax.all_to_all(slots, "ta", 0, 0)
    wide_second, wide_mean, wide_square = [
        got[:, n * flat : (n + 1) * flat].reshape(nt * flat, rank) for n in (0, 1, 2)
    ]
    a16 = got[:, 3 * flat :].astype(jnp.bfloat16).reshape(nt * rows, rank)

    pad = [a16[n * ranks : (n + 1) * ranks] for n in range(4)]
    slots = spread_slots(wide_second, [jnp.concatenate(pad, axis=1)])
    slots, a16, own_first = lax.optimization_barrier((slots, a16, own_first))
    b16, _ = spread_second(slots, ranks)
    a16 = join_cores(a16[None]).reshape(-1, rank)
    low, up = pick(high, a16, swap(a16, "zh", 1))
    a16 = jnp.concatenate([low, up], axis=0)
    low, up = pick(high, own_first, swap(own_first, "zh", 1))
    pair_first, pair_mean, pair_square = [
        jnp.concatenate([low[n : n + rows], up[n : n + rows]], axis=0)
        for n in (0, rows, 2 * rows)
    ]
    c16 = factor_time.astype(jnp.bfloat16)
    slope, part_second = make_slope(readings, a16, b16, c16)
    slots = second_slots(part_second, ni, [jnp.concatenate(pad, axis=1)])
    slope, slots = lax.optimization_barrier((slope, slots))
    second, _ = sum_second(slots, ranks)
    part_first, part_time = make_cross(slope, a16, b16, c16)
    part, [time_ja] = core_half(part_first, [part_time])
    both = jnp.concatenate([part, time_ja], axis=0)
    both = both + swap(both, "zh", 1)
    part, time_ja = both[: 8 * rows], both[8 * rows :]
    part = part.reshape(2, nt, rows, rank).transpose(1, 0, 2, 3).reshape(nt, 2 * rows, rank)
    second = stack_columns(second)
    slots = jnp.concatenate(
        [part, jnp.broadcast_to(second, (nt,) + second.shape)], axis=1
    )
    got = jnp.sum(lax.all_to_all(slots, "ta", 0, 0), axis=0)
    count = ADAM_STEP + 1
    wide_second, wide_mean, wide_square = adam(
        wide_second, got[2 * rows :] * scale_second, wide_mean, wide_square, count
    )
    pair_first, pair_mean, pair_square = adam(
        pair_first, got[: 2 * rows] * scale_first, pair_mean, pair_square, count
    )

    slots = spread_slots(wide_second, bf16_pair(fold(time_ja, ranks // 2)))
    b16, came = spread_second(slots, ranks)
    a16 = gather_first(pair_first.astype(jnp.bfloat16))
    time_sum = time_of(came, rank)[:n_time]
    factor_time, mean_time, square_time = adam(
        factor_time, time_sum * scale_time, mean_time, square_time, count
    )
    c16 = factor_time.astype(jnp.bfloat16)
    slope, part_second = make_slope(readings, a16, b16, c16)
    part_first, part_time = make_cross(slope, a16, b16, c16)
    second, came = sum_second(
        second_slots(part_second, ni, bf16_pair(fold(part_time, ranks // 2))), ranks
    )
    part, _ = core_half(part_first, [])
    keep, send = pick(high, part[: 4 * rows], part[4 * rows :])
    part = keep + swap(send, "zh", 1)
    time_sum = time_of(came, rank)
    for axis in ("co", "zh"):
        time_sum = time_sum + swap(time_sum, axis, 1)
    slots = jnp.concatenate(
        [part.reshape(nt, rows, rank), stack_columns(second).reshape(nt, flat, rank)], axis=1
    )
    got = jnp.sum(lax.all_to_all(slots, "ta", 0, 0), axis=0)
    count = ADAM_STEP + 2
    first = lambda x: jnp.where(high, x[rows:], x[:rows])
    own = lambda x: unstack_columns(lax.dynamic_slice_in_dim(x, ta * flat, flat, axis=0), ranks)
    factor_first, mean_first, square_first = adam(
        first(pair_first), got[:rows] * scale_first, first(pair_mean), first(pair_square), count
    )
    factor_second, mean_second, square_second = adam(
        own(wide_second),
        unstack_columns(got[rows:], ranks) * scale_second,
        own(wide_mean),
        own(wide_square),
        count,
    )
    factor_time, mean_time, square_time = adam(
        factor_time, time_sum[:n_time] * scale_time, mean_time, square_time, count
    )
    return (
        factor_first,
        factor_second,
        factor_time,
        mean_first,
        square_first,
        mean_second,
        square_second,
        mean_time,
        square_time,
    )


def solution(mesh):
    shape = (mesh.shape["ia"], 2, mesh.shape["ja"] // 2, mesh.shape["ta"])
    mesh = jax.sharding.Mesh(mesh.devices.reshape(shape), ("ia", "zh", "co", "ta"))
    first = P(("ia", "zh", "co", "ta"), None)
    second = P("ia", ("zh", "co", "ta"))
    time = P("ta", None)
    return jax.shard_map(
        body,
        mesh=mesh,
        in_specs=(
            P("ta", "ia", ("zh", "co")),
            first,
            second,
            time,
            first,
            first,
            second,
            second,
            time,
            time,
        ),
        out_specs=(first, second, time, first, first, second, second, time, time),
        check_vma=False,
    )
```

time: 157 us -> 128 us (0.82)
  starting transfers between devices: 71.4 us -> 53.7 us
  waiting for transfers between devices: 52.6 us -> 46 us
  matrix products: 21.4 us -> 15.5 us
    ppermute x32 -> x13, starting transfers between devices: 46.1 us -> 14.9 us  [swap(): return lax.ppermute(x, axis, [(i, i ^ k) for i in range(n)])]
    all_to_all x5 -> x7, starting transfers between devices: 25.3 us -> 38.8 us  [the longest x2 12.8 us: spread_second(): got = lax.all_to_all(slots, 'ia', 0, 0)]
    dot_general x6, matrix products: 21.4 us -> 15.5 us  [the longest x2 9.67 us: make_slope(): lax.dot_general(scaled, b16, (((2,), (0,)), ((), ())), preferred_element_...]
    all_to_all x5 -> x7, waiting for transfers between devices: 23.6 us -> 18.7 us  [the longest x2 8.4 us: body(): got = jnp.sum(lax.all_to_all(slots, 'ta', 0, 0), axis=0)]
    concatenate x13 -> x11, other arithmetic: 0.82 us -> 2.97 us  [the longest x2 1.6 us: second_slots(): return jnp.concatenate(slots, axis=1)]
    ppermute x32 -> x13, waiting for transfers between devices: 28.9 us -> 27.2 us  [swap(): return lax.ppermute(x, axis, [(i, i ^ k) for i in range(n)])]
  transfers between devices with their start and end apart: 37 -> 20, of which waited for: 23 -> 14; matrix products, arithmetic and copies ran while one was open for 6% -> 4% of each run, Pallas kernels for 0% -> 0%
where the time goes in v4:
time: 128 us; the launch traced here: 127 us
  starting transfers between devices  53.7 us (42%)
  waiting for transfers between devices  46 us (36%)
  matrix products  15.5 us (12%)
  other arithmetic  6.83 us (5%)
  local copies, waits for them, and re-layouts  1.86 us (1%)
  Pallas kernels  1.45 us (1%)
  between operations  1.32 us (1%)
    ppermute x13, waiting for transfers between devices, swap(): return lax.ppermute(x, axis, [(i, i ^ k) for i in range(n)])  27.2 us
    ppermute x13, starting transfers between devices, swap(): return lax.ppermute(x, axis, [(i, i ^ k) for i in range(n)])  14.9 us
    all_to_all x2, starting transfers between devices, spread_second(): got = lax.all_to_all(slots, 'ia', 0, 0)  12.8 us
    all_to_all x2, starting transfers between devices, sum_second(): got = lax.all_to_all(slots, 'ia', 0, 0)  11.4 us
    dot_general x2, matrix products, make_slope(): lax.dot_general(scaled, b16, (((2,), (0,)), ((), ())), preferred_element_...  9.67 us
    all_to_all x2, starting transfers between devices, body(): got = jnp.sum(lax.all_to_all(slots, 'ta', 0, 0), axis=0)  8.57 us
    all_to_all x2, waiting for transfers between devices, body(): got = jnp.sum(lax.all_to_all(slots, 'ta', 0, 0), axis=0)  8.4 us
    all_to_all x1, starting transfers between devices, body(): got = lax.all_to_all(slots, 'ta', 0, 0)  6 us
  transfers between devices with their start and end apart: 20, of which 14 were waited for; matrix products, arithmetic and copies ran while one was open for 4% of the time, Pallas kernels for 0%

profile of v4, /device:TPU:32, one launch (start us, length us, event | category | flops | bytes accessed | tf_op | source)
XLA Modules:
  0.0 126.7 jit_solution(13956448491287385411)
XLA Ops:
  0.6 1.4 %shard_map.169 = (f32[4,64,128]{2,1,0:T(8,128)}, f32[48,128]{1,0:T(8,128)}) custom-call(f32[16,128]{1,0:T(8,128)} %f0.1, f32[16,128]{1,0:T(8,128)} %f1.1, f32[16,128]{1,0:T(8,128)} %f2.1, f32[8,256]{1,0:T(8,128)} %s0.1, f32[8,256]{1,0:T(8,128)} %s1_.1, f32[8,256]{1,0:T(8,128)} %s2_.1), custom_call_target="tpu_custom_call" | custom-call | tf_op jit(solution)/shard_map/pallas_call | solution.py:70
  2.1 6.0 %all-to-all-start = ((f32[4,64,128]{2,1,0:T(8,128)}), f32[4,64,128]{2,1,0:T(8,128)S(1)}, u32[]{:S(2)}, u32[]{:S(2)}) async-start(f32[4,64,128]{2,1,0:T(8,128)} %get-tuple-element.16), calls=%async_computation | async-start | bytes 262144 | tf_op jit(solution)/shard_map/all_to_all | solution.py:218
  8.8 4.4 %all-to-all-done = f32[4,64,128]{2,1,0:T(8,128)S(1)} async-done(((f32[4,64,128]{2,1,0:T(8,128)}), f32[4,64,128]{2,1,0:T(8,128)S(1)}, u32[]{:S(2)}, u32[]{:S(2)}) %all-to-all-start) | async-done | bytes 131104 | tf_op jit(solution)/shard_map/all_to_all | solution.py:218
  14.1 7.0 %all-to-all-start.1 = ((bf16[16,24,512]{2,1,0:T(8,128)(2,1)}), bf16[16,24,512]{2,1,0:T(8,128)(2,1)S(1)}, u32[]{:S(2)}, u32[]{:S(2)}) async-start(bf16[16,24,512]{2,1,0:T(8,128)(2,1)} %broadcast_in_dim.14), calls=%async_computation.1 | async-start | bytes 786432 | tf_op jit(solution)/shard_map/all_to_all | solution.py:135
  21.2 4.7 %collective-permute-start = (f32[48,128]{1,0:T(8,128)}, f32[48,128]{1,0:T(8,128)S(1)}, u32[]{:S(2)}, u32[]{:S(2)}) collective-permute-start(f32[48,128]{1,0:T(8,128)} %get-tuple-element.18), channel_id=1, source_target_pairs={{0,8},{8,0},{1,9},{9,1},{2,10},{10,2},{3,11},{11,3},{4,12},{12,4},... | collective-permute-start | bytes 73736 | tf_op jit(solution)/shard_map/ppermute | solution.py:28
  25.9 1.4 %collective-permute-start.2 = (bf16[128,128]{1,0:T(8,128)(2,1)S(1)}, bf16[128,128]{1,0:T(8,128)(2,1)S(1)}, u32[]{:S(2)}, u32[]{:S(2)}) collective-permute-start(bf16[128,128]{1,0:T(8,128)(2,1)S(1)} %bitcast.101), channel_id=1, source_target_pairs={{0,8},{8,0},{1,9},{9,1},{2,10},{10,2},{3,11},{11,3},{4,12},{12,4},... | collective-permute-start | bytes 98312 | tf_op jit(solution)/shard_map/ppermute | solution.py:28
  27.3 1.9 %collective-permute-done = f32[48,128]{1,0:T(8,128)S(1)} collective-permute-done((f32[48,128]{1,0:T(8,128)}, f32[48,128]{1,0:T(8,128)S(1)}, u32[]{:S(2)}, u32[]{:S(2)}) %collective-permute-start) | collective-permute-done | bytes 24608 | tf_op jit(solution)/shard_map/ppermute | solution.py:28
  29.9 4.0 %collective-permute-done.2 = bf16[128,128]{1,0:T(8,128)(2,1)S(1)} collective-permute-done((bf16[128,128]{1,0:T(8,128)(2,1)S(1)}, bf16[128,128]{1,0:T(8,128)(2,1)S(1)}, u32[]{:S(2)}, u32[]{:S(2)}) %collective-permute-start.2) | collective-permute-done | bytes 32800 | tf_op jit(solution)/shard_map/ppermute | solution.py:28
  34.0 4.8 %fusion.1 = bf16[12,256,1024]{2,1,0:T(8,128)(2,1)S(1)} fusion(bf16[12,256,1024]{2,1,0:T(8,128)(2,1)} %param.10, f32[12,128]{1,0:T(8,128)S(1)} %convert_convert_fusion.1, f32[256,128]{1,0:T(8,128)S(1)} %maximum_convert_fusion, bf16[128,512]{1,0:T(8,128)(2,1)S(1)} %get-tuple-element.49, bf16[128,512]{1,0:T(8,128)(2,1)S(1)} %get-tuple-element.48), kind=kOutput, calls=%fused_computation.3 | convolution fusion | flops 822345728 | bytes 12982272 | tf_op jit(solution)/shard_map/dot_general | solution.py:165
  38.8 1.1 fusion.4
  40.7 1.9 %multiply_reduce_fusion.3 = (f32[256,128]{1,0:T(8,128)S(1)}, f32[12,128]{1,0:T(8,128)S(1)}) fusion(f32[12,128]{1,0:T(8,128)S(1)} %convert_convert_fusion.1, f32[256,128]{1,0:T(8,128)S(1)} %maximum_convert_fusion, bf16[12,256,1024]{2,1,0:T(8,128)(2,1)S(1)} %fusion.1, bf16[128,512]{1,0:T(8,128)(2,1)S(1)} %get-tuple-element.49, ...), kind=kOutput, calls=%fused_computation.10 | convolution fusion | flops 807369216 | bytes 6828032 | tf_op jit(solution)/shard_map/dot_general | solution.py:178
  42.8 7.1 %all-to-all-start.2 = ((bf16[16,24,512]{2,1,0:T(8,128)(2,1)}), bf16[16,24,512]{2,1,0:T(8,128)(2,1)S(1)}, u32[]{:S(2)}, u32[]{:S(2)}) async-start(bf16[16,24,512]{2,1,0:T(8,128)(2,1)} %pad_maximum_fusion), calls=%async_computation.2 | async-start | bytes 786432 | tf_op jit(solution)/shard_map/all_to_all | solution.py:156
  50.0 1.7 %collective-permute-start.4 = (f32[144,128]{1,0:T(8,128)S(1)}, f32[144,128]{1,0:T(8,128)S(1)}, u32[]{:S(2)}, u32[]{:S(2)}) collective-permute-start(f32[144,128]{1,0:T(8,128)S(1)} %pad_maximum_fusion.4), channel_id=1, source_target_pairs={{0,8},{8,0},{1,9},{9,1},{2,10},{10,2},{3,11},{11,3},{4,12},{12,4},... | collective-permute-start | bytes 221192 | tf_op jit(solution)/shard_map/ppermute | solution.py:28
  51.7 8.2 %collective-permute-done.4 = f32[144,128]{1,0:T(8,128)S(1)} collective-permute-done((f32[144,128]{1,0:T(8,128)S(1)}, f32[144,128]{1,0:T(8,128)S(1)}, u32[]{:S(2)}, u32[]{:S(2)}) %collective-permute-start.4) | collective-permute-done | bytes 73760 | tf_op jit(solution)/shard_map/ppermute | solution.py:28
  61.5 4.3 %all-to-all-start.3 = ((f32[4,96,128]{2,1,0:T(8,128)}), f32[4,96,128]{2,1,0:T(8,128)S(1)}, u32[]{:S(2)}, u32[]{:S(2)}) async-start(f32[4,96,128]{2,1,0:T(8,128)} %pad_maximum_fusion.2), calls=%async_computation.3 | async-start | bytes 393216 | tf_op jit(solution)/shard_map/all_to_all | solution.py:251
  65.8 5.8 %all-to-all-done.3 = f32[4,96,128]{2,1,0:T(8,128)S(1)} async-done(((f32[4,96,128]{2,1,0:T(8,128)}), f32[4,96,128]{2,1,0:T(8,128)S(1)}, u32[]{:S(2)}, u32[]{:S(2)}) %all-to-all-start.3) | async-done | bytes 196640 | tf_op jit(solution)/shard_map/all_to_all | solution.py:251
  72.6 5.8 %all-to-all-start.4 = ((bf16[16,24,512]{2,1,0:T(8,128)(2,1)}), bf16[16,24,512]{2,1,0:T(8,128)(2,1)S(1)}, u32[]{:S(2)}, u32[]{:S(2)}) async-start(bf16[16,24,512]{2,1,0:T(8,128)(2,1)} %broadcast_in_dim.33), calls=%async_computation.4 | async-start | bytes 786432 | tf_op jit(solution)/shard_map/all_to_all | solution.py:135
  78.6 3.8 %collective-permute-start.7 = (bf16[4,16,128]{2,1,0:T(8,128)(2,1)S(1)}, bf16[4,16,128]{2,1,0:T(8,128)(2,1)S(1)}, u32[]{:S(2)}, u32[]{:S(2)}) collective-permute-start(bf16[4,16,128]{2,1,0:T(8,128)(2,1)S(1)} %bitcast.107), channel_id=1, source_target_pairs={{0,2},{1,3},{2,0},{3,1},{4,6},{5,7},{6,4},{7,5},{8,10},{9,11},{10,... | collective-permute-start | bytes 49160 | tf_op jit(solution)/shard_map/ppermute | solution.py:28
  82.4 1.9 %collective-permute-done.7 = bf16[4,16,128]{2,1,0:T(8,128)(2,1)S(1)} collective-permute-done((bf16[4,16,128]{2,1,0:T(8,128)(2,1)S(1)}, bf16[4,16,128]{2,1,0:T(8,128)(2,1)S(1)}, u32[]{:S(2)}, u32[]{:S(2)}) %collective-permute-start.7) | collective-permute-done | bytes 16416 | tf_op jit(solution)/shard_map/ppermute | solution.py:28
  84.3 1.9 %collective-permute-done.8 = bf16[4,16,128]{2,1,0:T(8,128)(2,1)S(1)} collective-permute-done((bf16[4,16,128]{2,1,0:T(8,128)(2,1)S(1)}, bf16[4,16,128]{2,1,0:T(8,128)(2,1)S(1)}, u32[]{:S(2)}, u32[]{:S(2)}) %collective-permute-start.8) | collective-permute-done | bytes 16416 | tf_op jit(solution)/shard_map/ppermute | solution.py:28
  86.2 2.9 %all-to-all-done.4 = bf16[16,24,512]{2,1,0:T(8,128)(2,1)S(1)} async-done(((bf16[16,24,512]{2,1,0:T(8,128)(2,1)}), bf16[16,24,512]{2,1,0:T(8,128)(2,1)S(1)}, u32[]{:S(2)}, u32[]{:S(2)}) %all-to-all-start.4) | async-done | bytes 393248 | tf_op jit(solution)/shard_map/all_to_all | solution.py:135
  89.3 4.8 %fusion.3 = bf16[12,256,1024]{2,1,0:T(8,128)(2,1)S(1)} fusion(bf16[12,256,1024]{2,1,0:T(8,128)(2,1)} %param.10, f32[12,128]{1,0:T(8,128)S(1)} %get-tuple-element.40, f32[256,128]{1,0:T(8,128)S(1)} %bitcast.94, bf16[128,512]{1,0:T(8,128)(2,1)S(1)} %get-tuple-element.47, bf16[128,512]{1,0:T(8,128)(2,1)S(1)} %get-tuple-element.46), kind=kOutput, calls=%fused_computation.5 | convolution fusion | flops 822345728 | bytes 12982272 | tf_op jit(solution)/shard_map/dot_general | solution.py:165
  95.1 1.9 %multiply_reduce_fusion.1 = (f32[256,128]{1,0:T(8,128)S(1)}, f32[12,128]{1,0:T(8,128)S(1)}) fusion(f32[12,128]{1,0:T(8,128)S(1)} %get-tuple-element.40, f32[256,128]{1,0:T(8,128)S(1)} %bitcast.96, bf16[12,256,1024]{2,1,0:T(8,128)(2,1)S(1)} %fusion.3, bf16[128,512]{1,0:T(8,128)(2,1)S(1)} %get-tuple-element.47, bf16[128,512]{1,0:T(8,128)(2,1)S(1)} %get-tuple-element.46), kind=kOutput, calls=%fused_computation.7 | convolution fusion | flops 807369216 | bytes 6828032 | tf_op jit(solution)/shard_map/dot_general | solution.py:178
  98.1 4.3 %all-to-all-start.5 = ((bf16[16,24,512]{2,1,0:T(8,128)(2,1)}), bf16[16,24,512]{2,1,0:T(8,128)(2,1)S(1)}, u32[]{:S(2)}, u32[]{:S(2)}) async-start(bf16[16,24,512]{2,1,0:T(8,128)(2,1)} %pad_maximum_fusion.1), calls=%async_computation.5 | async-start | bytes 786432 | tf_op jit(solution)/shard_map/all_to_all | solution.py:156
  102.5 1.4 %collective-permute-start.10 = (f32[64,128]{1,0:T(8,128)S(1)}, f32[64,128]{1,0:T(8,128)S(1)}, u32[]{:S(2)}, u32[]{:S(2)}) collective-permute-start(f32[64,128]{1,0:T(8,128)S(1)} %slice_select_fusion), channel_id=1, source_target_pairs={{0,8},{8,0},{1,9},{9,1},{2,10},{10,2},{3,11},{11,3},{4,12},{12,4},... | collective-permute-start | bytes 98312 | tf_op jit(solution)/shard_map/ppermute | solution.py:28
  103.8 7.0 %collective-permute-done.10 = f32[64,128]{1,0:T(8,128)S(1)} collective-permute-done((f32[64,128]{1,0:T(8,128)S(1)}, f32[64,128]{1,0:T(8,128)S(1)}, u32[]{:S(2)}, u32[]{:S(2)}) %collective-permute-start.10) | collective-permute-done | bytes 32800 | tf_op jit(solution)/shard_map/ppermute | solution.py:28
  110.8 2.3 %all-to-all-done.5 = bf16[16,24,512]{2,1,0:T(8,128)(2,1)S(1)} async-done(((bf16[16,24,512]{2,1,0:T(8,128)(2,1)}), bf16[16,24,512]{2,1,0:T(8,128)(2,1)S(1)}, u32[]{:S(2)}, u32[]{:S(2)}) %all-to-all-start.5) | async-done | bytes 393248 | tf_op jit(solution)/shard_map/all_to_all | solution.py:156
  113.5 1.0 collective-permute-done.11
  114.5 1.4 %collective-permute-start.12 = (f32[16,128]{1,0:T(8,128)S(1)}, f32[16,128]{1,0:T(8,128)S(1)}, u32[]{:S(2)}, u32[]{:S(2)}) collective-permute-start(f32[16,128]{1,0:T(8,128)S(1)} %fusion.31), channel_id=1, source_target_pairs={{0,8},{8,0},{1,9},{9,1},{2,10},{10,2},{3,11},{11,3},{4,12},{12,4},... | collective-permute-start | bytes 24584 | tf_op jit(solution)/shard_map/ppermute | solution.py:28
  116.5 4.3 %all-to-all-start.6 = ((f32[4,32,128]{2,1,0:T(8,128)}), f32[4,32,128]{2,1,0:T(8,128)S(1)}, u32[]{:S(2)}, u32[]{:S(2)}) async-start(f32[4,32,128]{2,1,0:T(8,128)} %pad_maximum_fusion.6), calls=%async_computation.6 | async-start | bytes 131072 | tf_op jit(solution)/shard_map/all_to_all | solution.py:282
  120.8 1.4 %collective-permute-done.12 = f32[16,128]{1,0:T(8,128)S(1)} collective-permute-done((f32[16,128]{1,0:T(8,128)S(1)}, f32[16,128]{1,0:T(8,128)S(1)}, u32[]{:S(2)}, u32[]{:S(2)}) %collective-permute-start.12) | collective-permute-done | bytes 8224 | tf_op jit(solution)/shard_map/ppermute | solution.py:28
  122.8 2.6 %all-to-all-done.6 = f32[4,32,128]{2,1,0:T(8,128)S(1)} async-done(((f32[4,32,128]{2,1,0:T(8,128)}), f32[4,32,128]{2,1,0:T(8,128)S(1)}, u32[]{:S(2)}, u32[]{:S(2)}) %all-to-all-start.6) | async-done | bytes 65568 | tf_op jit(solution)/shard_map/all_to_all | solution.py:282
  (112 shorter events, 10.9 us)
Async XLA Ops:
  2.1 11.2 %all-to-all-start = ((f32[4,64,128]{2,1,0:T(8,128)}), f32[4,64,128]{2,1,0:T(8,128)S(1)}, u32[]{:S(2)}, u32[]{:S(2)}) async-start(f32[4,64,128]{2,1,0:T(8,128)} %get-tuple-element.16), calls=%async_computation | async-start | bytes 262144 | tf_op jit(solution)/shard_map/all_to_all | solution.py:218
  14.1 11.7 %collective-permute-start.1 = (bf16[1,64,128]{2,1,0:T(8,128)(2,1)S(1)}, bf16[1,64,128]{2,1,0:T(8,128)(2,1)S(1)}, u32[]{:S(2)}, u32[]{:S(2)}) collective-permute-start(bf16[1,64,128]{2,1,0:T(8,128)(2,1)S(1)} %bitcast.104), channel_id=1, source_target_pairs={{0,4},{4,0},{1,5},{5,1},{2,6},{6,2},{3,7},{7,3},{8,12},{12,8},{9,1... | collective-permute-start | bytes 49160 | tf_op jit(solution)/shard_map/ppermute | solution.py:28
  14.1 19.8 %all-to-all-start.1 = ((bf16[16,24,512]{2,1,0:T(8,128)(2,1)}), bf16[16,24,512]{2,1,0:T(8,128)(2,1)S(1)}, u32[]{:S(2)}, u32[]{:S(2)}) async-start(bf16[16,24,512]{2,1,0:T(8,128)(2,1)} %broadcast_in_dim.14), calls=%async_computation.1 | async-start | bytes 786432 | tf_op jit(solution)/shard_map/all_to_all | solution.py:135
  21.2 8.0 %collective-permute-start = (f32[48,128]{1,0:T(8,128)}, f32[48,128]{1,0:T(8,128)S(1)}, u32[]{:S(2)}, u32[]{:S(2)}) collective-permute-start(f32[48,128]{1,0:T(8,128)} %get-tuple-element.18), channel_id=1, source_target_pairs={{0,8},{8,0},{1,9},{9,1},{2,10},{10,2},{3,11},{11,3},{4,12},{12,4},... | collective-permute-start | bytes 73736 | tf_op jit(solution)/shard_map/ppermute | solution.py:28
  25.9 8.0 %collective-permute-start.2 = (bf16[128,128]{1,0:T(8,128)(2,1)S(1)}, bf16[128,128]{1,0:T(8,128)(2,1)S(1)}, u32[]{:S(2)}, u32[]{:S(2)}) collective-permute-start(bf16[128,128]{1,0:T(8,128)(2,1)S(1)} %bitcast.101), channel_id=1, source_target_pairs={{0,8},{8,0},{1,9},{9,1},{2,10},{10,2},{3,11},{11,3},{4,12},{12,4},... | collective-permute-start | bytes 98312 | tf_op jit(solution)/shard_map/ppermute | solution.py:28
  42.6 46.6 %copy-start = (f32[12,128]{1,0:T(8,128)S(1)}, f32[12,128]{1,0:T(8,128)}, u32[]{:S(2)}) copy-start(f32[12,128]{1,0:T(8,128)} %param.19) | copy-start | bytes 18436
  42.6 46.6 %copy-start.1 = (f32[12,128]{1,0:T(8,128)S(1)}, f32[12,128]{1,0:T(8,128)}, u32[]{:S(2)}) copy-start(f32[12,128]{1,0:T(8,128)} %param.18) | copy-start | bytes 18436
  42.6 46.6 %copy-start.2 = (f32[12,128]{1,0:T(8,128)S(1)}, f32[12,128]{1,0:T(8,128)}, u32[]{:S(2)}) copy-start(f32[12,128]{1,0:T(8,128)} %param.13) | copy-start | bytes 18436
  42.7 7.2 %collective-permute-start.3 = (f32[144,128]{1,0:T(8,128)S(1)}, f32[144,128]{1,0:T(8,128)S(1)}, u32[]{:S(2)}, u32[]{:S(2)}) collective-permute-start(f32[144,128]{1,0:T(8,128)S(1)} %pad_maximum_fusion.3), channel_id=1, source_target_pairs={{0,4},{4,0},{1,5},{5,1},{2,6},{6,2},{3,7},{7,3},{8,12},{12,8},{9,1... | collective-permute-start | bytes 221192 | tf_op jit(solution)/shard_map/ppermute | solution.py:28
  42.8 17.8 %all-to-all-start.2 = ((bf16[16,24,512]{2,1,0:T(8,128)(2,1)}), bf16[16,24,512]{2,1,0:T(8,128)(2,1)S(1)}, u32[]{:S(2)}, u32[]{:S(2)}) async-start(bf16[16,24,512]{2,1,0:T(8,128)(2,1)} %pad_maximum_fusion), calls=%async_computation.2 | async-start | bytes 786432 | tf_op jit(solution)/shard_map/all_to_all | solution.py:156
  50.0 9.9 %collective-permute-start.4 = (f32[144,128]{1,0:T(8,128)S(1)}, f32[144,128]{1,0:T(8,128)S(1)}, u32[]{:S(2)}, u32[]{:S(2)}) collective-permute-start(f32[144,128]{1,0:T(8,128)S(1)} %pad_maximum_fusion.4), channel_id=1, source_target_pairs={{0,8},{8,0},{1,9},{9,1},{2,10},{10,2},{3,11},{11,3},{4,12},{12,4},... | collective-permute-start | bytes 221192 | tf_op jit(solution)/shard_map/ppermute | solution.py:28
  61.5 10.1 %all-to-all-start.3 = ((f32[4,96,128]{2,1,0:T(8,128)}), f32[4,96,128]{2,1,0:T(8,128)S(1)}, u32[]{:S(2)}, u32[]{:S(2)}) async-start(f32[4,96,128]{2,1,0:T(8,128)} %pad_maximum_fusion.2), calls=%async_computation.3 | async-start | bytes 393216 | tf_op jit(solution)/shard_map/all_to_all | solution.py:251
  71.6 6.8 %collective-permute-start.5 = (bf16[2,16,128]{2,1,0:T(8,128)(2,1)S(1)}, bf16[2,16,128]{2,1,0:T(8,128)(2,1)S(1)}, u32[]{:S(2)}, u32[]{:S(2)}) collective-permute-start(bf16[2,16,128]{2,1,0:T(8,128)(2,1)S(1)} %bitcast.110), channel_id=1, source_target_pairs={{0,4},{4,0},{1,5},{5,1},{2,6},{6,2},{3,7},{7,3},{8,12},{12,8},{9,1... | collective-permute-start | bytes 24584 | tf_op jit(solution)/shard_map/ppermute | solution.py:28
  72.6 16.5 %all-to-all-start.4 = ((bf16[16,24,512]{2,1,0:T(8,128)(2,1)}), bf16[16,24,512]{2,1,0:T(8,128)(2,1)S(1)}, u32[]{:S(2)}, u32[]{:S(2)}) async-start(bf16[16,24,512]{2,1,0:T(8,128)(2,1)} %broadcast_in_dim.33), calls=%async_computation.4 | async-start | bytes 786432 | tf_op jit(solution)/shard_map/all_to_all | solution.py:135
  78.4 4.0 %collective-permute-start.6 = (bf16[4,16,128]{2,1,0:T(8,128)(2,1)S(1)}, bf16[4,16,128]{2,1,0:T(8,128)(2,1)S(1)}, u32[]{:S(2)}, u32[]{:S(2)}) collective-permute-start(bf16[4,16,128]{2,1,0:T(8,128)(2,1)S(1)} %bitcast.106), channel_id=1, source_target_pairs={{0,3},{1,2},{2,1},{3,0},{4,7},{5,6},{6,5},{7,4},{8,11},{9,10},{10,... | collective-permute-start | bytes 49160 | tf_op jit(solution)/shard_map/ppermute | solution.py:28
  78.6 5.7 %collective-permute-start.7 = (bf16[4,16,128]{2,1,0:T(8,128)(2,1)S(1)}, bf16[4,16,128]{2,1,0:T(8,128)(2,1)S(1)}, u32[]{:S(2)}, u32[]{:S(2)}) collective-permute-start(bf16[4,16,128]{2,1,0:T(8,128)(2,1)S(1)} %bitcast.107), channel_id=1, source_target_pairs={{0,2},{1,3},{2,0},{3,1},{4,6},{5,7},{6,4},{7,5},{8,10},{9,11},{10,... | collective-permute-start | bytes 49160 | tf_op jit(solution)/shard_map/ppermute | solution.py:28
  82.4 3.7 %collective-permute-start.8 = (bf16[4,16,128]{2,1,0:T(8,128)(2,1)S(1)}, bf16[4,16,128]{2,1,0:T(8,128)(2,1)S(1)}, u32[]{:S(2)}, u32[]{:S(2)}) collective-permute-start(bf16[4,16,128]{2,1,0:T(8,128)(2,1)S(1)} %bitcast.108), channel_id=1, source_target_pairs={{0,1},{1,0},{2,3},{3,2},{4,5},{5,4},{6,7},{7,6},{8,9},{9,8},{10,11... | collective-permute-start | bytes 49160 | tf_op jit(solution)/shard_map/ppermute | solution.py:28
  97.1 5.3 %collective-permute-start.9 = (f32[128,128]{1,0:T(8,128)S(1)}, f32[128,128]{1,0:T(8,128)S(1)}, u32[]{:S(2)}, u32[]{:S(2)}) collective-permute-start(f32[128,128]{1,0:T(8,128)S(1)} %pad_maximum_fusion.5), channel_id=1, source_target_pairs={{0,4},{4,0},{1,5},{5,1},{2,6},{6,2},{3,7},{7,3},{8,12},{12,8},{9,1... | collective-permute-start | bytes 196616 | tf_op jit(solution)/shard_map/ppermute | solution.py:28
  98.1 15.1 %all-to-all-start.5 = ((bf16[16,24,512]{2,1,0:T(8,128)(2,1)}), bf16[16,24,512]{2,1,0:T(8,128)(2,1)S(1)}, u32[]{:S(2)}, u32[]{:S(2)}) async-start(bf16[16,24,512]{2,1,0:T(8,128)(2,1)} %pad_maximum_fusion.1), calls=%async_computation.5 | async-start | bytes 786432 | tf_op jit(solution)/shard_map/all_to_all | solution.py:156
  102.5 8.4 %collective-permute-start.10 = (f32[64,128]{1,0:T(8,128)S(1)}, f32[64,128]{1,0:T(8,128)S(1)}, u32[]{:S(2)}, u32[]{:S(2)}) collective-permute-start(f32[64,128]{1,0:T(8,128)S(1)} %slice_select_fusion), channel_id=1, source_target_pairs={{0,8},{8,0},{1,9},{9,1},{2,10},{10,2},{3,11},{11,3},{4,12},{12,4},... | collective-permute-start | bytes 98312 | tf_op jit(solution)/shard_map/ppermute | solution.py:28
  113.2 1.3 collective-permute-start.11
  114.5 7.6 %collective-permute-start.12 = (f32[16,128]{1,0:T(8,128)S(1)}, f32[16,128]{1,0:T(8,128)S(1)}, u32[]{:S(2)}, u32[]{:S(2)}) collective-permute-start(f32[16,128]{1,0:T(8,128)S(1)} %fusion.31), channel_id=1, source_target_pairs={{0,8},{8,0},{1,9},{9,1},{2,10},{10,2},{3,11},{11,3},{4,12},{12,4},... | collective-permute-start | bytes 24584 | tf_op jit(solution)/shard_map/ppermute | solution.py:28
  116.5 8.9 %all-to-all-start.6 = ((f32[4,32,128]{2,1,0:T(8,128)}), f32[4,32,128]{2,1,0:T(8,128)S(1)}, u32[]{:S(2)}, u32[]{:S(2)}) async-start(f32[4,32,128]{2,1,0:T(8,128)} %pad_maximum_fusion.6), calls=%async_computation.6 | async-start | bytes 131072 | tf_op jit(solution)/shard_map/all_to_all | solution.py:282

commit v5 on v4

--- a/solution.py
+++ b/solution.py
@@ -223,38 +223,39 @@
 
     pad = [a16[n * ranks : (n + 1) * ranks] for n in range(4)]
     slots = spread_slots(wide_second, [jnp.concatenate(pad, axis=1)])
-    slots, a16, own_first = lax.optimization_barrier((slots, a16, own_first))
+    slots, a16 = lax.optimization_barrier((slots, a16))
     b16, _ = spread_second(slots, ranks)
     a16 = join_cores(a16[None]).reshape(-1, rank)
     low, up = pick(high, a16, swap(a16, "zh", 1))
     a16 = jnp.concatenate([low, up], axis=0)
-    low, up = pick(high, own_first, swap(own_first, "zh", 1))
+    c16 = factor_time.astype(jnp.bfloat16)
+    slope, part_second = make_slope(readings, a16, b16, c16)
+    part_first, part_time = make_cross(slope, a16, b16, c16)
+    second, _ = sum_second(second_slots(part_second, ni, []), ranks)
+    part, [part_time] = core_half(part_first, [part_time])
+    sent = jnp.concatenate([part, part_time, own_first], axis=0)
+    came = swap(sent, "zh", 1)
+    low, up = pick(high, own_first, came[9 * rows :])
     pair_first, pair_mean, pair_square = [
         jnp.concatenate([low[n : n + rows], up[n : n + rows]], axis=0)
         for n in (0, rows, 2 * rows)
     ]
-    c16 = factor_time.astype(jnp.bfloat16)
-    slope, part_second = make_slope(readings, a16, b16, c16)
-    slots = second_slots(part_second, ni, [jnp.concatenate(pad, axis=1)])
-    slope, slots = lax.optimization_barrier((slope, slots))
-    second, _ = sum_second(slots, ranks)
-    part_first, part_time = make_cross(slope, a16, b16, c16)
-    part, [time_ja] = core_half(part_first, [part_time])
-    both = jnp.concatenate([part, time_ja], axis=0)
-    both = both + swap(both, "zh", 1)
-    part, time_ja = both[: 8 * rows], both[8 * rows :]
+    part = part + came[: 8 * rows]
+    time_ja = part_time + came[8 * rows : 9 * rows]
     part = part.reshape(2, nt, rows, rank).transpose(1, 0, 2, 3).reshape(nt, 2 * rows, rank)
     second = stack_columns(second)
-    slots = jnp.concatenate(
-        [part, jnp.broadcast_to(second, (nt,) + second.shape)], axis=1
-    )
-    got = jnp.sum(lax.all_to_all(slots, "ta", 0, 0), axis=0)
+    slot = lambda t: jnp.concatenate(
+        [lax.dynamic_index_in_dim(part, t, 0, keepdims=False), second], axis=0
+    )
+    got = [slot(ta)] + [swap(slot(ta ^ k), "ta", k) for k in (1, 2, 3)]
+    got = (got[0] + got[1]) + (got[2] + got[3])
+    grad_first, grad_second = got[: 2 * rows], got[2 * rows :]
     count = ADAM_STEP + 1
     wide_second, wide_mean, wide_square = adam(
-        wide_second, got[2 * rows :] * scale_second, wide_mean, wide_square, count
+        wide_second, grad_second * scale_second, wide_mean, wide_square, count
     )
     pair_first, pair_mean, pair_square = adam(
-        pair_first, got[: 2 * rows] * scale_first, pair_mean, pair_square, count
+        pair_first, grad_first * scale_first, pair_mean, pair_square, count
     )
 
     slots = spread_slots(wide_second, bf16_pair(fold(time_ja, ranks // 2)))
@@ -267,19 +268,20 @@
     c16 = factor_time.astype(jnp.bfloat16)
     slope, part_second = make_slope(readings, a16, b16, c16)
     part_first, part_time = make_cross(slope, a16, b16, c16)
+    part, [part_time] = core_half(part_first, [part_time])
     second, came = sum_second(
         second_slots(part_second, ni, bf16_pair(fold(part_time, ranks // 2))), ranks
     )
-    part, _ = core_half(part_first, [])
     keep, send = pick(high, part[: 4 * rows], part[4 * rows :])
     part = keep + swap(send, "zh", 1)
     time_sum = time_of(came, rank)
-    for axis in ("co", "zh"):
-        time_sum = time_sum + swap(time_sum, axis, 1)
+    time_sum = time_sum + swap(time_sum, "zh", 1)
     slots = jnp.concatenate(
         [part.reshape(nt, rows, rank), stack_columns(second).reshape(nt, flat, rank)], axis=1
     )
-    got = jnp.sum(lax.all_to_all(slots, "ta", 0, 0), axis=0)
+    slot = lambda t: lax.dynamic_index_in_dim(slots, t, 0, keepdims=False)
+    got = [slot(ta)] + [swap(slot(ta ^ k), "ta", k) for k in (1, 2, 3)]
+    got = (got[0] + got[1]) + (got[2] + got[3])
     count = ADAM_STEP + 2
     first = lambda x: jnp.where(high, x[rows:], x[:rows])
     own = lambda x: unstack_columns(lax.dynamic_slice_in_dim(x, ta * flat, flat, axis=0), ranks)

time: 128 us -> 120 us (0.938)
  blocking collectives: 0 us -> 11.2 us
  starting transfers between devices: 53.7 us -> 43.5 us
  waiting for transfers between devices: 46 us -> 39.2 us
  other arithmetic: 6.83 us -> 4.73 us
    all_to_all x3 -> x0, starting transfers between devices: 14.6 us -> none  [the longest x2 8.57 us: body(): got = jnp.sum(lax.all_to_all(slots, 'ta', 0, 0), axis=0)]
    all_to_all x3 -> x0, waiting for transfers between devices: 12.8 us -> none  [the longest x2 8.4 us: body(): got = jnp.sum(lax.all_to_all(slots, 'ta', 0, 0), axis=0)]
    all_to_all x0 -> x1, blocking collectives: none -> 11.2 us  [body(): got = lax.all_to_all(slots, 'ta', 0, 0)]
    ppermute x13 -> x17, starting transfers between devices: 14.9 us -> 24.7 us  [swap(): return lax.ppermute(x, axis, [(i, i ^ k) for i in range(n)])]
    all_to_all x2, waiting for transfers between devices: 3.02 us -> 10.4 us  [sum_second(): got = lax.all_to_all(slots, 'ia', 0, 0)]
    ppermute x13 -> x17, waiting for transfers between devices: 27.2 us -> 21.7 us  [swap(): return lax.ppermute(x, axis, [(i, i ^ k) for i in range(n)])]
    all_to_all x2, waiting for transfers between devices: 2.88 us -> 7.1 us  [spread_second(): got = lax.all_to_all(slots, 'ia', 0, 0)]
    all_to_all x2, starting transfers between devices: 11.4 us -> 8.23 us  [sum_second(): got = lax.all_to_all(slots, 'ia', 0, 0)]
  transfers between devices with their start and end apart: 20 -> 21, of which waited for: 14 -> 16; matrix products, arithmetic and copies ran while one was open for 4% -> 3% of each run, Pallas kernels for 0% -> 0%
where the time goes in v5:
time: 120 us; the launch traced here: 119 us
  starting transfers between devices  43.5 us (36%)
  waiting for transfers between devices  39.2 us (33%)
  matrix products  15.6 us (13%)
  blocking collectives  11.2 us (9%)
  other arithmetic  4.73 us (4%)
  local copies, waits for them, and re-layouts  1.89 us (2%)
  Pallas kernels  1.45 us (1%)
  between operations  1.4 us (1%)
    ppermute x17, starting transfers between devices, swap(): return lax.ppermute(x, axis, [(i, i ^ k) for i in range(n)])  24.7 us
    ppermute x17, waiting for transfers between devices, swap(): return lax.ppermute(x, axis, [(i, i ^ k) for i in range(n)])  21.7 us
    all_to_all x1, blocking collectives, body(): got = lax.all_to_all(slots, 'ta', 0, 0)  11.2 us
    all_to_all x2, starting transfers between devices, spread_second(): got = lax.all_to_all(slots, 'ia', 0, 0)  10.6 us
    all_to_all x2, waiting for transfers between devices, sum_second(): got = lax.all_to_all(slots, 'ia', 0, 0)  10.4 us
    dot_general x2, matrix products, make_slope(): lax.dot_general(scaled, b16, (((2,), (0,)), ((), ())), preferred_element_...  9.68 us
    all_to_all x2, starting transfers between devices, sum_second(): got = lax.all_to_all(slots, 'ia', 0, 0)  8.23 us
    all_to_all x2, waiting for transfers between devices, spread_second(): got = lax.all_to_all(slots, 'ia', 0, 0)  7.1 us
  transfers between devices with their start and end apart: 21, of which 16 were waited for; matrix products, arithmetic and copies ran while one was open for 3% of the time, Pallas kernels for 0%

profile of v5, /device:TPU:32, one launch (start us, length us, event | category | flops | bytes accessed | tf_op | source)
XLA Modules:
  0.0 119.0 jit_solution(562585987519478544)
XLA Ops:
  0.6 1.5 %shard_map.169 = (f32[4,64,128]{2,1,0:T(8,128)}, f32[48,128]{1,0:T(8,128)}) custom-call(f32[16,128]{1,0:T(8,128)} %f0.1, f32[16,128]{1,0:T(8,128)} %f1.1, f32[16,128]{1,0:T(8,128)} %f2.1, f32[8,256]{1,0:T(8,128)} %s0.1, f32[8,256]{1,0:T(8,128)} %s1_.1, f32[8,256]{1,0:T(8,128)} %s2_.1), custom_call_target="tpu_custom_call" | custom-call | tf_op jit(solution)/shard_map/pallas_call | solution.py:70
  2.1 11.2 %all_to_all.25 = f32[4,64,128]{2,1,0:T(8,128)S(1)} all-to-all(f32[4,64,128]{2,1,0:T(8,128)} %get-tuple-element.13), channel_id=1, replica_groups=mesh['ia'=16,'zh'=2,'co'=2,'ta'=4] {'ta'}, dimensions={0} | all-to-all | bytes 262144 | tf_op jit(solution)/shard_map/all_to_all | solution.py:218
  14.1 7.0 %all-to-all-start.1 = ((bf16[16,24,512]{2,1,0:T(8,128)(2,1)}), bf16[16,24,512]{2,1,0:T(8,128)(2,1)S(1)}, u32[]{:S(2)}, u32[]{:S(2)}) async-start(bf16[16,24,512]{2,1,0:T(8,128)(2,1)} %broadcast_in_dim.10), calls=%async_computation.1 | async-start | bytes 786432 | tf_op jit(solution)/shard_map/all_to_all | solution.py:135
  21.2 4.7 %collective-permute-start.1 = (bf16[128,128]{1,0:T(8,128)(2,1)S(1)}, bf16[128,128]{1,0:T(8,128)(2,1)S(1)}, u32[]{:S(2)}, u32[]{:S(2)}) collective-permute-start(bf16[128,128]{1,0:T(8,128)(2,1)S(1)} %bitcast.125), channel_id=1, source_target_pairs={{0,8},{8,0},{1,9},{9,1},{2,10},{10,2},{3,11},{11,3},{4,12},{12,4},... | collective-permute-start | bytes 98312 | tf_op jit(solution)/shard_map/ppermute | solution.py:28
  26.6 2.9 %collective-permute-done.1 = bf16[128,128]{1,0:T(8,128)(2,1)S(1)} collective-permute-done((bf16[128,128]{1,0:T(8,128)(2,1)S(1)}, bf16[128,128]{1,0:T(8,128)(2,1)S(1)}, u32[]{:S(2)}, u32[]{:S(2)}) %collective-permute-start.1) | collective-permute-done | bytes 32800 | tf_op jit(solution)/shard_map/ppermute | solution.py:28
  29.5 2.4 %all-to-all-done.1 = bf16[16,24,512]{2,1,0:T(8,128)(2,1)S(1)} async-done(((bf16[16,24,512]{2,1,0:T(8,128)(2,1)}), bf16[16,24,512]{2,1,0:T(8,128)(2,1)S(1)}, u32[]{:S(2)}, u32[]{:S(2)}) %all-to-all-start.1) | async-done | bytes 393248 | tf_op jit(solution)/shard_map/all_to_all | solution.py:135
  31.9 4.9 %fusion.1 = bf16[12,256,1024]{2,1,0:T(8,128)(2,1)S(1)} fusion(bf16[12,256,1024]{2,1,0:T(8,128)(2,1)} %param.10, f32[12,128]{1,0:T(8,128)S(1)} %convert_convert_fusion.1, f32[256,128]{1,0:T(8,128)S(1)} %maximum_convert_fusion, bf16[128,512]{1,0:T(8,128)(2,1)S(1)} %get-tuple-element.43, bf16[128,512]{1,0:T(8,128)(2,1)S(1)} %get-tuple-element.42), kind=kOutput, calls=%fused_computation.3 | convolution fusion | flops 822345728 | bytes 12982272 | tf_op jit(solution)/shard_map/dot_general | solution.py:165
  36.8 1.9 %multiply_reduce_fusion.3 = (f32[256,128]{1,0:T(8,128)S(1)}, f32[12,128]{1,0:T(8,128)S(1)}) fusion(f32[12,128]{1,0:T(8,128)S(1)} %convert_convert_fusion.1, f32[256,128]{1,0:T(8,128)S(1)} %maximum_convert_fusion, bf16[12,256,1024]{2,1,0:T(8,128)(2,1)S(1)} %fusion.1, bf16[128,512]{1,0:T(8,128)(2,1)S(1)} %get-tuple-element.43, ...), kind=kOutput, calls=%fused_computation.10 | convolution fusion | flops 807369216 | bytes 6828032 | tf_op jit(solution)/shard_map/dot_general | solution.py:178
  40.0 1.2 %collective-permute-done.2 = f32[144,128]{1,0:T(8,128)S(1)} collective-permute-done((f32[144,128]{1,0:T(8,128)S(1)}, f32[144,128]{1,0:T(8,128)S(1)}, u32[]{:S(2)}, u32[]{:S(2)}) %collective-permute-start.2) | collective-permute-done | bytes 73760 | tf_op jit(solution)/shard_map/ppermute | solution.py:28
  41.3 4.6 %collective-permute-start.3 = (f32[192,128]{1,0:T(8,128)S(1)}, f32[192,128]{1,0:T(8,128)S(1)}, u32[]{:S(2)}, u32[]{:S(2)}) collective-permute-start(f32[192,128]{1,0:T(8,128)S(1)} %pad_maximum_fusion.2), channel_id=1, source_target_pairs={{0,8},{8,0},{1,9},{9,1},{2,10},{10,2},{3,11},{11,3},{4,12},{12,4},... | collective-permute-start | bytes 294920 | tf_op jit(solution)/shard_map/ppermute | solution.py:28
  46.6 4.7 %all-to-all-start.2 = ((bf16[16,16,512]{2,1,0:T(8,128)(2,1)}), bf16[16,16,512]{2,1,0:T(8,128)(2,1)S(1)}, u32[]{:S(2)}, u32[]{:S(2)}) async-start(bf16[16,16,512]{2,1,0:T(8,128)(2,1)} %pad_maximum_fusion.1), calls=%async_computation.2 | async-start | bytes 524288 | tf_op jit(solution)/shard_map/all_to_all | solution.py:156
  52.3 7.7 %all-to-all-done.2 = bf16[16,16,512]{2,1,0:T(8,128)(2,1)S(1)} async-done(((bf16[16,16,512]{2,1,0:T(8,128)(2,1)}), bf16[16,16,512]{2,1,0:T(8,128)(2,1)S(1)}, u32[]{:S(2)}, u32[]{:S(2)}) %all-to-all-start.2) | async-done | bytes 262176 | tf_op jit(solution)/shard_map/all_to_all | solution.py:156
  60.3 1.4 %collective-permute-start.5 = (f32[96,128]{1,0:T(8,128)S(1)}, f32[96,128]{1,0:T(8,128)S(1)}, u32[]{:S(2)}, u32[]{:S(2)}) collective-permute-start(f32[96,128]{1,0:T(8,128)S(1)} %constant_dynamic-update-slice_fusion.18), channel_id=1, source_target_pairs={{0,2},{1,3},{2,0},{3,1},{4,6},{5,7},{6,4},{7,5},{8,10},{9,11},{10,... | collective-permute-start | bytes 147464 | tf_op jit(solution)/shard_map/ppermute | solution.py:28
  61.7 1.1 collective-permute-start.6
  62.8 2.0 %collective-permute-start.4 = (f32[96,128]{1,0:T(8,128)S(1)}, f32[96,128]{1,0:T(8,128)S(1)}, u32[]{:S(2)}, u32[]{:S(2)}) collective-permute-start(f32[96,128]{1,0:T(8,128)S(1)} %get-tuple-element.80), channel_id=1, source_target_pairs={{0,1},{1,0},{2,3},{3,2},{4,5},{5,4},{6,7},{7,6},{8,9},{9,8},{10,11... | collective-permute-start | bytes 147464 | tf_op jit(solution)/shard_map/ppermute | solution.py:28
  66.0 1.4 %collective-permute-done.4 = f32[96,128]{1,0:T(8,128)S(1)} collective-permute-done((f32[96,128]{1,0:T(8,128)S(1)}, f32[96,128]{1,0:T(8,128)S(1)}, u32[]{:S(2)}, u32[]{:S(2)}) %collective-permute-start.4) | collective-permute-done | bytes 49184 | tf_op jit(solution)/shard_map/ppermute | solution.py:28
  68.4 3.6 %all-to-all-start.3 = ((bf16[16,24,512]{2,1,0:T(8,128)(2,1)}), bf16[16,24,512]{2,1,0:T(8,128)(2,1)S(1)}, u32[]{:S(2)}, u32[]{:S(2)}) async-start(bf16[16,24,512]{2,1,0:T(8,128)(2,1)} %broadcast_in_dim.12), calls=%async_computation.3 | async-start | bytes 786432 | tf_op jit(solution)/shard_map/all_to_all | solution.py:135
  72.0 1.6 %collective-permute-start.10 = (bf16[4,16,128]{2,1,0:T(8,128)(2,1)S(1)}, bf16[4,16,128]{2,1,0:T(8,128)(2,1)S(1)}, u32[]{:S(2)}, u32[]{:S(2)}) collective-permute-start(bf16[4,16,128]{2,1,0:T(8,128)(2,1)S(1)} %bitcast.129), channel_id=1, source_target_pairs={{0,1},{1,0},{2,3},{3,2},{4,5},{5,4},{6,7},{7,6},{8,9},{9,8},{10,11... | collective-permute-start | bytes 49160 | tf_op jit(solution)/shard_map/ppermute | solution.py:28
  74.0 1.6 %collective-permute-start.8 = (bf16[4,16,128]{2,1,0:T(8,128)(2,1)S(1)}, bf16[4,16,128]{2,1,0:T(8,128)(2,1)S(1)}, u32[]{:S(2)}, u32[]{:S(2)}) collective-permute-start(bf16[4,16,128]{2,1,0:T(8,128)(2,1)S(1)} %bitcast.131), channel_id=1, source_target_pairs={{0,3},{1,2},{2,1},{3,0},{4,7},{5,6},{6,5},{7,4},{8,11},{9,10},{10,... | collective-permute-start | bytes 49160 | tf_op jit(solution)/shard_map/ppermute | solution.py:28
  75.8 2.4 %collective-permute-done.9 = bf16[4,16,128]{2,1,0:T(8,128)(2,1)S(1)} collective-permute-done((bf16[4,16,128]{2,1,0:T(8,128)(2,1)S(1)}, bf16[4,16,128]{2,1,0:T(8,128)(2,1)S(1)}, u32[]{:S(2)}, u32[]{:S(2)}) %collective-permute-start.9) | collective-permute-done | bytes 16416 | tf_op jit(solution)/shard_map/ppermute | solution.py:28
  78.3 4.7 %all-to-all-done.3 = bf16[16,24,512]{2,1,0:T(8,128)(2,1)S(1)} async-done(((bf16[16,24,512]{2,1,0:T(8,128)(2,1)}), bf16[16,24,512]{2,1,0:T(8,128)(2,1)S(1)}, u32[]{:S(2)}, u32[]{:S(2)}) %all-to-all-start.3) | async-done | bytes 393248 | tf_op jit(solution)/shard_map/all_to_all | solution.py:135
  83.1 4.8 %fusion.3 = bf16[12,256,1024]{2,1,0:T(8,128)(2,1)S(1)} fusion(bf16[12,256,1024]{2,1,0:T(8,128)(2,1)} %param.10, f32[12,128]{1,0:T(8,128)S(1)} %get-tuple-element.34, f32[256,128]{1,0:T(8,128)S(1)} %bitcast.114, bf16[128,512]{1,0:T(8,128)(2,1)S(1)} %get-tuple-element.41, bf16[128,512]{1,0:T(8,128)(2,1)S(1)} %get-tuple-element.40), kind=kOutput, calls=%fused_computation.5 | convolution fusion | flops 822345728 | bytes 12982272 | tf_op jit(solution)/shard_map/dot_general | solution.py:165
  88.0 1.9 %multiply_reduce_fusion.1 = (f32[256,128]{1,0:T(8,128)S(1)}, f32[12,128]{1,0:T(8,128)S(1)}) fusion(f32[12,128]{1,0:T(8,128)S(1)} %get-tuple-element.34, f32[256,128]{1,0:T(8,128)S(1)} %bitcast.115, bf16[12,256,1024]{2,1,0:T(8,128)(2,1)S(1)} %fusion.3, bf16[128,512]{1,0:T(8,128)(2,1)S(1)} %get-tuple-element.41, bf16[128,512]{1,0:T(8,128)(2,1)S(1)} %get-tuple-element.40), kind=kOutput, calls=%fused_computation.7 | convolution fusion | flops 807369216 | bytes 6828032 | tf_op jit(solution)/shard_map/dot_general | solution.py:178
  91.1 1.2 %collective-permute-done.11 = f32[144,128]{1,0:T(8,128)S(1)} collective-permute-done((f32[144,128]{1,0:T(8,128)S(1)}, f32[144,128]{1,0:T(8,128)S(1)}, u32[]{:S(2)}, u32[]{:S(2)}) %collective-permute-start.11) | collective-permute-done | bytes 73760 | tf_op jit(solution)/shard_map/ppermute | solution.py:28
  93.3 3.6 %all-to-all-start.4 = ((bf16[16,24,512]{2,1,0:T(8,128)(2,1)}), bf16[16,24,512]{2,1,0:T(8,128)(2,1)S(1)}, u32[]{:S(2)}, u32[]{:S(2)}) async-start(bf16[16,24,512]{2,1,0:T(8,128)(2,1)} %pad_maximum_fusion), calls=%async_computation.4 | async-start | bytes 786432 | tf_op jit(solution)/shard_map/all_to_all | solution.py:156
  96.9 1.3 %collective-permute-start.12 = (f32[64,128]{1,0:T(8,128)S(1)}, f32[64,128]{1,0:T(8,128)S(1)}, u32[]{:S(2)}, u32[]{:S(2)}) collective-permute-start(f32[64,128]{1,0:T(8,128)S(1)} %slice_select_fusion), channel_id=1, source_target_pairs={{0,8},{8,0},{1,9},{9,1},{2,10},{10,2},{3,11},{11,3},{4,12},{12,4},... | collective-permute-start | bytes 98312 | tf_op jit(solution)/shard_map/ppermute | solution.py:28
  98.2 6.6 %collective-permute-done.12 = f32[64,128]{1,0:T(8,128)S(1)} collective-permute-done((f32[64,128]{1,0:T(8,128)S(1)}, f32[64,128]{1,0:T(8,128)S(1)}, u32[]{:S(2)}, u32[]{:S(2)}) %collective-permute-start.12) | collective-permute-done | bytes 32800 | tf_op jit(solution)/shard_map/ppermute | solution.py:28
  104.8 2.7 %all-to-all-done.4 = bf16[16,24,512]{2,1,0:T(8,128)(2,1)S(1)} async-done(((bf16[16,24,512]{2,1,0:T(8,128)(2,1)}), bf16[16,24,512]{2,1,0:T(8,128)(2,1)S(1)}, u32[]{:S(2)}, u32[]{:S(2)}) %all-to-all-start.4) | async-done | bytes 393248 | tf_op jit(solution)/shard_map/all_to_all | solution.py:156
  107.6 1.3 %collective-permute-start.16 = (f32[16,128]{1,0:T(8,128)S(1)}, f32[16,128]{1,0:T(8,128)S(1)}, u32[]{:S(2)}, u32[]{:S(2)}) collective-permute-start(f32[16,128]{1,0:T(8,128)S(1)} %pad_maximum_fusion.12), channel_id=1, source_target_pairs={{0,8},{8,0},{1,9},{9,1},{2,10},{10,2},{3,11},{11,3},{4,12},{12,4},... | collective-permute-start | bytes 24584 | tf_op jit(solution)/shard_map/ppermute | solution.py:28
  109.5 3.6 %collective-permute-start.13 = (f32[32,128]{1,0:T(8,128)S(1)}, f32[32,128]{1,0:T(8,128)S(1)}, u32[]{:S(2)}, u32[]{:S(2)}) collective-permute-start(f32[32,128]{1,0:T(8,128)S(1)} %get-tuple-element.62), channel_id=1, source_target_pairs={{0,1},{1,0},{2,3},{3,2},{4,5},{5,4},{6,7},{7,6},{8,9},{9,8},{10,11... | collective-permute-start | bytes 49160 | tf_op jit(solution)/shard_map/ppermute | solution.py:28
  113.4 1.9 %collective-permute-done.16 = f32[16,128]{1,0:T(8,128)S(1)} collective-permute-done((f32[16,128]{1,0:T(8,128)S(1)}, f32[16,128]{1,0:T(8,128)S(1)}, u32[]{:S(2)}, u32[]{:S(2)}) %collective-permute-start.16) | collective-permute-done | bytes 8224 | tf_op jit(solution)/shard_map/ppermute | solution.py:28
  116.0 1.7 %collective-permute-done.14 = f32[32,128]{1,0:T(8,128)S(1)} collective-permute-done((f32[32,128]{1,0:T(8,128)S(1)}, f32[32,128]{1,0:T(8,128)S(1)}, u32[]{:S(2)}, u32[]{:S(2)}) %collective-permute-start.14) | collective-permute-done | bytes 16416 | tf_op jit(solution)/shard_map/ppermute | solution.py:28
  (126 shorter events, 12.6 us)
Async XLA Ops:
  14.1 7.0 %collective-permute-start = (bf16[1,64,128]{2,1,0:T(8,128)(2,1)S(1)}, bf16[1,64,128]{2,1,0:T(8,128)(2,1)S(1)}, u32[]{:S(2)}, u32[]{:S(2)}) collective-permute-start(bf16[1,64,128]{2,1,0:T(8,128)(2,1)S(1)} %bitcast.127), channel_id=1, source_target_pairs={{0,4},{4,0},{1,5},{5,1},{2,6},{6,2},{3,7},{7,3},{8,12},{12,8},{9,1... | collective-permute-start | bytes 49160 | tf_op jit(solution)/shard_map/ppermute | solution.py:28
  14.1 17.8 %all-to-all-start.1 = ((bf16[16,24,512]{2,1,0:T(8,128)(2,1)}), bf16[16,24,512]{2,1,0:T(8,128)(2,1)S(1)}, u32[]{:S(2)}, u32[]{:S(2)}) async-start(bf16[16,24,512]{2,1,0:T(8,128)(2,1)} %broadcast_in_dim.10), calls=%async_computation.1 | async-start | bytes 786432 | tf_op jit(solution)/shard_map/all_to_all | solution.py:135
  21.2 8.3 %collective-permute-start.1 = (bf16[128,128]{1,0:T(8,128)(2,1)S(1)}, bf16[128,128]{1,0:T(8,128)(2,1)S(1)}, u32[]{:S(2)}, u32[]{:S(2)}) collective-permute-start(bf16[128,128]{1,0:T(8,128)(2,1)S(1)} %bitcast.125), channel_id=1, source_target_pairs={{0,8},{8,0},{1,9},{9,1},{2,10},{10,2},{3,11},{11,3},{4,12},{12,4},... | collective-permute-start | bytes 98312 | tf_op jit(solution)/shard_map/ppermute | solution.py:28
  38.7 2.5 %copy-start = (f32[48,128]{1,0:T(8,128)S(1)}, f32[48,128]{1,0:T(8,128)}, u32[]{:S(2)}) copy-start(f32[48,128]{1,0:T(8,128)} %get-tuple-element.16) | copy-start | bytes 73732
  39.8 43.3 %copy-start.1 = (f32[12,128]{1,0:T(8,128)S(1)}, f32[12,128]{1,0:T(8,128)}, u32[]{:S(2)}) copy-start(f32[12,128]{1,0:T(8,128)} %param.19) | copy-start | bytes 18436
  39.8 43.3 %copy-start.2 = (f32[12,128]{1,0:T(8,128)S(1)}, f32[12,128]{1,0:T(8,128)}, u32[]{:S(2)}) copy-start(f32[12,128]{1,0:T(8,128)} %param.18) | copy-start | bytes 18436
  39.8 43.3 %copy-start.3 = (f32[12,128]{1,0:T(8,128)S(1)}, f32[12,128]{1,0:T(8,128)}, u32[]{:S(2)}) copy-start(f32[12,128]{1,0:T(8,128)} %param.13) | copy-start | bytes 18436
  39.9 1.4 %collective-permute-start.2 = (f32[144,128]{1,0:T(8,128)S(1)}, f32[144,128]{1,0:T(8,128)S(1)}, u32[]{:S(2)}, u32[]{:S(2)}) collective-permute-start(f32[144,128]{1,0:T(8,128)S(1)} %pad_maximum_fusion.3), channel_id=1, source_target_pairs={{0,4},{4,0},{1,5},{5,1},{2,6},{6,2},{3,7},{7,3},{8,12},{12,8},{9,1... | collective-permute-start | bytes 221192 | tf_op jit(solution)/shard_map/ppermute | solution.py:28
  41.3 11.0 %collective-permute-start.3 = (f32[192,128]{1,0:T(8,128)S(1)}, f32[192,128]{1,0:T(8,128)S(1)}, u32[]{:S(2)}, u32[]{:S(2)}) collective-permute-start(f32[192,128]{1,0:T(8,128)S(1)} %pad_maximum_fusion.2), channel_id=1, source_target_pairs={{0,8},{8,0},{1,9},{9,1},{2,10},{10,2},{3,11},{11,3},{4,12},{12,4},... | collective-permute-start | bytes 294920 | tf_op jit(solution)/shard_map/ppermute | solution.py:28
  46.6 13.4 %all-to-all-start.2 = ((bf16[16,16,512]{2,1,0:T(8,128)(2,1)}), bf16[16,16,512]{2,1,0:T(8,128)(2,1)S(1)}, u32[]{:S(2)}, u32[]{:S(2)}) async-start(bf16[16,16,512]{2,1,0:T(8,128)(2,1)} %pad_maximum_fusion.1), calls=%async_computation.2 | async-start | bytes 524288 | tf_op jit(solution)/shard_map/all_to_all | solution.py:156
  60.3 5.1 %collective-permute-start.5 = (f32[96,128]{1,0:T(8,128)S(1)}, f32[96,128]{1,0:T(8,128)S(1)}, u32[]{:S(2)}, u32[]{:S(2)}) collective-permute-start(f32[96,128]{1,0:T(8,128)S(1)} %constant_dynamic-update-slice_fusion.18), channel_id=1, source_target_pairs={{0,2},{1,3},{2,0},{3,1},{4,6},{5,7},{6,4},{7,5},{8,10},{9,11},{10,... | collective-permute-start | bytes 147464 | tf_op jit(solution)/shard_map/ppermute | solution.py:28
  61.7 4.2 %collective-permute-start.6 = (f32[96,128]{1,0:T(8,128)S(1)}, f32[96,128]{1,0:T(8,128)S(1)}, u32[]{:S(2)}, u32[]{:S(2)}) collective-permute-start(f32[96,128]{1,0:T(8,128)S(1)} %get-tuple-element.98), channel_id=1, source_target_pairs={{0,3},{1,2},{2,1},{3,0},{4,7},{5,6},{6,5},{7,4},{8,11},{9,10},{10,... | collective-permute-start | bytes 147464 | tf_op jit(solution)/shard_map/ppermute | solution.py:28
  62.8 4.6 %collective-permute-start.4 = (f32[96,128]{1,0:T(8,128)S(1)}, f32[96,128]{1,0:T(8,128)S(1)}, u32[]{:S(2)}, u32[]{:S(2)}) collective-permute-start(f32[96,128]{1,0:T(8,128)S(1)} %get-tuple-element.80), channel_id=1, source_target_pairs={{0,1},{1,0},{2,3},{3,2},{4,5},{5,4},{6,7},{7,6},{8,9},{9,8},{10,11... | collective-permute-start | bytes 147464 | tf_op jit(solution)/shard_map/ppermute | solution.py:28
  67.5 4.5 %collective-permute-start.7 = (bf16[2,16,128]{2,1,0:T(8,128)(2,1)S(1)}, bf16[2,16,128]{2,1,0:T(8,128)(2,1)S(1)}, u32[]{:S(2)}, u32[]{:S(2)}) collective-permute-start(bf16[2,16,128]{2,1,0:T(8,128)(2,1)S(1)} %bitcast.132), channel_id=1, source_target_pairs={{0,4},{4,0},{1,5},{5,1},{2,6},{6,2},{3,7},{7,3},{8,12},{12,8},{9,1... | collective-permute-start | bytes 24584 | tf_op jit(solution)/shard_map/ppermute | solution.py:28
  68.4 14.6 %all-to-all-start.3 = ((bf16[16,24,512]{2,1,0:T(8,128)(2,1)}), bf16[16,24,512]{2,1,0:T(8,128)(2,1)S(1)}, u32[]{:S(2)}, u32[]{:S(2)}) async-start(bf16[16,24,512]{2,1,0:T(8,128)(2,1)} %broadcast_in_dim.12), calls=%async_computation.3 | async-start | bytes 786432 | tf_op jit(solution)/shard_map/all_to_all | solution.py:135
  72.0 3.8 %collective-permute-start.10 = (bf16[4,16,128]{2,1,0:T(8,128)(2,1)S(1)}, bf16[4,16,128]{2,1,0:T(8,128)(2,1)S(1)}, u32[]{:S(2)}, u32[]{:S(2)}) collective-permute-start(bf16[4,16,128]{2,1,0:T(8,128)(2,1)S(1)} %bitcast.129), channel_id=1, source_target_pairs={{0,1},{1,0},{2,3},{3,2},{4,5},{5,4},{6,7},{7,6},{8,9},{9,8},{10,11... | collective-permute-start | bytes 49160 | tf_op jit(solution)/shard_map/ppermute | solution.py:28
  73.6 4.6 %collective-permute-start.9 = (bf16[4,16,128]{2,1,0:T(8,128)(2,1)S(1)}, bf16[4,16,128]{2,1,0:T(8,128)(2,1)S(1)}, u32[]{:S(2)}, u32[]{:S(2)}) collective-permute-start(bf16[4,16,128]{2,1,0:T(8,128)(2,1)S(1)} %bitcast.130), channel_id=1, source_target_pairs={{0,2},{1,3},{2,0},{3,1},{4,6},{5,7},{6,4},{7,5},{8,10},{9,11},{10,... | collective-permute-start | bytes 49160 | tf_op jit(solution)/shard_map/ppermute | solution.py:28
  74.0 4.2 %collective-permute-start.8 = (bf16[4,16,128]{2,1,0:T(8,128)(2,1)S(1)}, bf16[4,16,128]{2,1,0:T(8,128)(2,1)S(1)}, u32[]{:S(2)}, u32[]{:S(2)}) collective-permute-start(bf16[4,16,128]{2,1,0:T(8,128)(2,1)S(1)} %bitcast.131), channel_id=1, source_target_pairs={{0,3},{1,2},{2,1},{3,0},{4,7},{5,6},{6,5},{7,4},{8,11},{9,10},{10,... | collective-permute-start | bytes 49160 | tf_op jit(solution)/shard_map/ppermute | solution.py:28
  91.0 1.4 %collective-permute-start.11 = (f32[144,128]{1,0:T(8,128)S(1)}, f32[144,128]{1,0:T(8,128)S(1)}, u32[]{:S(2)}, u32[]{:S(2)}) collective-permute-start(f32[144,128]{1,0:T(8,128)S(1)} %pad_maximum_fusion.4), channel_id=1, source_target_pairs={{0,4},{4,0},{1,5},{5,1},{2,6},{6,2},{3,7},{7,3},{8,12},{12,8},{9,1... | collective-permute-start | bytes 221192 | tf_op jit(solution)/shard_map/ppermute | solution.py:28
  93.3 14.2 %all-to-all-start.4 = ((bf16[16,24,512]{2,1,0:T(8,128)(2,1)}), bf16[16,24,512]{2,1,0:T(8,128)(2,1)S(1)}, u32[]{:S(2)}, u32[]{:S(2)}) async-start(bf16[16,24,512]{2,1,0:T(8,128)(2,1)} %pad_maximum_fusion), calls=%async_computation.4 | async-start | bytes 786432 | tf_op jit(solution)/shard_map/all_to_all | solution.py:156
  96.9 7.9 %collective-permute-start.12 = (f32[64,128]{1,0:T(8,128)S(1)}, f32[64,128]{1,0:T(8,128)S(1)}, u32[]{:S(2)}, u32[]{:S(2)}) collective-permute-start(f32[64,128]{1,0:T(8,128)S(1)} %slice_select_fusion), channel_id=1, source_target_pairs={{0,8},{8,0},{1,9},{9,1},{2,10},{10,2},{3,11},{11,3},{4,12},{12,4},... | collective-permute-start | bytes 98312 | tf_op jit(solution)/shard_map/ppermute | solution.py:28
  107.6 7.8 %collective-permute-start.16 = (f32[16,128]{1,0:T(8,128)S(1)}, f32[16,128]{1,0:T(8,128)S(1)}, u32[]{:S(2)}, u32[]{:S(2)}) collective-permute-start(f32[16,128]{1,0:T(8,128)S(1)} %pad_maximum_fusion.12), channel_id=1, source_target_pairs={{0,8},{8,0},{1,9},{9,1},{2,10},{10,2},{3,11},{11,3},{4,12},{12,4},... | collective-permute-start | bytes 24584 | tf_op jit(solution)/shard_map/ppermute | solution.py:28
  109.0 7.0 %collective-permute-start.15 = (f32[32,128]{1,0:T(8,128)S(1)}, f32[32,128]{1,0:T(8,128)S(1)}, u32[]{:S(2)}, u32[]{:S(2)}) collective-permute-start(f32[32,128]{1,0:T(8,128)S(1)} %get-tuple-element.61), channel_id=1, source_target_pairs={{0,3},{1,2},{2,1},{3,0},{4,7},{5,6},{6,5},{7,4},{8,11},{9,10},{10,... | collective-permute-start | bytes 49160 | tf_op jit(solution)/shard_map/ppermute | solution.py:28
  109.5 6.5 %collective-permute-start.13 = (f32[32,128]{1,0:T(8,128)S(1)}, f32[32,128]{1,0:T(8,128)S(1)}, u32[]{:S(2)}, u32[]{:S(2)}) collective-permute-start(f32[32,128]{1,0:T(8,128)S(1)} %get-tuple-element.62), channel_id=1, source_target_pairs={{0,1},{1,0},{2,3},{3,2},{4,5},{5,4},{6,7},{7,6},{8,9},{9,8},{10,11... | collective-permute-start | bytes 49160 | tf_op jit(solution)/shard_map/ppermute | solution.py:28
  113.1 4.6 %collective-permute-start.14 = (f32[32,128]{1,0:T(8,128)S(1)}, f32[32,128]{1,0:T(8,128)S(1)}, u32[]{:S(2)}, u32[]{:S(2)}) collective-permute-start(f32[32,128]{1,0:T(8,128)S(1)} %get-tuple-element.63), channel_id=1, source_target_pairs={{0,2},{1,3},{2,0},{3,1},{4,6},{5,7},{6,4},{7,5},{8,10},{9,11},{10,... | collective-permute-start | bytes 49160 | tf_op jit(solution)/shard_map/ppermute | solution.py:28

commit v6 on v5

--- a/solution.py
+++ b/solution.py
@@ -143,44 +143,93 @@
     return b16, got[:, 2 * ranks :]
 
 
-def second_slots(part, ni, extra):
-    ranks = part.shape[0] // ni
-    half = part.shape[1] // 2
-    cut = part.astype(jnp.bfloat16).reshape(ni, ranks, 2, half)
-    slots = [cut[:, :, 0], cut[:, :, 1]]
-    slots += [jnp.broadcast_to(x, (ni,) + x.shape) for x in extra]
-    return jnp.concatenate(slots, axis=1)
-
-
 def sum_second(slots, ranks):
     got = lax.all_to_all(slots, "ia", 0, 0)
     total = jnp.sum(got[:, : 2 * ranks].astype(jnp.float32), axis=0)
     return jnp.concatenate([total[:ranks], total[ranks:]], axis=1), got[:, 2 * ranks :]
 
 
-def make_slope(readings, a16, b16, c16):
-    af = a16.astype(jnp.float32)
-    cf = c16.astype(jnp.float32)
-    scaled = (af[None, :, :] * cf[:, None, :]).astype(jnp.bfloat16)
-    model = lax.dot_general(
-        scaled, b16, (((2,), (0,)), ((), ())), preferred_element_type=jnp.float32
-    )
-    slope = ((model - readings.astype(jnp.float32)) / (model * model)).astype(jnp.bfloat16)
-    part_second = lax.dot_general(
-        scaled, slope, (((0, 1), (0, 1)), ((), ())), preferred_element_type=jnp.float32
-    )
-    return slope, part_second
-
-
-def make_cross(slope, a16, b16, c16):
-    af = a16.astype(jnp.float32)
-    cf = c16.astype(jnp.float32)
-    cross = lax.dot_general(
-        slope, b16, (((2,), (1,)), ((), ())), preferred_element_type=jnp.float32
-    )
-    part_first = jnp.sum(cross * cf[:, None, :], axis=0)
-    part_time = jnp.sum(cross * af[None, :, :], axis=1)
-    return part_first, jnp.pad(part_time, ((0, 16 - part_time.shape[0]), (0, 0)))
+def step_kernel(readings, a16, b16, times, part_first, slots, part_time, total):
+    block = readings.shape[0]
+    now = pl.program_id(0)
+    af = a16[...].astype(jnp.float32)
+    bf = b16[...]
+
+    @pl.when(now == 0)
+    def _():
+        total[...] = jnp.zeros_like(total)
+        part_first[...] = jnp.zeros_like(part_first)
+        part_time[...] = jnp.zeros_like(part_time)
+
+    row = lax.broadcasted_iota(jnp.int32, part_time.shape, 0)
+    first, time = part_first[...], part_time[...]
+    all_scaled, all_slope = [], []
+    for t in range(block):
+        cf = times[now * block + t]
+        scaled = (af * cf).astype(jnp.bfloat16)
+        model = jnp.dot(scaled, bf, preferred_element_type=jnp.float32)
+        inverse = 1.0 / model
+        slope = inverse * (1.0 - readings[t].astype(jnp.float32) * inverse)
+        slope = slope.astype(jnp.bfloat16)
+        cross = lax.dot_general(
+            slope, bf, (((1,), (1,)), ((), ())), preferred_element_type=jnp.float32
+        )
+        first = first + cross * cf
+        line = jnp.sum(cross * af, axis=0, keepdims=True)
+        time = time + jnp.where(row == now * block + t, line, 0.0)
+        all_scaled.append(scaled)
+        all_slope.append(slope)
+    part_first[...] = first
+    part_time[...] = time
+    total[...] += lax.dot_general(
+        jnp.concatenate(all_scaled, axis=0),
+        jnp.concatenate(all_slope, axis=0),
+        (((0,), (0,)), ((), ())),
+        preferred_element_type=jnp.float32,
+    )
+
+    @pl.when(now == pl.num_programs(0) - 1)
+    def _():
+        count = slots.shape[0]
+        ranks = total.shape[0] // count
+        half = total.shape[1] // 2
+        for p in range(count):
+            rows = total[p * ranks : (p + 1) * ranks, :]
+            flat = jnp.concatenate([rows[:, :half], rows[:, half:]], axis=0)
+            slots[p] = flat.astype(slots.dtype)
+
+
+def step_parts(readings, a16, b16, c16, ni):
+    times, rows, cols = readings.shape
+    rank = a16.shape[1]
+    block = 4
+    return pl.pallas_call(
+        step_kernel,
+        grid=(times // block,),
+        in_specs=[
+            pl.BlockSpec((block, rows, cols), lambda k: (k, 0, 0)),
+            pl.BlockSpec((rows, rank), lambda k: (0, 0)),
+            pl.BlockSpec((rank, cols), lambda k: (0, 0)),
+            pl.BlockSpec((times, 1, rank), lambda k: (0, 0, 0)),
+        ],
+        out_specs=[
+            pl.BlockSpec((rows, rank), lambda k: (0, 0)),
+            pl.BlockSpec((ni, 2 * rank // ni, cols // 2), lambda k: (0, 0, 0)),
+            pl.BlockSpec((16, rank), lambda k: (0, 0)),
+        ],
+        out_shape=[
+            jax.ShapeDtypeStruct((rows, rank), jnp.float32),
+            jax.ShapeDtypeStruct((ni, 2 * rank // ni, cols // 2), jnp.bfloat16),
+            jax.ShapeDtypeStruct((16, rank), jnp.float32),
+        ],
+        scratch_shapes=[pltpu.VMEM((rank, cols), jnp.float32)],
+        compiler_params=pltpu.CompilerParams(vmem_limit_bytes=50 * 2**20),
+        cost_estimate=pl.CostEstimate(
+            flops=6 * times * rows * cols * rank,
+            bytes_accessed=2 * times * rows * cols,
+            transcendentals=times * rows * cols,
+        ),
+    )(readings, a16, b16, c16.astype(jnp.float32)[:, None, :])
 
 
 def body(
@@ -229,9 +278,8 @@
     low, up = pick(high, a16, swap(a16, "zh", 1))
     a16 = jnp.concatenate([low, up], axis=0)
     c16 = factor_time.astype(jnp.bfloat16)
-    slope, part_second = make_slope(readings, a16, b16, c16)
-    part_first, part_time = make_cross(slope, a16, b16, c16)
-    second, _ = sum_second(second_slots(part_second, ni, []), ranks)
+    part_first, slots, part_time = step_parts(readings, a16, b16, c16, ni)
+    second, _ = sum_second(slots, ranks)
     part, [part_time] = core_half(part_first, [part_time])
     sent = jnp.concatenate([part, part_time, own_first], axis=0)
     came = swap(sent, "zh", 1)
@@ -266,12 +314,11 @@
         factor_time, time_sum * scale_time, mean_time, square_time, count
     )
     c16 = factor_time.astype(jnp.bfloat16)
-    slope, part_second = make_slope(readings, a16, b16, c16)
-    part_first, part_time = make_cross(slope, a16, b16, c16)
+    part_first, slots, part_time = step_parts(readings, a16, b16, c16, ni)
     part, [part_time] = core_half(part_first, [part_time])
-    second, came = sum_second(
-        second_slots(part_second, ni, bf16_pair(fold(part_time, ranks // 2))), ranks
-    )
+    line = jnp.concatenate(bf16_pair(fold(part_time, ranks // 2)), axis=0)
+    line = jnp.broadcast_to(line, (ni,) + line.shape)
+    second, came = sum_second(jnp.concatenate([slots, line], axis=1), ranks)
     keep, send = pick(high, part[: 4 * rows], part[4 * rows :])
     part = keep + swap(send, "zh", 1)
     time_sum = time_of(came, rank)

time: 120 us -> 117 us (0.975)
  matrix products: 15.6 us -> 0 us
  Pallas kernels: 1.45 us -> 14.9 us
    dot_general x6 -> x0, matrix products: 15.6 us -> none  [the longest x2 9.68 us: make_slope(): lax.dot_general(scaled, b16, (((2,), (0,)), ((), ())), preferred_element_...]
    pallas_call x0 -> x2, Pallas kernels: none -> 13.4 us  [step_parts(): pl.pallas_call(step_kernel, grid=(times // block,), in_specs=[pl.BlockSpe...]
  transfers between devices with their start and end apart: 21 -> 21, of which waited for: 16 -> 16; matrix products, arithmetic and copies ran while one was open for 3% -> 2% of each run, Pallas kernels for 0% -> 0%
where the time goes in v6:
time: 117 us; the launch traced here: 116 us
  starting transfers between devices  43.8 us (37%)
  waiting for transfers between devices  39 us (33%)
  Pallas kernels  14.9 us (13%)
  blocking collectives  11.2 us (10%)
  other arithmetic  4 us (3%)
  local copies, waits for them, and re-layouts  1.83 us (2%)
  between operations  1.36 us (1%)
    ppermute x17, starting transfers between devices, swap(): return lax.ppermute(x, axis, [(i, i ^ k) for i in range(n)])  25.1 us
    ppermute x17, waiting for transfers between devices, swap(): return lax.ppermute(x, axis, [(i, i ^ k) for i in range(n)])  22.5 us
    pallas_call x2, Pallas kernels, step_parts(): pl.pallas_call(step_kernel, grid=(times // block,), in_specs=[pl.BlockSpe...  13.4 us
    all_to_all x1, blocking collectives, body(): got = lax.all_to_all(slots, 'ta', 0, 0)  11.2 us
    all_to_all x2, starting transfers between devices, spread_second(): got = lax.all_to_all(slots, 'ia', 0, 0)  10.6 us
    all_to_all x2, waiting for transfers between devices, sum_second(): got = lax.all_to_all(slots, 'ia', 0, 0)  9.38 us
    all_to_all x2, starting transfers between devices, sum_second(): got = lax.all_to_all(slots, 'ia', 0, 0)  8.08 us
    all_to_all x2, waiting for transfers between devices, spread_second(): got = lax.all_to_all(slots, 'ia', 0, 0)  7.14 us
  transfers between devices with their start and end apart: 21, of which 16 were waited for; matrix products, arithmetic and copies ran while one was open for 2% of the time, Pallas kernels for 0%

profile of v6, /device:TPU:32, one launch (start us, length us, event | category | flops | bytes accessed | tf_op | source)
XLA Modules:
  0.0 116.0 jit_solution(13204747338645933240)
XLA Ops:
  0.6 1.5 %shard_map.169 = (f32[4,64,128]{2,1,0:T(8,128)}, f32[48,128]{1,0:T(8,128)}) custom-call(f32[16,128]{1,0:T(8,128)} %f0.1, f32[16,128]{1,0:T(8,128)} %f1.1, f32[16,128]{1,0:T(8,128)} %f2.1, f32[8,256]{1,0:T(8,128)} %s0.1, f32[8,256]{1,0:T(8,128)} %s1_.1, f32[8,256]{1,0:T(8,128)} %s2_.1), custom_call_target="tpu_custom_call" | custom-call | tf_op jit(solution)/shard_map/pallas_call | solution.py:70
  2.1 11.2 %all_to_all.25 = f32[4,64,128]{2,1,0:T(8,128)S(1)} all-to-all(f32[4,64,128]{2,1,0:T(8,128)} %get-tuple-element.19), channel_id=1, replica_groups=mesh['ia'=16,'zh'=2,'co'=2,'ta'=4] {'ta'}, dimensions={0} | all-to-all | bytes 262144 | tf_op jit(solution)/shard_map/all_to_all | solution.py:267
  14.1 7.0 %all-to-all-start.1 = ((bf16[16,24,512]{2,1,0:T(8,128)(2,1)}), bf16[16,24,512]{2,1,0:T(8,128)(2,1)S(1)}, u32[]{:S(2)}, u32[]{:S(2)}) async-start(bf16[16,24,512]{2,1,0:T(8,128)(2,1)} %broadcast_in_dim.22), calls=%async_computation.1 | async-start | bytes 786432 | tf_op jit(solution)/shard_map/all_to_all | solution.py:135
  21.2 4.7 %collective-permute-start.1 = (bf16[128,128]{1,0:T(8,128)(2,1)S(1)}, bf16[128,128]{1,0:T(8,128)(2,1)S(1)}, u32[]{:S(2)}, u32[]{:S(2)}) collective-permute-start(bf16[128,128]{1,0:T(8,128)(2,1)S(1)} %bitcast.87), channel_id=1, source_target_pairs={{0,8},{8,0},{1,9},{9,1},{2,10},{10,2},{3,11},{11,3},{4,12},{12,4},... | collective-permute-start | bytes 98312 | tf_op jit(solution)/shard_map/ppermute | solution.py:28
  26.6 2.9 %collective-permute-done.1 = bf16[128,128]{1,0:T(8,128)(2,1)S(1)} collective-permute-done((bf16[128,128]{1,0:T(8,128)(2,1)S(1)}, bf16[128,128]{1,0:T(8,128)(2,1)S(1)}, u32[]{:S(2)}, u32[]{:S(2)}) %collective-permute-start.1) | collective-permute-done | bytes 32800 | tf_op jit(solution)/shard_map/ppermute | solution.py:28
  29.5 2.4 %all-to-all-done.1 = bf16[16,24,512]{2,1,0:T(8,128)(2,1)S(1)} async-done(((bf16[16,24,512]{2,1,0:T(8,128)(2,1)}), bf16[16,24,512]{2,1,0:T(8,128)(2,1)S(1)}, u32[]{:S(2)}, u32[]{:S(2)}) %all-to-all-start.1) | async-done | bytes 393248 | tf_op jit(solution)/shard_map/all_to_all | solution.py:135
  32.0 7.1 %shard_map.170 = (f32[256,128]{1,0:T(8,128)S(1)}, bf16[16,16,512]{2,1,0:T(8,128)(2,1)}, f32[16,128]{1,0:T(8,128)S(1)}) custom-call(bf16[12,256,1024]{2,1,0:T(8,128)(2,1)} %readings.3, bf16[256,128]{1,0:T(8,128)(2,1)S(1)} %pad_maximum_fusion.6.a16, bf16[128,1024]{1,0:T(8,128)(2,1)S(1)} %pad_maximum_fusion.1.b16, f32[12,1,128]{2,1,0:T(1,128)S(1)} %reshape.80.times), custom_call_target="tpu_custom_call" | custom-call | flops 2415919104 | bytes 6291456 | tf_op jit(solution)/shard_map/pallas_call | solution.py:206
  39.2 1.3 %collective-permute-done.2 = f32[144,128]{1,0:T(8,128)S(1)} collective-permute-done((f32[144,128]{1,0:T(8,128)S(1)}, f32[144,128]{1,0:T(8,128)S(1)}, u32[]{:S(2)}, u32[]{:S(2)}) %collective-permute-start.2) | collective-permute-done | bytes 73760 | tf_op jit(solution)/shard_map/ppermute | solution.py:28
  40.5 4.7 %collective-permute-start.3 = (f32[192,128]{1,0:T(8,128)S(1)}, f32[192,128]{1,0:T(8,128)S(1)}, u32[]{:S(2)}, u32[]{:S(2)}) collective-permute-start(f32[192,128]{1,0:T(8,128)S(1)} %pad_maximum_fusion.3), channel_id=1, source_target_pairs={{0,8},{8,0},{1,9},{9,1},{2,10},{10,2},{3,11},{11,3},{4,12},{12,4},... | collective-permute-start | bytes 294920 | tf_op jit(solution)/shard_map/ppermute | solution.py:28
  45.2 4.5 %all-to-all-start.2 = ((bf16[16,16,512]{2,1,0:T(8,128)(2,1)}), bf16[16,16,512]{2,1,0:T(8,128)(2,1)S(1)}, u32[]{:S(2)}, u32[]{:S(2)}) async-start(bf16[16,16,512]{2,1,0:T(8,128)(2,1)} %get-tuple-element.25), calls=%async_computation.2 | async-start | bytes 524288 | tf_op jit(solution)/shard_map/all_to_all | solution.py:147
  49.7 1.7 %collective-permute-done.3 = f32[192,128]{1,0:T(8,128)S(1)} collective-permute-done((f32[192,128]{1,0:T(8,128)S(1)}, f32[192,128]{1,0:T(8,128)S(1)}, u32[]{:S(2)}, u32[]{:S(2)}) %collective-permute-start.3) | collective-permute-done | bytes 98336 | tf_op jit(solution)/shard_map/ppermute | solution.py:28
  51.6 6.9 %all-to-all-done.2 = bf16[16,16,512]{2,1,0:T(8,128)(2,1)S(1)} async-done(((bf16[16,16,512]{2,1,0:T(8,128)(2,1)}), bf16[16,16,512]{2,1,0:T(8,128)(2,1)S(1)}, u32[]{:S(2)}, u32[]{:S(2)}) %all-to-all-start.2) | async-done | bytes 262176 | tf_op jit(solution)/shard_map/all_to_all | solution.py:147
  58.7 1.5 %collective-permute-start.5 = (f32[96,128]{1,0:T(8,128)S(1)}, f32[96,128]{1,0:T(8,128)S(1)}, u32[]{:S(2)}, u32[]{:S(2)}) collective-permute-start(f32[96,128]{1,0:T(8,128)S(1)} %constant_dynamic-update-slice_fusion.18), channel_id=1, source_target_pairs={{0,2},{1,3},{2,0},{3,1},{4,6},{5,7},{6,4},{7,5},{8,10},{9,11},{10,... | collective-permute-start | bytes 147464 | tf_op jit(solution)/shard_map/ppermute | solution.py:28
  60.3 1.0 collective-permute-start.6
  61.2 2.0 %collective-permute-start.4 = (f32[96,128]{1,0:T(8,128)S(1)}, f32[96,128]{1,0:T(8,128)S(1)}, u32[]{:S(2)}, u32[]{:S(2)}) collective-permute-start(f32[96,128]{1,0:T(8,128)S(1)} %get-tuple-element.84), channel_id=1, source_target_pairs={{0,1},{1,0},{2,3},{3,2},{4,5},{5,4},{6,7},{7,6},{8,9},{9,8},{10,11... | collective-permute-start | bytes 147464 | tf_op jit(solution)/shard_map/ppermute | solution.py:28
  64.4 1.4 %collective-permute-done.4 = f32[96,128]{1,0:T(8,128)S(1)} collective-permute-done((f32[96,128]{1,0:T(8,128)S(1)}, f32[96,128]{1,0:T(8,128)S(1)}, u32[]{:S(2)}, u32[]{:S(2)}) %collective-permute-start.4) | collective-permute-done | bytes 49184 | tf_op jit(solution)/shard_map/ppermute | solution.py:28
  66.8 3.6 %all-to-all-start.3 = ((bf16[16,24,512]{2,1,0:T(8,128)(2,1)}), bf16[16,24,512]{2,1,0:T(8,128)(2,1)S(1)}, u32[]{:S(2)}, u32[]{:S(2)}) async-start(bf16[16,24,512]{2,1,0:T(8,128)(2,1)} %broadcast_in_dim.26), calls=%async_computation.3 | async-start | bytes 786432 | tf_op jit(solution)/shard_map/all_to_all | solution.py:135
  70.4 1.6 %collective-permute-start.10 = (bf16[4,16,128]{2,1,0:T(8,128)(2,1)S(1)}, bf16[4,16,128]{2,1,0:T(8,128)(2,1)S(1)}, u32[]{:S(2)}, u32[]{:S(2)}) collective-permute-start(bf16[4,16,128]{2,1,0:T(8,128)(2,1)S(1)} %bitcast.91), channel_id=1, source_target_pairs={{0,1},{1,0},{2,3},{3,2},{4,5},{5,4},{6,7},{7,6},{8,9},{9,8},{10,11... | collective-permute-start | bytes 49160 | tf_op jit(solution)/shard_map/ppermute | solution.py:28
  72.6 1.4 %collective-permute-start.8 = (bf16[4,16,128]{2,1,0:T(8,128)(2,1)S(1)}, bf16[4,16,128]{2,1,0:T(8,128)(2,1)S(1)}, u32[]{:S(2)}, u32[]{:S(2)}) collective-permute-start(bf16[4,16,128]{2,1,0:T(8,128)(2,1)S(1)} %bitcast.93), channel_id=1, source_target_pairs={{0,3},{1,2},{2,1},{3,0},{4,7},{5,6},{6,5},{7,4},{8,11},{9,10},{10,... | collective-permute-start | bytes 49160 | tf_op jit(solution)/shard_map/ppermute | solution.py:28
  74.2 2.4 %collective-permute-done.9 = bf16[4,16,128]{2,1,0:T(8,128)(2,1)S(1)} collective-permute-done((bf16[4,16,128]{2,1,0:T(8,128)(2,1)S(1)}, bf16[4,16,128]{2,1,0:T(8,128)(2,1)S(1)}, u32[]{:S(2)}, u32[]{:S(2)}) %collective-permute-start.9) | collective-permute-done | bytes 16416 | tf_op jit(solution)/shard_map/ppermute | solution.py:28
  76.7 4.7 %all-to-all-done.3 = bf16[16,24,512]{2,1,0:T(8,128)(2,1)S(1)} async-done(((bf16[16,24,512]{2,1,0:T(8,128)(2,1)}), bf16[16,24,512]{2,1,0:T(8,128)(2,1)S(1)}, u32[]{:S(2)}, u32[]{:S(2)}) %all-to-all-start.3) | async-done | bytes 393248 | tf_op jit(solution)/shard_map/all_to_all | solution.py:135
  81.6 6.4 %shard_map.171 = (f32[256,128]{1,0:T(8,128)S(1)}, bf16[16,16,512]{2,1,0:T(8,128)(2,1)S(1)}, f32[16,128]{1,0:T(8,128)S(1)}) custom-call(bf16[12,256,1024]{2,1,0:T(8,128)(2,1)} %readings.3, bf16[256,128]{1,0:T(8,128)(2,1)S(1)} %bitcast.80, bf16[128,1024]{1,0:T(8,128)(2,1)S(1)} %pad_maximum_fusion.2.b16, f32[12,1,128]{2,1,0:T(1,128)S(1)} %reshape.81.times), custom_call_target="tpu_custom_call" | custom-call | flops 2415919104 | bytes 6291456 | tf_op jit(solution)/shard_map/pallas_call | solution.py:206
  88.1 1.2 %collective-permute-done.11 = f32[144,128]{1,0:T(8,128)S(1)} collective-permute-done((f32[144,128]{1,0:T(8,128)S(1)}, f32[144,128]{1,0:T(8,128)S(1)}, u32[]{:S(2)}, u32[]{:S(2)}) %collective-permute-start.11) | collective-permute-done | bytes 73760 | tf_op jit(solution)/shard_map/ppermute | solution.py:28
  89.4 0.8 pad_maximum_fusion
  90.2 3.6 %all-to-all-start.4 = ((bf16[16,24,512]{2,1,0:T(8,128)(2,1)}), bf16[16,24,512]{2,1,0:T(8,128)(2,1)S(1)}, u32[]{:S(2)}, u32[]{:S(2)}) async-start(bf16[16,24,512]{2,1,0:T(8,128)(2,1)} %pad_maximum_fusion), calls=%async_computation.4 | async-start | bytes 786432 | tf_op jit(solution)/shard_map/all_to_all | solution.py:147
  93.8 1.6 %collective-permute-start.12 = (f32[64,128]{1,0:T(8,128)S(1)}, f32[64,128]{1,0:T(8,128)S(1)}, u32[]{:S(2)}, u32[]{:S(2)}) collective-permute-start(f32[64,128]{1,0:T(8,128)S(1)} %slice_select_fusion), channel_id=1, source_target_pairs={{0,8},{8,0},{1,9},{9,1},{2,10},{10,2},{3,11},{11,3},{4,12},{12,4},... | collective-permute-start | bytes 98312 | tf_op jit(solution)/shard_map/ppermute | solution.py:28
  95.4 6.5 %collective-permute-done.12 = f32[64,128]{1,0:T(8,128)S(1)} collective-permute-done((f32[64,128]{1,0:T(8,128)S(1)}, f32[64,128]{1,0:T(8,128)S(1)}, u32[]{:S(2)}, u32[]{:S(2)}) %collective-permute-start.12) | collective-permute-done | bytes 32800 | tf_op jit(solution)/shard_map/ppermute | solution.py:28
  101.9 2.5 %all-to-all-done.4 = bf16[16,24,512]{2,1,0:T(8,128)(2,1)S(1)} async-done(((bf16[16,24,512]{2,1,0:T(8,128)(2,1)}), bf16[16,24,512]{2,1,0:T(8,128)(2,1)S(1)}, u32[]{:S(2)}, u32[]{:S(2)}) %all-to-all-start.4) | async-done | bytes 393248 | tf_op jit(solution)/shard_map/all_to_all | solution.py:147
  104.5 1.5 %collective-permute-start.16 = (f32[16,128]{1,0:T(8,128)S(1)}, f32[16,128]{1,0:T(8,128)S(1)}, u32[]{:S(2)}, u32[]{:S(2)}) collective-permute-start(f32[16,128]{1,0:T(8,128)S(1)} %pad_maximum_fusion.16), channel_id=1, source_target_pairs={{0,8},{8,0},{1,9},{9,1},{2,10},{10,2},{3,11},{11,3},{4,12},{12,4},... | collective-permute-start | bytes 24584 | tf_op jit(solution)/shard_map/ppermute | solution.py:28
  106.4 3.7 %collective-permute-start.13 = (f32[32,128]{1,0:T(8,128)S(1)}, f32[32,128]{1,0:T(8,128)S(1)}, u32[]{:S(2)}, u32[]{:S(2)}) collective-permute-start(f32[32,128]{1,0:T(8,128)S(1)} %get-tuple-element.66), channel_id=1, source_target_pairs={{0,1},{1,0},{2,3},{3,2},{4,5},{5,4},{6,7},{7,6},{8,9},{9,8},{10,11... | collective-permute-start | bytes 49160 | tf_op jit(solution)/shard_map/ppermute | solution.py:28
  110.5 1.8 %collective-permute-done.16 = f32[16,128]{1,0:T(8,128)S(1)} collective-permute-done((f32[16,128]{1,0:T(8,128)S(1)}, f32[16,128]{1,0:T(8,128)S(1)}, u32[]{:S(2)}, u32[]{:S(2)}) %collective-permute-start.16) | collective-permute-done | bytes 8224 | tf_op jit(solution)/shard_map/ppermute | solution.py:28
  112.9 1.8 %collective-permute-done.14 = f32[32,128]{1,0:T(8,128)S(1)} collective-permute-done((f32[32,128]{1,0:T(8,128)S(1)}, f32[32,128]{1,0:T(8,128)S(1)}, u32[]{:S(2)}, u32[]{:S(2)}) %collective-permute-start.14) | collective-permute-done | bytes 16416 | tf_op jit(solution)/shard_map/ppermute | solution.py:28
  (121 shorter events, 8.0 us)
Async XLA Ops:
  13.3 27.2 %copy-start = (f32[48,128]{1,0:T(8,128)S(1)}, f32[48,128]{1,0:T(8,128)}, u32[]{:S(2)}) copy-start(f32[48,128]{1,0:T(8,128)} %get-tuple-element.24) | copy-start | bytes 73732
  14.1 7.0 %collective-permute-start = (bf16[1,64,128]{2,1,0:T(8,128)(2,1)S(1)}, bf16[1,64,128]{2,1,0:T(8,128)(2,1)S(1)}, u32[]{:S(2)}, u32[]{:S(2)}) collective-permute-start(bf16[1,64,128]{2,1,0:T(8,128)(2,1)S(1)} %bitcast.89), channel_id=1, source_target_pairs={{0,4},{4,0},{1,5},{5,1},{2,6},{6,2},{3,7},{7,3},{8,12},{12,8},{9,1... | collective-permute-start | bytes 49160 | tf_op jit(solution)/shard_map/ppermute | solution.py:28
  14.1 17.8 %all-to-all-start.1 = ((bf16[16,24,512]{2,1,0:T(8,128)(2,1)}), bf16[16,24,512]{2,1,0:T(8,128)(2,1)S(1)}, u32[]{:S(2)}, u32[]{:S(2)}) async-start(bf16[16,24,512]{2,1,0:T(8,128)(2,1)} %broadcast_in_dim.22), calls=%async_computation.1 | async-start | bytes 786432 | tf_op jit(solution)/shard_map/all_to_all | solution.py:135
  21.2 8.3 %collective-permute-start.1 = (bf16[128,128]{1,0:T(8,128)(2,1)S(1)}, bf16[128,128]{1,0:T(8,128)(2,1)S(1)}, u32[]{:S(2)}, u32[]{:S(2)}) collective-permute-start(bf16[128,128]{1,0:T(8,128)(2,1)S(1)} %bitcast.87), channel_id=1, source_target_pairs={{0,8},{8,0},{1,9},{9,1},{2,10},{10,2},{3,11},{11,3},{4,12},{12,4},... | collective-permute-start | bytes 98312 | tf_op jit(solution)/shard_map/ppermute | solution.py:28
  32.0 49.5 %copy-start.1 = (f32[12,128]{1,0:T(8,128)S(1)}, f32[12,128]{1,0:T(8,128)}, u32[]{:S(2)}) copy-start(f32[12,128]{1,0:T(8,128)} %param.19) | copy-start | bytes 18436
  32.0 49.5 %copy-start.2 = (f32[12,128]{1,0:T(8,128)S(1)}, f32[12,128]{1,0:T(8,128)}, u32[]{:S(2)}) copy-start(f32[12,128]{1,0:T(8,128)} %param.18) | copy-start | bytes 18436
  32.0 49.5 %copy-start.3 = (f32[12,128]{1,0:T(8,128)S(1)}, f32[12,128]{1,0:T(8,128)}, u32[]{:S(2)}) copy-start(f32[12,128]{1,0:T(8,128)} %param.13) | copy-start | bytes 18436
  39.1 1.4 %collective-permute-start.2 = (f32[144,128]{1,0:T(8,128)S(1)}, f32[144,128]{1,0:T(8,128)S(1)}, u32[]{:S(2)}, u32[]{:S(2)}) collective-permute-start(f32[144,128]{1,0:T(8,128)S(1)} %pad_maximum_fusion.4), channel_id=1, source_target_pairs={{0,4},{4,0},{1,5},{5,1},{2,6},{6,2},{3,7},{7,3},{8,12},{12,8},{9,1... | collective-permute-start | bytes 221192 | tf_op jit(solution)/shard_map/ppermute | solution.py:28
  40.5 11.0 %collective-permute-start.3 = (f32[192,128]{1,0:T(8,128)S(1)}, f32[192,128]{1,0:T(8,128)S(1)}, u32[]{:S(2)}, u32[]{:S(2)}) collective-permute-start(f32[192,128]{1,0:T(8,128)S(1)} %pad_maximum_fusion.3), channel_id=1, source_target_pairs={{0,8},{8,0},{1,9},{9,1},{2,10},{10,2},{3,11},{11,3},{4,12},{12,4},... | collective-permute-start | bytes 294920 | tf_op jit(solution)/shard_map/ppermute | solution.py:28
  45.2 13.3 %all-to-all-start.2 = ((bf16[16,16,512]{2,1,0:T(8,128)(2,1)}), bf16[16,16,512]{2,1,0:T(8,128)(2,1)S(1)}, u32[]{:S(2)}, u32[]{:S(2)}) async-start(bf16[16,16,512]{2,1,0:T(8,128)(2,1)} %get-tuple-element.25), calls=%async_computation.2 | async-start | bytes 524288 | tf_op jit(solution)/shard_map/all_to_all | solution.py:147
  58.7 5.1 %collective-permute-start.5 = (f32[96,128]{1,0:T(8,128)S(1)}, f32[96,128]{1,0:T(8,128)S(1)}, u32[]{:S(2)}, u32[]{:S(2)}) collective-permute-start(f32[96,128]{1,0:T(8,128)S(1)} %constant_dynamic-update-slice_fusion.18), channel_id=1, source_target_pairs={{0,2},{1,3},{2,0},{3,1},{4,6},{5,7},{6,4},{7,5},{8,10},{9,11},{10,... | collective-permute-start | bytes 147464 | tf_op jit(solution)/shard_map/ppermute | solution.py:28
  60.3 4.1 %collective-permute-start.6 = (f32[96,128]{1,0:T(8,128)S(1)}, f32[96,128]{1,0:T(8,128)S(1)}, u32[]{:S(2)}, u32[]{:S(2)}) collective-permute-start(f32[96,128]{1,0:T(8,128)S(1)} %get-tuple-element.102), channel_id=1, source_target_pairs={{0,3},{1,2},{2,1},{3,0},{4,7},{5,6},{6,5},{7,4},{8,11},{9,10},{10,... | collective-permute-start | bytes 147464 | tf_op jit(solution)/shard_map/ppermute | solution.py:28
  61.2 4.6 %collective-permute-start.4 = (f32[96,128]{1,0:T(8,128)S(1)}, f32[96,128]{1,0:T(8,128)S(1)}, u32[]{:S(2)}, u32[]{:S(2)}) collective-permute-start(f32[96,128]{1,0:T(8,128)S(1)} %get-tuple-element.84), channel_id=1, source_target_pairs={{0,1},{1,0},{2,3},{3,2},{4,5},{5,4},{6,7},{7,6},{8,9},{9,8},{10,11... | collective-permute-start | bytes 147464 | tf_op jit(solution)/shard_map/ppermute | solution.py:28
  65.9 4.5 %collective-permute-start.7 = (bf16[2,16,128]{2,1,0:T(8,128)(2,1)S(1)}, bf16[2,16,128]{2,1,0:T(8,128)(2,1)S(1)}, u32[]{:S(2)}, u32[]{:S(2)}) collective-permute-start(bf16[2,16,128]{2,1,0:T(8,128)(2,1)S(1)} %bitcast.94), channel_id=1, source_target_pairs={{0,4},{4,0},{1,5},{5,1},{2,6},{6,2},{3,7},{7,3},{8,12},{12,8},{9,1... | collective-permute-start | bytes 24584 | tf_op jit(solution)/shard_map/ppermute | solution.py:28
  66.8 14.6 %all-to-all-start.3 = ((bf16[16,24,512]{2,1,0:T(8,128)(2,1)}), bf16[16,24,512]{2,1,0:T(8,128)(2,1)S(1)}, u32[]{:S(2)}, u32[]{:S(2)}) async-start(bf16[16,24,512]{2,1,0:T(8,128)(2,1)} %broadcast_in_dim.26), calls=%async_computation.3 | async-start | bytes 786432 | tf_op jit(solution)/shard_map/all_to_all | solution.py:135
  70.4 3.8 %collective-permute-start.10 = (bf16[4,16,128]{2,1,0:T(8,128)(2,1)S(1)}, bf16[4,16,128]{2,1,0:T(8,128)(2,1)S(1)}, u32[]{:S(2)}, u32[]{:S(2)}) collective-permute-start(bf16[4,16,128]{2,1,0:T(8,128)(2,1)S(1)} %bitcast.91), channel_id=1, source_target_pairs={{0,1},{1,0},{2,3},{3,2},{4,5},{5,4},{6,7},{7,6},{8,9},{9,8},{10,11... | collective-permute-start | bytes 49160 | tf_op jit(solution)/shard_map/ppermute | solution.py:28
  72.0 4.6 %collective-permute-start.9 = (bf16[4,16,128]{2,1,0:T(8,128)(2,1)S(1)}, bf16[4,16,128]{2,1,0:T(8,128)(2,1)S(1)}, u32[]{:S(2)}, u32[]{:S(2)}) collective-permute-start(bf16[4,16,128]{2,1,0:T(8,128)(2,1)S(1)} %bitcast.92), channel_id=1, source_target_pairs={{0,2},{1,3},{2,0},{3,1},{4,6},{5,7},{6,4},{7,5},{8,10},{9,11},{10,... | collective-permute-start | bytes 49160 | tf_op jit(solution)/shard_map/ppermute | solution.py:28
  72.6 4.1 %collective-permute-start.8 = (bf16[4,16,128]{2,1,0:T(8,128)(2,1)S(1)}, bf16[4,16,128]{2,1,0:T(8,128)(2,1)S(1)}, u32[]{:S(2)}, u32[]{:S(2)}) collective-permute-start(bf16[4,16,128]{2,1,0:T(8,128)(2,1)S(1)} %bitcast.93), channel_id=1, source_target_pairs={{0,3},{1,2},{2,1},{3,0},{4,7},{5,6},{6,5},{7,4},{8,11},{9,10},{10,... | collective-permute-start | bytes 49160 | tf_op jit(solution)/shard_map/ppermute | solution.py:28
  88.0 1.4 %collective-permute-start.11 = (f32[144,128]{1,0:T(8,128)S(1)}, f32[144,128]{1,0:T(8,128)S(1)}, u32[]{:S(2)}, u32[]{:S(2)}) collective-permute-start(f32[144,128]{1,0:T(8,128)S(1)} %pad_maximum_fusion.5), channel_id=1, source_target_pairs={{0,4},{4,0},{1,5},{5,1},{2,6},{6,2},{3,7},{7,3},{8,12},{12,8},{9,1... | collective-permute-start | bytes 221192 | tf_op jit(solution)/shard_map/ppermute | solution.py:28
  90.2 14.2 %all-to-all-start.4 = ((bf16[16,24,512]{2,1,0:T(8,128)(2,1)}), bf16[16,24,512]{2,1,0:T(8,128)(2,1)S(1)}, u32[]{:S(2)}, u32[]{:S(2)}) async-start(bf16[16,24,512]{2,1,0:T(8,128)(2,1)} %pad_maximum_fusion), calls=%async_computation.4 | async-start | bytes 786432 | tf_op jit(solution)/shard_map/all_to_all | solution.py:147
  93.8 8.1 %collective-permute-start.12 = (f32[64,128]{1,0:T(8,128)S(1)}, f32[64,128]{1,0:T(8,128)S(1)}, u32[]{:S(2)}, u32[]{:S(2)}) collective-permute-start(f32[64,128]{1,0:T(8,128)S(1)} %slice_select_fusion), channel_id=1, source_target_pairs={{0,8},{8,0},{1,9},{9,1},{2,10},{10,2},{3,11},{11,3},{4,12},{12,4},... | collective-permute-start | bytes 98312 | tf_op jit(solution)/shard_map/ppermute | solution.py:28
  104.5 7.8 %collective-permute-start.16 = (f32[16,128]{1,0:T(8,128)S(1)}, f32[16,128]{1,0:T(8,128)S(1)}, u32[]{:S(2)}, u32[]{:S(2)}) collective-permute-start(f32[16,128]{1,0:T(8,128)S(1)} %pad_maximum_fusion.16), channel_id=1, source_target_pairs={{0,8},{8,0},{1,9},{9,1},{2,10},{10,2},{3,11},{11,3},{4,12},{12,4},... | collective-permute-start | bytes 24584 | tf_op jit(solution)/shard_map/ppermute | solution.py:28
  106.1 6.8 %collective-permute-start.15 = (f32[32,128]{1,0:T(8,128)S(1)}, f32[32,128]{1,0:T(8,128)S(1)}, u32[]{:S(2)}, u32[]{:S(2)}) collective-permute-start(f32[32,128]{1,0:T(8,128)S(1)} %get-tuple-element.65), channel_id=1, source_target_pairs={{0,3},{1,2},{2,1},{3,0},{4,7},{5,6},{6,5},{7,4},{8,11},{9,10},{10,... | collective-permute-start | bytes 49160 | tf_op jit(solution)/shard_map/ppermute | solution.py:28
  106.4 6.5 %collective-permute-start.13 = (f32[32,128]{1,0:T(8,128)S(1)}, f32[32,128]{1,0:T(8,128)S(1)}, u32[]{:S(2)}, u32[]{:S(2)}) collective-permute-start(f32[32,128]{1,0:T(8,128)S(1)} %get-tuple-element.66), channel_id=1, source_target_pairs={{0,1},{1,0},{2,3},{3,2},{4,5},{5,4},{6,7},{7,6},{8,9},{9,8},{10,11... | collective-permute-start | bytes 49160 | tf_op jit(solution)/shard_map/ppermute | solution.py:28
  110.1 4.6 %collective-permute-start.14 = (f32[32,128]{1,0:T(8,128)S(1)}, f32[32,128]{1,0:T(8,128)S(1)}, u32[]{:S(2)}, u32[]{:S(2)}) collective-permute-start(f32[32,128]{1,0:T(8,128)S(1)} %get-tuple-element.67), channel_id=1, source_target_pairs={{0,2},{1,3},{2,0},{3,1},{4,6},{5,7},{6,4},{7,5},{8,10},{9,11},{10,... | collective-permute-start | bytes 49160 | tf_op jit(solution)/shard_map/ppermute | solution.py:28

commit v7 on v6

--- a/solution.py
+++ b/solution.py
@@ -260,11 +260,11 @@
     high = zh == 1
 
     slots, own_first = pack(
-        nt,
+        1,
         (factor_first, mean_first, square_first),
         (factor_second, mean_second, square_second),
     )
-    got = lax.all_to_all(slots, "ta", 0, 0)
+    got = jnp.stack(gather_ta(slots[0]), axis=0)
     wide_second, wide_mean, wide_square = [
         got[:, n * flat : (n + 1) * flat].reshape(nt * flat, rank) for n in (0, 1, 2)
     ]

time: 117 us -> 115 us (0.983)
  blocking collectives: 11.2 us -> 0 us
  starting transfers between devices: 43.8 us -> 48.9 us
  waiting for transfers between devices: 39 us -> 42.6 us
    all_to_all x1 -> x0, blocking collectives: 11.2 us -> none  [body(): got = lax.all_to_all(slots, 'ta', 0, 0)]
    ppermute x17 -> x20, starting transfers between devices: 25.1 us -> 30.3 us  [swap(): return lax.ppermute(x, axis, [(i, i ^ k) for i in range(n)])]
    all_to_all x2, waiting for transfers between devices: 9.38 us -> 11.3 us  [sum_second(): got = lax.all_to_all(slots, 'ia', 0, 0)]
    ppermute x17 -> x20, waiting for transfers between devices: 22.5 us -> 23.9 us  [swap(): return lax.ppermute(x, axis, [(i, i ^ k) for i in range(n)])]
  transfers between devices with their start and end apart: 21 -> 24, of which waited for: 16 -> 19; matrix products, arithmetic and copies ran while one was open for 2% -> 2% of each run, Pallas kernels for 0% -> 0%
where the time goes in v7:
time: 115 us; the launch traced here: 114 us
  starting transfers between devices  48.9 us (43%)
  waiting for transfers between devices  42.6 us (37%)
  Pallas kernels  14.8 us (13%)
  other arithmetic  4.79 us (4%)
  local copies, waits for them, and re-layouts  1.84 us (2%)
  between operations  1.39 us (1%)
    ppermute x20, starting transfers between devices, swap(): return lax.ppermute(x, axis, [(i, i ^ k) for i in range(n)])  30.3 us
    ppermute x20, waiting for transfers between devices, swap(): return lax.ppermute(x, axis, [(i, i ^ k) for i in range(n)])  23.9 us
    pallas_call x2, Pallas kernels, step_parts(): pl.pallas_call(step_kernel, grid=(times // block,), in_specs=[pl.BlockSpe...  13.4 us
    all_to_all x2, waiting for transfers between devices, sum_second(): got = lax.all_to_all(slots, 'ia', 0, 0)  11.3 us
    all_to_all x2, starting transfers between devices, spread_second(): got = lax.all_to_all(slots, 'ia', 0, 0)  10.6 us
    all_to_all x2, starting transfers between devices, sum_second(): got = lax.all_to_all(slots, 'ia', 0, 0)  8 us
    all_to_all x2, waiting for transfers between devices, spread_second(): got = lax.all_to_all(slots, 'ia', 0, 0)  7.44 us
  transfers between devices with their start and end apart: 24, of which 19 were waited for; matrix products, arithmetic and copies ran while one was open for 2% of the time, Pallas kernels for 0%

profile of v7, /device:TPU:32, one launch (start us, length us, event | category | flops | bytes accessed | tf_op | source)
XLA Modules:
  0.0 114.4 jit_solution(4358611874964685270)
XLA Ops:
  0.6 1.4 %shard_map.169 = (f32[1,64,128]{2,1,0:T(8,128)}, f32[48,128]{1,0:T(8,128)}) custom-call(f32[16,128]{1,0:T(8,128)} %f0.1, f32[16,128]{1,0:T(8,128)} %f1.1, f32[16,128]{1,0:T(8,128)} %f2.1, f32[8,256]{1,0:T(8,128)} %s0.1, f32[8,256]{1,0:T(8,128)} %s1_.1, f32[8,256]{1,0:T(8,128)} %s2_.1), custom_call_target="tpu_custom_call" | custom-call | tf_op jit(solution)/shard_map/pallas_call | solution.py:70
  2.0 1.8 %collective-permute-start.2 = (f32[64,128]{1,0:T(8,128)}, f32[64,128]{1,0:T(8,128)S(1)}, u32[]{:S(2)}, u32[]{:S(2)}) collective-permute-start(f32[64,128]{1,0:T(8,128)} %bitcast.107), channel_id=1, source_target_pairs={{0,1},{1,0},{2,3},{3,2},{4,5},{5,4},{6,7},{7,6},{8,9},{9,8},{10,11... | collective-permute-start | bytes 98312 | tf_op jit(solution)/shard_map/ppermute | solution.py:28
  3.9 1.5 %collective-permute-start.1 = (f32[64,128]{1,0:T(8,128)}, f32[64,128]{1,0:T(8,128)S(1)}, u32[]{:S(2)}, u32[]{:S(2)}) collective-permute-start(f32[64,128]{1,0:T(8,128)} %bitcast.108), channel_id=1, source_target_pairs={{0,2},{1,3},{2,0},{3,1},{4,6},{5,7},{6,4},{7,5},{8,10},{9,11},{10,... | collective-permute-start | bytes 98312 | tf_op jit(solution)/shard_map/ppermute | solution.py:28
  6.2 2.7 %collective-permute-done.1 = f32[64,128]{1,0:T(8,128)S(1)} collective-permute-done((f32[64,128]{1,0:T(8,128)}, f32[64,128]{1,0:T(8,128)S(1)}, u32[]{:S(2)}, u32[]{:S(2)}) %collective-permute-start.1) | collective-permute-done | bytes 32800 | tf_op jit(solution)/shard_map/ppermute | solution.py:28
  11.2 7.0 %all-to-all-start = ((bf16[16,24,512]{2,1,0:T(8,128)(2,1)}), bf16[16,24,512]{2,1,0:T(8,128)(2,1)S(1)}, u32[]{:S(2)}, u32[]{:S(2)}) async-start(bf16[16,24,512]{2,1,0:T(8,128)(2,1)} %broadcast_in_dim.22), calls=%async_computation | async-start | bytes 786432 | tf_op jit(solution)/shard_map/all_to_all | solution.py:135
  18.3 5.6 %collective-permute-start.4 = (bf16[128,128]{1,0:T(8,128)(2,1)S(1)}, bf16[128,128]{1,0:T(8,128)(2,1)S(1)}, u32[]{:S(2)}, u32[]{:S(2)}) collective-permute-start(bf16[128,128]{1,0:T(8,128)(2,1)S(1)} %bitcast.100), channel_id=1, source_target_pairs={{0,8},{8,0},{1,9},{9,1},{2,10},{10,2},{3,11},{11,3},{4,12},{12,4},... | collective-permute-start | bytes 98312 | tf_op jit(solution)/shard_map/ppermute | solution.py:28
  24.6 1.6 %collective-permute-done.4 = bf16[128,128]{1,0:T(8,128)(2,1)S(1)} collective-permute-done((bf16[128,128]{1,0:T(8,128)(2,1)S(1)}, bf16[128,128]{1,0:T(8,128)(2,1)S(1)}, u32[]{:S(2)}, u32[]{:S(2)}) %collective-permute-start.4) | collective-permute-done | bytes 32800 | tf_op jit(solution)/shard_map/ppermute | solution.py:28
  26.2 2.8 %all-to-all-done = bf16[16,24,512]{2,1,0:T(8,128)(2,1)S(1)} async-done(((bf16[16,24,512]{2,1,0:T(8,128)(2,1)}), bf16[16,24,512]{2,1,0:T(8,128)(2,1)S(1)}, u32[]{:S(2)}, u32[]{:S(2)}) %all-to-all-start) | async-done | bytes 393248 | tf_op jit(solution)/shard_map/all_to_all | solution.py:135
  29.1 7.1 %shard_map.170 = (f32[256,128]{1,0:T(8,128)S(1)}, bf16[16,16,512]{2,1,0:T(8,128)(2,1)}, f32[16,128]{1,0:T(8,128)S(1)}) custom-call(bf16[12,256,1024]{2,1,0:T(8,128)(2,1)} %readings.3, bf16[256,128]{1,0:T(8,128)(2,1)S(1)} %pad_maximum_fusion.7.a16, bf16[128,1024]{1,0:T(8,128)(2,1)S(1)} %pad_maximum_fusion.1.b16, f32[12,1,128]{2,1,0:T(1,128)S(1)} %reshape.80.times), custom_call_target="tpu_custom_call" | custom-call | flops 2415919104 | bytes 6291456 | tf_op jit(solution)/shard_map/pallas_call | solution.py:206
  36.3 1.3 %collective-permute-done.5 = f32[144,128]{1,0:T(8,128)S(1)} collective-permute-done((f32[144,128]{1,0:T(8,128)S(1)}, f32[144,128]{1,0:T(8,128)S(1)}, u32[]{:S(2)}, u32[]{:S(2)}) %collective-permute-start.5) | collective-permute-done | bytes 73760 | tf_op jit(solution)/shard_map/ppermute | solution.py:28
  37.6 5.6 %collective-permute-start.6 = (f32[192,128]{1,0:T(8,128)S(1)}, f32[192,128]{1,0:T(8,128)S(1)}, u32[]{:S(2)}, u32[]{:S(2)}) collective-permute-start(f32[192,128]{1,0:T(8,128)S(1)} %pad_maximum_fusion.4), channel_id=1, source_target_pairs={{0,8},{8,0},{1,9},{9,1},{2,10},{10,2},{3,11},{11,3},{4,12},{12,4},... | collective-permute-start | bytes 294920 | tf_op jit(solution)/shard_map/ppermute | solution.py:28
  43.2 4.4 %all-to-all-start.1 = ((bf16[16,16,512]{2,1,0:T(8,128)(2,1)}), bf16[16,16,512]{2,1,0:T(8,128)(2,1)S(1)}, u32[]{:S(2)}, u32[]{:S(2)}) async-start(bf16[16,16,512]{2,1,0:T(8,128)(2,1)} %get-tuple-element.25), calls=%async_computation.1 | async-start | bytes 524288 | tf_op jit(solution)/shard_map/all_to_all | solution.py:147
  47.8 8.6 %all-to-all-done.1 = bf16[16,16,512]{2,1,0:T(8,128)(2,1)S(1)} async-done(((bf16[16,16,512]{2,1,0:T(8,128)(2,1)}), bf16[16,16,512]{2,1,0:T(8,128)(2,1)S(1)}, u32[]{:S(2)}, u32[]{:S(2)}) %all-to-all-start.1) | async-done | bytes 262176 | tf_op jit(solution)/shard_map/all_to_all | solution.py:147
  56.7 3.2 %collective-permute-start.8 = (f32[96,128]{1,0:T(8,128)S(1)}, f32[96,128]{1,0:T(8,128)S(1)}, u32[]{:S(2)}, u32[]{:S(2)}) collective-permute-start(f32[96,128]{1,0:T(8,128)S(1)} %constant_dynamic-update-slice_fusion.18), channel_id=1, source_target_pairs={{0,2},{1,3},{2,0},{3,1},{4,6},{5,7},{6,4},{7,5},{8,10},{9,11},{10,... | collective-permute-start | bytes 147464 | tf_op jit(solution)/shard_map/ppermute | solution.py:28
  59.9 1.0 collective-permute-start.9
  62.2 2.3 %collective-permute-done.9 = f32[96,128]{1,0:T(8,128)S(1)} collective-permute-done((f32[96,128]{1,0:T(8,128)S(1)}, f32[96,128]{1,0:T(8,128)S(1)}, u32[]{:S(2)}, u32[]{:S(2)}) %collective-permute-start.9) | collective-permute-done | bytes 49184 | tf_op jit(solution)/shard_map/ppermute | solution.py:28
  66.0 3.6 %all-to-all-start.2 = ((bf16[16,24,512]{2,1,0:T(8,128)(2,1)}), bf16[16,24,512]{2,1,0:T(8,128)(2,1)S(1)}, u32[]{:S(2)}, u32[]{:S(2)}) async-start(bf16[16,24,512]{2,1,0:T(8,128)(2,1)} %broadcast_in_dim.26), calls=%async_computation.2 | async-start | bytes 786432 | tf_op jit(solution)/shard_map/all_to_all | solution.py:135
  69.6 1.1 collective-permute-start.13
  70.8 1.4 %collective-permute-start.12 = (bf16[4,16,128]{2,1,0:T(8,128)(2,1)S(1)}, bf16[4,16,128]{2,1,0:T(8,128)(2,1)S(1)}, u32[]{:S(2)}, u32[]{:S(2)}) collective-permute-start(bf16[4,16,128]{2,1,0:T(8,128)(2,1)S(1)} %bitcast.105), channel_id=1, source_target_pairs={{0,2},{1,3},{2,0},{3,1},{4,6},{5,7},{6,4},{7,5},{8,10},{9,11},{10,... | collective-permute-start | bytes 49160 | tf_op jit(solution)/shard_map/ppermute | solution.py:28
  72.2 1.0 collective-permute-start.11
  73.5 1.9 %collective-permute-done.12 = bf16[4,16,128]{2,1,0:T(8,128)(2,1)S(1)} collective-permute-done((bf16[4,16,128]{2,1,0:T(8,128)(2,1)S(1)}, bf16[4,16,128]{2,1,0:T(8,128)(2,1)S(1)}, u32[]{:S(2)}, u32[]{:S(2)}) %collective-permute-start.12) | collective-permute-done | bytes 16416 | tf_op jit(solution)/shard_map/ppermute | solution.py:28
  75.9 4.7 %all-to-all-done.2 = bf16[16,24,512]{2,1,0:T(8,128)(2,1)S(1)} async-done(((bf16[16,24,512]{2,1,0:T(8,128)(2,1)}), bf16[16,24,512]{2,1,0:T(8,128)(2,1)S(1)}, u32[]{:S(2)}, u32[]{:S(2)}) %all-to-all-start.2) | async-done | bytes 393248 | tf_op jit(solution)/shard_map/all_to_all | solution.py:135
  80.8 6.4 %shard_map.171 = (f32[256,128]{1,0:T(8,128)S(1)}, bf16[16,16,512]{2,1,0:T(8,128)(2,1)S(1)}, f32[16,128]{1,0:T(8,128)S(1)}) custom-call(bf16[12,256,1024]{2,1,0:T(8,128)(2,1)} %readings.3, bf16[256,128]{1,0:T(8,128)(2,1)S(1)} %bitcast.93, bf16[128,1024]{1,0:T(8,128)(2,1)S(1)} %pad_maximum_fusion.2.b16, f32[12,1,128]{2,1,0:T(1,128)S(1)} %reshape.81.times), custom_call_target="tpu_custom_call" | custom-call | flops 2415919104 | bytes 6291456 | tf_op jit(solution)/shard_map/pallas_call | solution.py:206
  87.3 1.2 %collective-permute-done.14 = f32[144,128]{1,0:T(8,128)S(1)} collective-permute-done((f32[144,128]{1,0:T(8,128)S(1)}, f32[144,128]{1,0:T(8,128)S(1)}, u32[]{:S(2)}, u32[]{:S(2)}) %collective-permute-start.14) | collective-permute-done | bytes 73760 | tf_op jit(solution)/shard_map/ppermute | solution.py:28
  89.4 3.6 %all-to-all-start.3 = ((bf16[16,24,512]{2,1,0:T(8,128)(2,1)}), bf16[16,24,512]{2,1,0:T(8,128)(2,1)S(1)}, u32[]{:S(2)}, u32[]{:S(2)}) async-start(bf16[16,24,512]{2,1,0:T(8,128)(2,1)} %pad_maximum_fusion), calls=%async_computation.3 | async-start | bytes 786432 | tf_op jit(solution)/shard_map/all_to_all | solution.py:147
  93.0 1.5 %collective-permute-start.15 = (f32[64,128]{1,0:T(8,128)S(1)}, f32[64,128]{1,0:T(8,128)S(1)}, u32[]{:S(2)}, u32[]{:S(2)}) collective-permute-start(f32[64,128]{1,0:T(8,128)S(1)} %slice_select_fusion), channel_id=1, source_target_pairs={{0,8},{8,0},{1,9},{9,1},{2,10},{10,2},{3,11},{11,3},{4,12},{12,4},... | collective-permute-start | bytes 98312 | tf_op jit(solution)/shard_map/ppermute | solution.py:28
  94.5 6.4 %collective-permute-done.15 = f32[64,128]{1,0:T(8,128)S(1)} collective-permute-done((f32[64,128]{1,0:T(8,128)S(1)}, f32[64,128]{1,0:T(8,128)S(1)}, u32[]{:S(2)}, u32[]{:S(2)}) %collective-permute-start.15) | collective-permute-done | bytes 32800 | tf_op jit(solution)/shard_map/ppermute | solution.py:28
  100.9 2.7 %all-to-all-done.3 = bf16[16,24,512]{2,1,0:T(8,128)(2,1)S(1)} async-done(((bf16[16,24,512]{2,1,0:T(8,128)(2,1)}), bf16[16,24,512]{2,1,0:T(8,128)(2,1)S(1)}, u32[]{:S(2)}, u32[]{:S(2)}) %all-to-all-start.3) | async-done | bytes 393248 | tf_op jit(solution)/shard_map/all_to_all | solution.py:147
  103.7 1.5 %collective-permute-start.19 = (f32[16,128]{1,0:T(8,128)S(1)}, f32[16,128]{1,0:T(8,128)S(1)}, u32[]{:S(2)}, u32[]{:S(2)}) collective-permute-start(f32[16,128]{1,0:T(8,128)S(1)} %pad_maximum_fusion.17), channel_id=1, source_target_pairs={{0,8},{8,0},{1,9},{9,1},{2,10},{10,2},{3,11},{11,3},{4,12},{12,4},... | collective-permute-start | bytes 24584 | tf_op jit(solution)/shard_map/ppermute | solution.py:28
  105.5 2.9 %collective-permute-start.16 = (f32[32,128]{1,0:T(8,128)S(1)}, f32[32,128]{1,0:T(8,128)S(1)}, u32[]{:S(2)}, u32[]{:S(2)}) collective-permute-start(f32[32,128]{1,0:T(8,128)S(1)} %get-tuple-element.70), channel_id=1, source_target_pairs={{0,1},{1,0},{2,3},{3,2},{4,5},{5,4},{6,7},{7,6},{8,9},{9,8},{10,11... | collective-permute-start | bytes 49160 | tf_op jit(solution)/shard_map/ppermute | solution.py:28
  109.0 2.4 %collective-permute-done.19 = f32[16,128]{1,0:T(8,128)S(1)} collective-permute-done((f32[16,128]{1,0:T(8,128)S(1)}, f32[16,128]{1,0:T(8,128)S(1)}, u32[]{:S(2)}, u32[]{:S(2)}) %collective-permute-start.19) | collective-permute-done | bytes 8224 | tf_op jit(solution)/shard_map/ppermute | solution.py:28
  112.0 1.1 collective-permute-done.17
  (128 shorter events, 11.5 us)
Async XLA Ops:
  2.0 4.1 %collective-permute-start.2 = (f32[64,128]{1,0:T(8,128)}, f32[64,128]{1,0:T(8,128)S(1)}, u32[]{:S(2)}, u32[]{:S(2)}) collective-permute-start(f32[64,128]{1,0:T(8,128)} %bitcast.107), channel_id=1, source_target_pairs={{0,1},{1,0},{2,3},{3,2},{4,5},{5,4},{6,7},{7,6},{8,9},{9,8},{10,11... | collective-permute-start | bytes 98312 | tf_op jit(solution)/shard_map/ppermute | solution.py:28
  3.9 5.0 %collective-permute-start.1 = (f32[64,128]{1,0:T(8,128)}, f32[64,128]{1,0:T(8,128)S(1)}, u32[]{:S(2)}, u32[]{:S(2)}) collective-permute-start(f32[64,128]{1,0:T(8,128)} %bitcast.108), channel_id=1, source_target_pairs={{0,2},{1,3},{2,0},{3,1},{4,6},{5,7},{6,4},{7,5},{8,10},{9,11},{10,... | collective-permute-start | bytes 98312 | tf_op jit(solution)/shard_map/ppermute | solution.py:28
  5.4 4.1 %collective-permute-start = (f32[64,128]{1,0:T(8,128)}, f32[64,128]{1,0:T(8,128)S(1)}, u32[]{:S(2)}, u32[]{:S(2)}) collective-permute-start(f32[64,128]{1,0:T(8,128)} %bitcast.109), channel_id=1, source_target_pairs={{0,3},{1,2},{2,1},{3,0},{4,7},{5,6},{6,5},{7,4},{8,11},{9,10},{10,... | collective-permute-start | bytes 98312 | tf_op jit(solution)/shard_map/ppermute | solution.py:28
  10.4 27.2 %copy-start = (f32[48,128]{1,0:T(8,128)S(1)}, f32[48,128]{1,0:T(8,128)}, u32[]{:S(2)}) copy-start(f32[48,128]{1,0:T(8,128)} %get-tuple-element.24) | copy-start | bytes 73732
  11.2 7.0 %collective-permute-start.3 = (bf16[1,64,128]{2,1,0:T(8,128)(2,1)S(1)}, bf16[1,64,128]{2,1,0:T(8,128)(2,1)S(1)}, u32[]{:S(2)}, u32[]{:S(2)}) collective-permute-start(bf16[1,64,128]{2,1,0:T(8,128)(2,1)S(1)} %bitcast.102), channel_id=1, source_target_pairs={{0,4},{4,0},{1,5},{5,1},{2,6},{6,2},{3,7},{7,3},{8,12},{12,8},{9,1... | collective-permute-start | bytes 49160 | tf_op jit(solution)/shard_map/ppermute | solution.py:28
  11.2 17.8 %all-to-all-start = ((bf16[16,24,512]{2,1,0:T(8,128)(2,1)}), bf16[16,24,512]{2,1,0:T(8,128)(2,1)S(1)}, u32[]{:S(2)}, u32[]{:S(2)}) async-start(bf16[16,24,512]{2,1,0:T(8,128)(2,1)} %broadcast_in_dim.22), calls=%async_computation | async-start | bytes 786432 | tf_op jit(solution)/shard_map/all_to_all | solution.py:135
  18.3 7.9 %collective-permute-start.4 = (bf16[128,128]{1,0:T(8,128)(2,1)S(1)}, bf16[128,128]{1,0:T(8,128)(2,1)S(1)}, u32[]{:S(2)}, u32[]{:S(2)}) collective-permute-start(bf16[128,128]{1,0:T(8,128)(2,1)S(1)} %bitcast.100), channel_id=1, source_target_pairs={{0,8},{8,0},{1,9},{9,1},{2,10},{10,2},{3,11},{11,3},{4,12},{12,4},... | collective-permute-start | bytes 98312 | tf_op jit(solution)/shard_map/ppermute | solution.py:28
  29.1 51.6 %copy-start.1 = (f32[12,128]{1,0:T(8,128)S(1)}, f32[12,128]{1,0:T(8,128)}, u32[]{:S(2)}) copy-start(f32[12,128]{1,0:T(8,128)} %param.19) | copy-start | bytes 18436
  29.1 51.6 %copy-start.2 = (f32[12,128]{1,0:T(8,128)S(1)}, f32[12,128]{1,0:T(8,128)}, u32[]{:S(2)}) copy-start(f32[12,128]{1,0:T(8,128)} %param.18) | copy-start | bytes 18436
  29.1 51.6 %copy-start.3 = (f32[12,128]{1,0:T(8,128)S(1)}, f32[12,128]{1,0:T(8,128)}, u32[]{:S(2)}) copy-start(f32[12,128]{1,0:T(8,128)} %param.13) | copy-start | bytes 18436
  36.2 1.4 %collective-permute-start.5 = (f32[144,128]{1,0:T(8,128)S(1)}, f32[144,128]{1,0:T(8,128)S(1)}, u32[]{:S(2)}, u32[]{:S(2)}) collective-permute-start(f32[144,128]{1,0:T(8,128)S(1)} %pad_maximum_fusion.5), channel_id=1, source_target_pairs={{0,4},{4,0},{1,5},{5,1},{2,6},{6,2},{3,7},{7,3},{8,12},{12,8},{9,1... | collective-permute-start | bytes 221192 | tf_op jit(solution)/shard_map/ppermute | solution.py:28
  37.6 10.1 %collective-permute-start.6 = (f32[192,128]{1,0:T(8,128)S(1)}, f32[192,128]{1,0:T(8,128)S(1)}, u32[]{:S(2)}, u32[]{:S(2)}) collective-permute-start(f32[192,128]{1,0:T(8,128)S(1)} %pad_maximum_fusion.4), channel_id=1, source_target_pairs={{0,8},{8,0},{1,9},{9,1},{2,10},{10,2},{3,11},{11,3},{4,12},{12,4},... | collective-permute-start | bytes 294920 | tf_op jit(solution)/shard_map/ppermute | solution.py:28
  43.2 13.2 %all-to-all-start.1 = ((bf16[16,16,512]{2,1,0:T(8,128)(2,1)}), bf16[16,16,512]{2,1,0:T(8,128)(2,1)S(1)}, u32[]{:S(2)}, u32[]{:S(2)}) async-start(bf16[16,16,512]{2,1,0:T(8,128)(2,1)} %get-tuple-element.25), calls=%async_computation.1 | async-start | bytes 524288 | tf_op jit(solution)/shard_map/all_to_all | solution.py:147
  56.7 5.5 %collective-permute-start.8 = (f32[96,128]{1,0:T(8,128)S(1)}, f32[96,128]{1,0:T(8,128)S(1)}, u32[]{:S(2)}, u32[]{:S(2)}) collective-permute-start(f32[96,128]{1,0:T(8,128)S(1)} %constant_dynamic-update-slice_fusion.18), channel_id=1, source_target_pairs={{0,2},{1,3},{2,0},{3,1},{4,6},{5,7},{6,4},{7,5},{8,10},{9,11},{10,... | collective-permute-start | bytes 147464 | tf_op jit(solution)/shard_map/ppermute | solution.py:28
  59.9 4.6 %collective-permute-start.9 = (f32[96,128]{1,0:T(8,128)S(1)}, f32[96,128]{1,0:T(8,128)S(1)}, u32[]{:S(2)}, u32[]{:S(2)}) collective-permute-start(f32[96,128]{1,0:T(8,128)S(1)} %get-tuple-element.106), channel_id=1, source_target_pairs={{0,3},{1,2},{2,1},{3,0},{4,7},{5,6},{6,5},{7,4},{8,11},{9,10},{10,... | collective-permute-start | bytes 147464 | tf_op jit(solution)/shard_map/ppermute | solution.py:28
  60.9 4.1 %collective-permute-start.7 = (f32[96,128]{1,0:T(8,128)S(1)}, f32[96,128]{1,0:T(8,128)S(1)}, u32[]{:S(2)}, u32[]{:S(2)}) collective-permute-start(f32[96,128]{1,0:T(8,128)S(1)} %get-tuple-element.88), channel_id=1, source_target_pairs={{0,1},{1,0},{2,3},{3,2},{4,5},{5,4},{6,7},{7,6},{8,9},{9,8},{10,11... | collective-permute-start | bytes 147464 | tf_op jit(solution)/shard_map/ppermute | solution.py:28
  65.1 4.5 %collective-permute-start.10 = (bf16[2,16,128]{2,1,0:T(8,128)(2,1)S(1)}, bf16[2,16,128]{2,1,0:T(8,128)(2,1)S(1)}, u32[]{:S(2)}, u32[]{:S(2)}) collective-permute-start(bf16[2,16,128]{2,1,0:T(8,128)(2,1)S(1)} %bitcast.110), channel_id=1, source_target_pairs={{0,4},{4,0},{1,5},{5,1},{2,6},{6,2},{3,7},{7,3},{8,12},{12,8},{9,1... | collective-permute-start | bytes 24584 | tf_op jit(solution)/shard_map/ppermute | solution.py:28
  66.0 14.6 %all-to-all-start.2 = ((bf16[16,24,512]{2,1,0:T(8,128)(2,1)}), bf16[16,24,512]{2,1,0:T(8,128)(2,1)S(1)}, u32[]{:S(2)}, u32[]{:S(2)}) async-start(bf16[16,24,512]{2,1,0:T(8,128)(2,1)} %broadcast_in_dim.26), calls=%async_computation.2 | async-start | bytes 786432 | tf_op jit(solution)/shard_map/all_to_all | solution.py:135
  69.6 3.8 %collective-permute-start.13 = (bf16[4,16,128]{2,1,0:T(8,128)(2,1)S(1)}, bf16[4,16,128]{2,1,0:T(8,128)(2,1)S(1)}, u32[]{:S(2)}, u32[]{:S(2)}) collective-permute-start(bf16[4,16,128]{2,1,0:T(8,128)(2,1)S(1)} %bitcast.104), channel_id=1, source_target_pairs={{0,1},{1,0},{2,3},{3,2},{4,5},{5,4},{6,7},{7,6},{8,9},{9,8},{10,11... | collective-permute-start | bytes 49160 | tf_op jit(solution)/shard_map/ppermute | solution.py:28
  70.8 4.6 %collective-permute-start.12 = (bf16[4,16,128]{2,1,0:T(8,128)(2,1)S(1)}, bf16[4,16,128]{2,1,0:T(8,128)(2,1)S(1)}, u32[]{:S(2)}, u32[]{:S(2)}) collective-permute-start(bf16[4,16,128]{2,1,0:T(8,128)(2,1)S(1)} %bitcast.105), channel_id=1, source_target_pairs={{0,2},{1,3},{2,0},{3,1},{4,6},{5,7},{6,4},{7,5},{8,10},{9,11},{10,... | collective-permute-start | bytes 49160 | tf_op jit(solution)/shard_map/ppermute | solution.py:28
  72.2 3.7 %collective-permute-start.11 = (bf16[4,16,128]{2,1,0:T(8,128)(2,1)S(1)}, bf16[4,16,128]{2,1,0:T(8,128)(2,1)S(1)}, u32[]{:S(2)}, u32[]{:S(2)}) collective-permute-start(bf16[4,16,128]{2,1,0:T(8,128)(2,1)S(1)} %bitcast.106), channel_id=1, source_target_pairs={{0,3},{1,2},{2,1},{3,0},{4,7},{5,6},{6,5},{7,4},{8,11},{9,10},{10,... | collective-permute-start | bytes 49160 | tf_op jit(solution)/shard_map/ppermute | solution.py:28
  87.2 1.4 %collective-permute-start.14 = (f32[144,128]{1,0:T(8,128)S(1)}, f32[144,128]{1,0:T(8,128)S(1)}, u32[]{:S(2)}, u32[]{:S(2)}) collective-permute-start(f32[144,128]{1,0:T(8,128)S(1)} %pad_maximum_fusion.6), channel_id=1, source_target_pairs={{0,4},{4,0},{1,5},{5,1},{2,6},{6,2},{3,7},{7,3},{8,12},{12,8},{9,1... | collective-permute-start | bytes 221192 | tf_op jit(solution)/shard_map/ppermute | solution.py:28
  89.4 14.2 %all-to-all-start.3 = ((bf16[16,24,512]{2,1,0:T(8,128)(2,1)}), bf16[16,24,512]{2,1,0:T(8,128)(2,1)S(1)}, u32[]{:S(2)}, u32[]{:S(2)}) async-start(bf16[16,24,512]{2,1,0:T(8,128)(2,1)} %pad_maximum_fusion), calls=%async_computation.3 | async-start | bytes 786432 | tf_op jit(solution)/shard_map/all_to_all | solution.py:147
  93.0 7.9 %collective-permute-start.15 = (f32[64,128]{1,0:T(8,128)S(1)}, f32[64,128]{1,0:T(8,128)S(1)}, u32[]{:S(2)}, u32[]{:S(2)}) collective-permute-start(f32[64,128]{1,0:T(8,128)S(1)} %slice_select_fusion), channel_id=1, source_target_pairs={{0,8},{8,0},{1,9},{9,1},{2,10},{10,2},{3,11},{11,3},{4,12},{12,4},... | collective-permute-start | bytes 98312 | tf_op jit(solution)/shard_map/ppermute | solution.py:28
  103.7 7.6 %collective-permute-start.19 = (f32[16,128]{1,0:T(8,128)S(1)}, f32[16,128]{1,0:T(8,128)S(1)}, u32[]{:S(2)}, u32[]{:S(2)}) collective-permute-start(f32[16,128]{1,0:T(8,128)S(1)} %pad_maximum_fusion.17), channel_id=1, source_target_pairs={{0,8},{8,0},{1,9},{9,1},{2,10},{10,2},{3,11},{11,3},{4,12},{12,4},... | collective-permute-start | bytes 24584 | tf_op jit(solution)/shard_map/ppermute | solution.py:28
  105.4 6.6 %collective-permute-start.18 = (f32[32,128]{1,0:T(8,128)S(1)}, f32[32,128]{1,0:T(8,128)S(1)}, u32[]{:S(2)}, u32[]{:S(2)}) collective-permute-start(f32[32,128]{1,0:T(8,128)S(1)} %get-tuple-element.69), channel_id=1, source_target_pairs={{0,3},{1,2},{2,1},{3,0},{4,7},{5,6},{6,5},{7,4},{8,11},{9,10},{10,... | collective-permute-start | bytes 49160 | tf_op jit(solution)/shard_map/ppermute | solution.py:28
  105.5 6.5 %collective-permute-start.16 = (f32[32,128]{1,0:T(8,128)S(1)}, f32[32,128]{1,0:T(8,128)S(1)}, u32[]{:S(2)}, u32[]{:S(2)}) collective-permute-start(f32[32,128]{1,0:T(8,128)S(1)} %get-tuple-element.70), channel_id=1, source_target_pairs={{0,1},{1,0},{2,3},{3,2},{4,5},{5,4},{6,7},{7,6},{8,9},{9,8},{10,11... | collective-permute-start | bytes 49160 | tf_op jit(solution)/shard_map/ppermute | solution.py:28
  108.5 4.6 %collective-permute-start.17 = (f32[32,128]{1,0:T(8,128)S(1)}, f32[32,128]{1,0:T(8,128)S(1)}, u32[]{:S(2)}, u32[]{:S(2)}) collective-permute-start(f32[32,128]{1,0:T(8,128)S(1)} %get-tuple-element.71), channel_id=1, source_target_pairs={{0,2},{1,3},{2,0},{3,1},{4,6},{5,7},{6,4},{7,5},{8,10},{9,11},{10,... | collective-permute-start | bytes 49160 | tf_op jit(solution)/shard_map/ppermute | solution.py:28

commit v8 on v7

--- a/solution.py
+++ b/solution.py
@@ -294,8 +294,9 @@
     second = stack_columns(second)
     slot = lambda t: jnp.concatenate(
         [lax.dynamic_index_in_dim(part, t, 0, keepdims=False), second], axis=0
-    )
+    ).astype(jnp.bfloat16)
     got = [slot(ta)] + [swap(slot(ta ^ k), "ta", k) for k in (1, 2, 3)]
+    got = [x.astype(jnp.float32) for x in got]
     got = (got[0] + got[1]) + (got[2] + got[3])
     grad_first, grad_second = got[: 2 * rows], got[2 * rows :]
     count = ADAM_STEP + 1

time: 115 us -> 117 us (1.017)
  starting transfers between devices: 48.9 us -> 52.6 us
  waiting for transfers between devices: 42.6 us -> 40.4 us
    ppermute x20, starting transfers between devices: 30.3 us -> 33.2 us  [swap(): return lax.ppermute(x, axis, [(i, i ^ k) for i in range(n)])]
    all_to_all x2, waiting for transfers between devices: 7.44 us -> 5.64 us  [spread_second(): got = lax.all_to_all(slots, 'ia', 0, 0)]
  transfers between devices with their start and end apart: 24 -> 24, of which waited for: 19 -> 18; matrix products, arithmetic and copies ran while one was open for 2% -> 2% of each run, Pallas kernels for 0% -> 0%
where the time goes in v8:
time: 117 us; the launch traced here: 116 us
  starting transfers between devices  52.6 us (45%)
  waiting for transfers between devices  40.4 us (35%)
  Pallas kernels  14.8 us (13%)
  other arithmetic  4.81 us (4%)
  local copies, waits for them, and re-layouts  1.95 us (2%)
  between operations  1.28 us (1%)
    ppermute x20, starting transfers between devices, swap(): return lax.ppermute(x, axis, [(i, i ^ k) for i in range(n)])  33.2 us
    ppermute x20, waiting for transfers between devices, swap(): return lax.ppermute(x, axis, [(i, i ^ k) for i in range(n)])  23.7 us
    pallas_call x2, Pallas kernels, step_parts(): pl.pallas_call(step_kernel, grid=(times // block,), in_specs=[pl.BlockSpe...  13.4 us
    all_to_all x2, waiting for transfers between devices, sum_second(): got = lax.all_to_all(slots, 'ia', 0, 0)  11 us
    all_to_all x2, starting transfers between devices, spread_second(): got = lax.all_to_all(slots, 'ia', 0, 0)  10.6 us
    all_to_all x2, starting transfers between devices, sum_second(): got = lax.all_to_all(slots, 'ia', 0, 0)  8.75 us
    all_to_all x2, waiting for transfers between devices, spread_second(): got = lax.all_to_all(slots, 'ia', 0, 0)  5.64 us
  transfers between devices with their start and end apart: 24, of which 18 were waited for; matrix products, arithmetic and copies ran while one was open for 2% of the time, Pallas kernels for 0%

profile of v8, /device:TPU:32, one launch (start us, length us, event | category | flops | bytes accessed | tf_op | source)
XLA Modules:
  0.0 115.9 jit_solution(6610427052606222350)
XLA Ops:
  0.6 1.4 %shard_map.169 = (f32[1,64,128]{2,1,0:T(8,128)}, f32[48,128]{1,0:T(8,128)}) custom-call(f32[16,128]{1,0:T(8,128)} %f0.1, f32[16,128]{1,0:T(8,128)} %f1.1, f32[16,128]{1,0:T(8,128)} %f2.1, f32[8,256]{1,0:T(8,128)} %s0.1, f32[8,256]{1,0:T(8,128)} %s1_.1, f32[8,256]{1,0:T(8,128)} %s2_.1), custom_call_target="tpu_custom_call" | custom-call | tf_op jit(solution)/shard_map/pallas_call | solution.py:70
  2.1 1.8 %collective-permute-start.2 = (f32[64,128]{1,0:T(8,128)}, f32[64,128]{1,0:T(8,128)S(1)}, u32[]{:S(2)}, u32[]{:S(2)}) collective-permute-start(f32[64,128]{1,0:T(8,128)} %bitcast.115), channel_id=1, source_target_pairs={{0,1},{1,0},{2,3},{3,2},{4,5},{5,4},{6,7},{7,6},{8,9},{9,8},{10,11... | collective-permute-start | bytes 98312 | tf_op jit(solution)/shard_map/ppermute | solution.py:28
  3.9 1.5 %collective-permute-start.1 = (f32[64,128]{1,0:T(8,128)}, f32[64,128]{1,0:T(8,128)S(1)}, u32[]{:S(2)}, u32[]{:S(2)}) collective-permute-start(f32[64,128]{1,0:T(8,128)} %bitcast.116), channel_id=1, source_target_pairs={{0,2},{1,3},{2,0},{3,1},{4,6},{5,7},{6,4},{7,5},{8,10},{9,11},{10,... | collective-permute-start | bytes 98312 | tf_op jit(solution)/shard_map/ppermute | solution.py:28
  6.2 2.7 %collective-permute-done.1 = f32[64,128]{1,0:T(8,128)S(1)} collective-permute-done((f32[64,128]{1,0:T(8,128)}, f32[64,128]{1,0:T(8,128)S(1)}, u32[]{:S(2)}, u32[]{:S(2)}) %collective-permute-start.1) | collective-permute-done | bytes 32800 | tf_op jit(solution)/shard_map/ppermute | solution.py:28
  11.2 7.0 %all-to-all-start = ((bf16[16,24,512]{2,1,0:T(8,128)(2,1)}), bf16[16,24,512]{2,1,0:T(8,128)(2,1)S(1)}, u32[]{:S(2)}, u32[]{:S(2)}) async-start(bf16[16,24,512]{2,1,0:T(8,128)(2,1)} %broadcast_in_dim.22), calls=%async_computation | async-start | bytes 786432 | tf_op jit(solution)/shard_map/all_to_all | solution.py:135
  18.3 5.6 %collective-permute-start.4 = (bf16[128,128]{1,0:T(8,128)(2,1)S(1)}, bf16[128,128]{1,0:T(8,128)(2,1)S(1)}, u32[]{:S(2)}, u32[]{:S(2)}) collective-permute-start(bf16[128,128]{1,0:T(8,128)(2,1)S(1)} %bitcast.108), channel_id=1, source_target_pairs={{0,8},{8,0},{1,9},{9,1},{2,10},{10,2},{3,11},{11,3},{4,12},{12,4},... | collective-permute-start | bytes 98312 | tf_op jit(solution)/shard_map/ppermute | solution.py:28
  24.6 1.6 %collective-permute-done.4 = bf16[128,128]{1,0:T(8,128)(2,1)S(1)} collective-permute-done((bf16[128,128]{1,0:T(8,128)(2,1)S(1)}, bf16[128,128]{1,0:T(8,128)(2,1)S(1)}, u32[]{:S(2)}, u32[]{:S(2)}) %collective-permute-start.4) | collective-permute-done | bytes 32800 | tf_op jit(solution)/shard_map/ppermute | solution.py:28
  26.3 2.8 %all-to-all-done = bf16[16,24,512]{2,1,0:T(8,128)(2,1)S(1)} async-done(((bf16[16,24,512]{2,1,0:T(8,128)(2,1)}), bf16[16,24,512]{2,1,0:T(8,128)(2,1)S(1)}, u32[]{:S(2)}, u32[]{:S(2)}) %all-to-all-start) | async-done | bytes 393248 | tf_op jit(solution)/shard_map/all_to_all | solution.py:135
  29.1 7.1 %shard_map.170 = (f32[256,128]{1,0:T(8,128)S(1)}, bf16[16,16,512]{2,1,0:T(8,128)(2,1)}, f32[16,128]{1,0:T(8,128)S(1)}) custom-call(bf16[12,256,1024]{2,1,0:T(8,128)(2,1)} %readings.3, bf16[256,128]{1,0:T(8,128)(2,1)S(1)} %pad_maximum_fusion.7.a16, bf16[128,1024]{1,0:T(8,128)(2,1)S(1)} %pad_maximum_fusion.1.b16, f32[12,1,128]{2,1,0:T(1,128)S(1)} %reshape.80.times), custom_call_target="tpu_custom_call" | custom-call | flops 2415919104 | bytes 6291456 | tf_op jit(solution)/shard_map/pallas_call | solution.py:206
  36.3 1.3 %collective-permute-done.5 = f32[144,128]{1,0:T(8,128)S(1)} collective-permute-done((f32[144,128]{1,0:T(8,128)S(1)}, f32[144,128]{1,0:T(8,128)S(1)}, u32[]{:S(2)}, u32[]{:S(2)}) %collective-permute-start.5) | collective-permute-done | bytes 73760 | tf_op jit(solution)/shard_map/ppermute | solution.py:28
  37.6 5.6 %collective-permute-start.6 = (f32[192,128]{1,0:T(8,128)S(1)}, f32[192,128]{1,0:T(8,128)S(1)}, u32[]{:S(2)}, u32[]{:S(2)}) collective-permute-start(f32[192,128]{1,0:T(8,128)S(1)} %pad_maximum_fusion.4), channel_id=1, source_target_pairs={{0,8},{8,0},{1,9},{9,1},{2,10},{10,2},{3,11},{11,3},{4,12},{12,4},... | collective-permute-start | bytes 294920 | tf_op jit(solution)/shard_map/ppermute | solution.py:28
  43.2 4.4 %all-to-all-start.1 = ((bf16[16,16,512]{2,1,0:T(8,128)(2,1)}), bf16[16,16,512]{2,1,0:T(8,128)(2,1)S(1)}, u32[]{:S(2)}, u32[]{:S(2)}) async-start(bf16[16,16,512]{2,1,0:T(8,128)(2,1)} %get-tuple-element.25), calls=%async_computation.1 | async-start | bytes 524288 | tf_op jit(solution)/shard_map/all_to_all | solution.py:147
  47.8 8.6 %all-to-all-done.1 = bf16[16,16,512]{2,1,0:T(8,128)(2,1)S(1)} async-done(((bf16[16,16,512]{2,1,0:T(8,128)(2,1)}), bf16[16,16,512]{2,1,0:T(8,128)(2,1)S(1)}, u32[]{:S(2)}, u32[]{:S(2)}) %all-to-all-start.1) | async-done | bytes 262176 | tf_op jit(solution)/shard_map/all_to_all | solution.py:147
  56.7 2.8 %collective-permute-start.7 = (bf16[96,128]{1,0:T(8,128)(2,1)S(1)}, bf16[96,128]{1,0:T(8,128)(2,1)S(1)}, u32[]{:S(2)}, u32[]{:S(2)}) collective-permute-start(bf16[96,128]{1,0:T(8,128)(2,1)S(1)} %get-tuple-element.155), channel_id=1, source_target_pairs={{0,1},{1,0},{2,3},{3,2},{4,5},{5,4},{6,7},{7,6},{8,9},{9,8},{10,11... | collective-permute-start | bytes 73736 | tf_op jit(solution)/shard_map/ppermute | solution.py:28
  60.0 1.0 collective-permute-start.9
  61.3 2.9 %collective-permute-done.8 = bf16[96,128]{1,0:T(8,128)(2,1)S(1)} collective-permute-done((bf16[96,128]{1,0:T(8,128)(2,1)S(1)}, bf16[96,128]{1,0:T(8,128)(2,1)S(1)}, u32[]{:S(2)}, u32[]{:S(2)}) %collective-permute-start.8) | collective-permute-done | bytes 24608 | tf_op jit(solution)/shard_map/ppermute | solution.py:28
  65.2 3.6 %all-to-all-start.2 = ((bf16[16,24,512]{2,1,0:T(8,128)(2,1)}), bf16[16,24,512]{2,1,0:T(8,128)(2,1)S(1)}, u32[]{:S(2)}, u32[]{:S(2)}) async-start(bf16[16,24,512]{2,1,0:T(8,128)(2,1)} %broadcast_in_dim.26), calls=%async_computation.2 | async-start | bytes 786432 | tf_op jit(solution)/shard_map/all_to_all | solution.py:135
  68.8 3.4 %collective-permute-start.13 = (bf16[4,16,128]{2,1,0:T(8,128)(2,1)S(1)}, bf16[4,16,128]{2,1,0:T(8,128)(2,1)S(1)}, u32[]{:S(2)}, u32[]{:S(2)}) collective-permute-start(bf16[4,16,128]{2,1,0:T(8,128)(2,1)S(1)} %bitcast.112), channel_id=1, source_target_pairs={{0,1},{1,0},{2,3},{3,2},{4,5},{5,4},{6,7},{7,6},{8,9},{9,8},{10,11... | collective-permute-start | bytes 49160 | tf_op jit(solution)/shard_map/ppermute | solution.py:28
  72.8 1.0 collective-permute-start.11
  74.0 2.9 %collective-permute-done.12 = bf16[4,16,128]{2,1,0:T(8,128)(2,1)S(1)} collective-permute-done((bf16[4,16,128]{2,1,0:T(8,128)(2,1)S(1)}, bf16[4,16,128]{2,1,0:T(8,128)(2,1)S(1)}, u32[]{:S(2)}, u32[]{:S(2)}) %collective-permute-start.12) | collective-permute-done | bytes 16416 | tf_op jit(solution)/shard_map/ppermute | solution.py:28
  76.9 2.9 %all-to-all-done.2 = bf16[16,24,512]{2,1,0:T(8,128)(2,1)S(1)} async-done(((bf16[16,24,512]{2,1,0:T(8,128)(2,1)}), bf16[16,24,512]{2,1,0:T(8,128)(2,1)S(1)}, u32[]{:S(2)}, u32[]{:S(2)}) %all-to-all-start.2) | async-done | bytes 393248 | tf_op jit(solution)/shard_map/all_to_all | solution.py:135
  80.0 6.4 %shard_map.171 = (f32[256,128]{1,0:T(8,128)S(1)}, bf16[16,16,512]{2,1,0:T(8,128)(2,1)S(1)}, f32[16,128]{1,0:T(8,128)S(1)}) custom-call(bf16[12,256,1024]{2,1,0:T(8,128)(2,1)} %readings.3, bf16[256,128]{1,0:T(8,128)(2,1)S(1)} %bitcast.101, bf16[128,1024]{1,0:T(8,128)(2,1)S(1)} %pad_maximum_fusion.2.b16, f32[12,1,128]{2,1,0:T(1,128)S(1)} %reshape.81.times), custom_call_target="tpu_custom_call" | custom-call | flops 2415919104 | bytes 6291456 | tf_op jit(solution)/shard_map/pallas_call | solution.py:206
  86.5 1.2 %collective-permute-done.14 = f32[144,128]{1,0:T(8,128)S(1)} collective-permute-done((f32[144,128]{1,0:T(8,128)S(1)}, f32[144,128]{1,0:T(8,128)S(1)}, u32[]{:S(2)}, u32[]{:S(2)}) %collective-permute-start.14) | collective-permute-done | bytes 73760 | tf_op jit(solution)/shard_map/ppermute | solution.py:28
  88.6 4.3 %all-to-all-start.3 = ((bf16[16,24,512]{2,1,0:T(8,128)(2,1)}), bf16[16,24,512]{2,1,0:T(8,128)(2,1)S(1)}, u32[]{:S(2)}, u32[]{:S(2)}) async-start(bf16[16,24,512]{2,1,0:T(8,128)(2,1)} %pad_maximum_fusion), calls=%async_computation.3 | async-start | bytes 786432 | tf_op jit(solution)/shard_map/all_to_all | solution.py:147
  93.0 1.2 %collective-permute-start.15 = (f32[64,128]{1,0:T(8,128)S(1)}, f32[64,128]{1,0:T(8,128)S(1)}, u32[]{:S(2)}, u32[]{:S(2)}) collective-permute-start(f32[64,128]{1,0:T(8,128)S(1)} %slice_select_fusion), channel_id=1, source_target_pairs={{0,8},{8,0},{1,9},{9,1},{2,10},{10,2},{3,11},{11,3},{4,12},{12,4},... | collective-permute-start | bytes 98312 | tf_op jit(solution)/shard_map/ppermute | solution.py:28
  94.1 6.7 %collective-permute-done.15 = f32[64,128]{1,0:T(8,128)S(1)} collective-permute-done((f32[64,128]{1,0:T(8,128)S(1)}, f32[64,128]{1,0:T(8,128)S(1)}, u32[]{:S(2)}, u32[]{:S(2)}) %collective-permute-start.15) | collective-permute-done | bytes 32800 | tf_op jit(solution)/shard_map/ppermute | solution.py:28
  100.9 2.5 %all-to-all-done.3 = bf16[16,24,512]{2,1,0:T(8,128)(2,1)S(1)} async-done(((bf16[16,24,512]{2,1,0:T(8,128)(2,1)}), bf16[16,24,512]{2,1,0:T(8,128)(2,1)S(1)}, u32[]{:S(2)}, u32[]{:S(2)}) %all-to-all-start.3) | async-done | bytes 393248 | tf_op jit(solution)/shard_map/all_to_all | solution.py:147
  103.4 1.2 %collective-permute-start.19 = (f32[16,128]{1,0:T(8,128)S(1)}, f32[16,128]{1,0:T(8,128)S(1)}, u32[]{:S(2)}, u32[]{:S(2)}) collective-permute-start(f32[16,128]{1,0:T(8,128)S(1)} %pad_maximum_fusion.17), channel_id=1, source_target_pairs={{0,8},{8,0},{1,9},{9,1},{2,10},{10,2},{3,11},{11,3},{4,12},{12,4},... | collective-permute-start | bytes 24584 | tf_op jit(solution)/shard_map/ppermute | solution.py:28
  104.8 1.5 %collective-permute-start.18 = (f32[32,128]{1,0:T(8,128)S(1)}, f32[32,128]{1,0:T(8,128)S(1)}, u32[]{:S(2)}, u32[]{:S(2)}) collective-permute-start(f32[32,128]{1,0:T(8,128)S(1)} %get-tuple-element.85), channel_id=1, source_target_pairs={{0,3},{1,2},{2,1},{3,0},{4,7},{5,6},{6,5},{7,4},{8,11},{9,10},{10,... | collective-permute-start | bytes 49160 | tf_op jit(solution)/shard_map/ppermute | solution.py:28
  106.2 3.7 %collective-permute-start.16 = (f32[32,128]{1,0:T(8,128)S(1)}, f32[32,128]{1,0:T(8,128)S(1)}, u32[]{:S(2)}, u32[]{:S(2)}) collective-permute-start(f32[32,128]{1,0:T(8,128)S(1)} %get-tuple-element.86), channel_id=1, source_target_pairs={{0,1},{1,0},{2,3},{3,2},{4,5},{5,4},{6,7},{7,6},{8,9},{9,8},{10,11... | collective-permute-start | bytes 49160 | tf_op jit(solution)/shard_map/ppermute | solution.py:28
  110.0 1.0 collective-permute-start.17
  112.0 2.6 %collective-permute-done.17 = f32[32,128]{1,0:T(8,128)S(1)} collective-permute-done((f32[32,128]{1,0:T(8,128)S(1)}, f32[32,128]{1,0:T(8,128)S(1)}, u32[]{:S(2)}, u32[]{:S(2)}) %collective-permute-start.17) | collective-permute-done | bytes 16416 | tf_op jit(solution)/shard_map/ppermute | solution.py:28
  (123 shorter events, 10.3 us)
Async XLA Ops:
  2.1 4.1 %collective-permute-start.2 = (f32[64,128]{1,0:T(8,128)}, f32[64,128]{1,0:T(8,128)S(1)}, u32[]{:S(2)}, u32[]{:S(2)}) collective-permute-start(f32[64,128]{1,0:T(8,128)} %bitcast.115), channel_id=1, source_target_pairs={{0,1},{1,0},{2,3},{3,2},{4,5},{5,4},{6,7},{7,6},{8,9},{9,8},{10,11... | collective-permute-start | bytes 98312 | tf_op jit(solution)/shard_map/ppermute | solution.py:28
  3.9 5.0 %collective-permute-start.1 = (f32[64,128]{1,0:T(8,128)}, f32[64,128]{1,0:T(8,128)S(1)}, u32[]{:S(2)}, u32[]{:S(2)}) collective-permute-start(f32[64,128]{1,0:T(8,128)} %bitcast.116), channel_id=1, source_target_pairs={{0,2},{1,3},{2,0},{3,1},{4,6},{5,7},{6,4},{7,5},{8,10},{9,11},{10,... | collective-permute-start | bytes 98312 | tf_op jit(solution)/shard_map/ppermute | solution.py:28
  5.4 4.1 %collective-permute-start = (f32[64,128]{1,0:T(8,128)}, f32[64,128]{1,0:T(8,128)S(1)}, u32[]{:S(2)}, u32[]{:S(2)}) collective-permute-start(f32[64,128]{1,0:T(8,128)} %bitcast.117), channel_id=1, source_target_pairs={{0,3},{1,2},{2,1},{3,0},{4,7},{5,6},{6,5},{7,4},{8,11},{9,10},{10,... | collective-permute-start | bytes 98312 | tf_op jit(solution)/shard_map/ppermute | solution.py:28
  10.4 27.2 %copy-start = (f32[48,128]{1,0:T(8,128)S(1)}, f32[48,128]{1,0:T(8,128)}, u32[]{:S(2)}) copy-start(f32[48,128]{1,0:T(8,128)} %get-tuple-element.24) | copy-start | bytes 73732
  11.2 7.0 %collective-permute-start.3 = (bf16[1,64,128]{2,1,0:T(8,128)(2,1)S(1)}, bf16[1,64,128]{2,1,0:T(8,128)(2,1)S(1)}, u32[]{:S(2)}, u32[]{:S(2)}) collective-permute-start(bf16[1,64,128]{2,1,0:T(8,128)(2,1)S(1)} %bitcast.110), channel_id=1, source_target_pairs={{0,4},{4,0},{1,5},{5,1},{2,6},{6,2},{3,7},{7,3},{8,12},{12,8},{9,1... | collective-permute-start | bytes 49160 | tf_op jit(solution)/shard_map/ppermute | solution.py:28
  11.2 17.8 %all-to-all-start = ((bf16[16,24,512]{2,1,0:T(8,128)(2,1)}), bf16[16,24,512]{2,1,0:T(8,128)(2,1)S(1)}, u32[]{:S(2)}, u32[]{:S(2)}) async-start(bf16[16,24,512]{2,1,0:T(8,128)(2,1)} %broadcast_in_dim.22), calls=%async_computation | async-start | bytes 786432 | tf_op jit(solution)/shard_map/all_to_all | solution.py:135
  18.3 7.9 %collective-permute-start.4 = (bf16[128,128]{1,0:T(8,128)(2,1)S(1)}, bf16[128,128]{1,0:T(8,128)(2,1)S(1)}, u32[]{:S(2)}, u32[]{:S(2)}) collective-permute-start(bf16[128,128]{1,0:T(8,128)(2,1)S(1)} %bitcast.108), channel_id=1, source_target_pairs={{0,8},{8,0},{1,9},{9,1},{2,10},{10,2},{3,11},{11,3},{4,12},{12,4},... | collective-permute-start | bytes 98312 | tf_op jit(solution)/shard_map/ppermute | solution.py:28
  29.1 50.8 %copy-start.1 = (f32[12,128]{1,0:T(8,128)S(1)}, f32[12,128]{1,0:T(8,128)}, u32[]{:S(2)}) copy-start(f32[12,128]{1,0:T(8,128)} %param.19) | copy-start | bytes 18436
  29.1 50.8 %copy-start.2 = (f32[12,128]{1,0:T(8,128)S(1)}, f32[12,128]{1,0:T(8,128)}, u32[]{:S(2)}) copy-start(f32[12,128]{1,0:T(8,128)} %param.18) | copy-start | bytes 18436
  29.1 50.8 %copy-start.3 = (f32[12,128]{1,0:T(8,128)S(1)}, f32[12,128]{1,0:T(8,128)}, u32[]{:S(2)}) copy-start(f32[12,128]{1,0:T(8,128)} %param.13) | copy-start | bytes 18436
  36.2 1.4 %collective-permute-start.5 = (f32[144,128]{1,0:T(8,128)S(1)}, f32[144,128]{1,0:T(8,128)S(1)}, u32[]{:S(2)}, u32[]{:S(2)}) collective-permute-start(f32[144,128]{1,0:T(8,128)S(1)} %pad_maximum_fusion.5), channel_id=1, source_target_pairs={{0,4},{4,0},{1,5},{5,1},{2,6},{6,2},{3,7},{7,3},{8,12},{12,8},{9,1... | collective-permute-start | bytes 221192 | tf_op jit(solution)/shard_map/ppermute | solution.py:28
  37.6 10.1 %collective-permute-start.6 = (f32[192,128]{1,0:T(8,128)S(1)}, f32[192,128]{1,0:T(8,128)S(1)}, u32[]{:S(2)}, u32[]{:S(2)}) collective-permute-start(f32[192,128]{1,0:T(8,128)S(1)} %pad_maximum_fusion.4), channel_id=1, source_target_pairs={{0,8},{8,0},{1,9},{9,1},{2,10},{10,2},{3,11},{11,3},{4,12},{12,4},... | collective-permute-start | bytes 294920 | tf_op jit(solution)/shard_map/ppermute | solution.py:28
  43.2 13.2 %all-to-all-start.1 = ((bf16[16,16,512]{2,1,0:T(8,128)(2,1)}), bf16[16,16,512]{2,1,0:T(8,128)(2,1)S(1)}, u32[]{:S(2)}, u32[]{:S(2)}) async-start(bf16[16,16,512]{2,1,0:T(8,128)(2,1)} %get-tuple-element.25), calls=%async_computation.1 | async-start | bytes 524288 | tf_op jit(solution)/shard_map/all_to_all | solution.py:147
  56.7 4.6 %collective-permute-start.7 = (bf16[96,128]{1,0:T(8,128)(2,1)S(1)}, bf16[96,128]{1,0:T(8,128)(2,1)S(1)}, u32[]{:S(2)}, u32[]{:S(2)}) collective-permute-start(bf16[96,128]{1,0:T(8,128)(2,1)S(1)} %get-tuple-element.155), channel_id=1, source_target_pairs={{0,1},{1,0},{2,3},{3,2},{4,5},{5,4},{6,7},{7,6},{8,9},{9,8},{10,11... | collective-permute-start | bytes 73736 | tf_op jit(solution)/shard_map/ppermute | solution.py:28
  59.4 4.7 %collective-permute-start.8 = (bf16[96,128]{1,0:T(8,128)(2,1)S(1)}, bf16[96,128]{1,0:T(8,128)(2,1)S(1)}, u32[]{:S(2)}, u32[]{:S(2)}) collective-permute-start(bf16[96,128]{1,0:T(8,128)(2,1)S(1)} %get-tuple-element.156), channel_id=1, source_target_pairs={{0,2},{1,3},{2,0},{3,1},{4,6},{5,7},{6,4},{7,5},{8,10},{9,11},{10,... | collective-permute-start | bytes 73736 | tf_op jit(solution)/shard_map/ppermute | solution.py:28
  60.0 4.2 %collective-permute-start.9 = (bf16[96,128]{1,0:T(8,128)(2,1)S(1)}, bf16[96,128]{1,0:T(8,128)(2,1)S(1)}, u32[]{:S(2)}, u32[]{:S(2)}) collective-permute-start(bf16[96,128]{1,0:T(8,128)(2,1)S(1)} %get-tuple-element.157), channel_id=1, source_target_pairs={{0,3},{1,2},{2,1},{3,0},{4,7},{5,6},{6,5},{7,4},{8,11},{9,10},{10,... | collective-permute-start | bytes 73736 | tf_op jit(solution)/shard_map/ppermute | solution.py:28
  64.3 4.5 %collective-permute-start.10 = (bf16[2,16,128]{2,1,0:T(8,128)(2,1)S(1)}, bf16[2,16,128]{2,1,0:T(8,128)(2,1)S(1)}, u32[]{:S(2)}, u32[]{:S(2)}) collective-permute-start(bf16[2,16,128]{2,1,0:T(8,128)(2,1)S(1)} %bitcast.118), channel_id=1, source_target_pairs={{0,4},{4,0},{1,5},{5,1},{2,6},{6,2},{3,7},{7,3},{8,12},{12,8},{9,1... | collective-permute-start | bytes 24584 | tf_op jit(solution)/shard_map/ppermute | solution.py:28
  65.2 14.6 %all-to-all-start.2 = ((bf16[16,24,512]{2,1,0:T(8,128)(2,1)}), bf16[16,24,512]{2,1,0:T(8,128)(2,1)S(1)}, u32[]{:S(2)}, u32[]{:S(2)}) async-start(bf16[16,24,512]{2,1,0:T(8,128)(2,1)} %broadcast_in_dim.26), calls=%async_computation.2 | async-start | bytes 786432 | tf_op jit(solution)/shard_map/all_to_all | solution.py:135
  68.8 5.2 %collective-permute-start.13 = (bf16[4,16,128]{2,1,0:T(8,128)(2,1)S(1)}, bf16[4,16,128]{2,1,0:T(8,128)(2,1)S(1)}, u32[]{:S(2)}, u32[]{:S(2)}) collective-permute-start(bf16[4,16,128]{2,1,0:T(8,128)(2,1)S(1)} %bitcast.112), channel_id=1, source_target_pairs={{0,1},{1,0},{2,3},{3,2},{4,5},{5,4},{6,7},{7,6},{8,9},{9,8},{10,11... | collective-permute-start | bytes 49160 | tf_op jit(solution)/shard_map/ppermute | solution.py:28
  72.3 4.6 %collective-permute-start.12 = (bf16[4,16,128]{2,1,0:T(8,128)(2,1)S(1)}, bf16[4,16,128]{2,1,0:T(8,128)(2,1)S(1)}, u32[]{:S(2)}, u32[]{:S(2)}) collective-permute-start(bf16[4,16,128]{2,1,0:T(8,128)(2,1)S(1)} %bitcast.113), channel_id=1, source_target_pairs={{0,2},{1,3},{2,0},{3,1},{4,6},{5,7},{6,4},{7,5},{8,10},{9,11},{10,... | collective-permute-start | bytes 49160 | tf_op jit(solution)/shard_map/ppermute | solution.py:28
  72.8 4.1 %collective-permute-start.11 = (bf16[4,16,128]{2,1,0:T(8,128)(2,1)S(1)}, bf16[4,16,128]{2,1,0:T(8,128)(2,1)S(1)}, u32[]{:S(2)}, u32[]{:S(2)}) collective-permute-start(bf16[4,16,128]{2,1,0:T(8,128)(2,1)S(1)} %bitcast.114), channel_id=1, source_target_pairs={{0,3},{1,2},{2,1},{3,0},{4,7},{5,6},{6,5},{7,4},{8,11},{9,10},{10,... | collective-permute-start | bytes 49160 | tf_op jit(solution)/shard_map/ppermute | solution.py:28
  86.4 1.4 %collective-permute-start.14 = (f32[144,128]{1,0:T(8,128)S(1)}, f32[144,128]{1,0:T(8,128)S(1)}, u32[]{:S(2)}, u32[]{:S(2)}) collective-permute-start(f32[144,128]{1,0:T(8,128)S(1)} %pad_maximum_fusion.6), channel_id=1, source_target_pairs={{0,4},{4,0},{1,5},{5,1},{2,6},{6,2},{3,7},{7,3},{8,12},{12,8},{9,1... | collective-permute-start | bytes 221192 | tf_op jit(solution)/shard_map/ppermute | solution.py:28
  88.6 14.7 %all-to-all-start.3 = ((bf16[16,24,512]{2,1,0:T(8,128)(2,1)}), bf16[16,24,512]{2,1,0:T(8,128)(2,1)S(1)}, u32[]{:S(2)}, u32[]{:S(2)}) async-start(bf16[16,24,512]{2,1,0:T(8,128)(2,1)} %pad_maximum_fusion), calls=%async_computation.3 | async-start | bytes 786432 | tf_op jit(solution)/shard_map/all_to_all | solution.py:147
  93.0 7.9 %collective-permute-start.15 = (f32[64,128]{1,0:T(8,128)S(1)}, f32[64,128]{1,0:T(8,128)S(1)}, u32[]{:S(2)}, u32[]{:S(2)}) collective-permute-start(f32[64,128]{1,0:T(8,128)S(1)} %slice_select_fusion), channel_id=1, source_target_pairs={{0,8},{8,0},{1,9},{9,1},{2,10},{10,2},{3,11},{11,3},{4,12},{12,4},... | collective-permute-start | bytes 98312 | tf_op jit(solution)/shard_map/ppermute | solution.py:28
  103.4 7.6 %collective-permute-start.19 = (f32[16,128]{1,0:T(8,128)S(1)}, f32[16,128]{1,0:T(8,128)S(1)}, u32[]{:S(2)}, u32[]{:S(2)}) collective-permute-start(f32[16,128]{1,0:T(8,128)S(1)} %pad_maximum_fusion.17), channel_id=1, source_target_pairs={{0,8},{8,0},{1,9},{9,1},{2,10},{10,2},{3,11},{11,3},{4,12},{12,4},... | collective-permute-start | bytes 24584 | tf_op jit(solution)/shard_map/ppermute | solution.py:28
  104.8 6.9 %collective-permute-start.18 = (f32[32,128]{1,0:T(8,128)S(1)}, f32[32,128]{1,0:T(8,128)S(1)}, u32[]{:S(2)}, u32[]{:S(2)}) collective-permute-start(f32[32,128]{1,0:T(8,128)S(1)} %get-tuple-element.85), channel_id=1, source_target_pairs={{0,3},{1,2},{2,1},{3,0},{4,7},{5,6},{6,5},{7,4},{8,11},{9,10},{10,... | collective-permute-start | bytes 49160 | tf_op jit(solution)/shard_map/ppermute | solution.py:28
  106.2 5.8 %collective-permute-start.16 = (f32[32,128]{1,0:T(8,128)S(1)}, f32[32,128]{1,0:T(8,128)S(1)}, u32[]{:S(2)}, u32[]{:S(2)}) collective-permute-start(f32[32,128]{1,0:T(8,128)S(1)} %get-tuple-element.86), channel_id=1, source_target_pairs={{0,1},{1,0},{2,3},{3,2},{4,5},{5,4},{6,7},{7,6},{8,9},{9,8},{10,11... | collective-permute-start | bytes 49160 | tf_op jit(solution)/shard_map/ppermute | solution.py:28
  110.0 4.6 %collective-permute-start.17 = (f32[32,128]{1,0:T(8,128)S(1)}, f32[32,128]{1,0:T(8,128)S(1)}, u32[]{:S(2)}, u32[]{:S(2)}) collective-permute-start(f32[32,128]{1,0:T(8,128)S(1)} %get-tuple-element.87), channel_id=1, source_target_pairs={{0,2},{1,3},{2,0},{3,1},{4,6},{5,7},{6,4},{7,5},{8,10},{9,11},{10,... | collective-permute-start | bytes 49160 | tf_op jit(solution)/shard_map/ppermute | solution.py:28
